TPU v7x, 32 devices: a whole 2x2x4 slice. The times are simulated.
32 devices in a mesh: tok: 8 (over y, x, core), tp: 4 (over z).
Axes of the slice: x: 2, y: 2, z: 4, core: 2. Of those that a mesh axis runs over, the one named last changes fastest.
Arguments:
- tokens: bfloat16 [6144, 2048], P('tok'), may hold values from -6 to 6
- gain_attn: float32 [2048], replicated, may hold values from 0.5 to 1.5
- w_query: bfloat16 [2048, 2048], P(None, 'tp'), may hold values from -0.125 to 0.125
- w_key: bfloat16 [2048, 512], P(None, 'tp'), may hold values from -0.125 to 0.125
- w_value: bfloat16 [2048, 512], P(None, 'tp'), may hold values from -0.125 to 0.125
- w_out: bfloat16 [2048, 2048], P('tp'), may hold values from -0.5 to 0.5
- gain_ffn: float32 [2048], replicated, may hold values from 0.5 to 1.5
- w_gate: bfloat16 [2048, 5632], P(None, 'tp'), may hold values from -0.125 to 0.125
- w_up: bfloat16 [2048, 5632], P(None, 'tp'), may hold values from -0.125 to 0.125
- w_down: bfloat16 [5632, 2048], P('tp'), may hold values from -0.078125 to 0.078125
- cotangent: bfloat16 [6144, 2048], P('tok'), may hold values from -6 to 6
- doc_lengths: int32 [6], replicated, may hold values from 128 to 2432, as said below
- keep_flags: int32 [6], replicated, may hold values from 0 to 1, as said below
Outputs:
- mixed: bfloat16 [6144, 2048], P('tok')
- token_grad: bfloat16 [6144, 2048], P('tok')
- grad_gain_attn: float32 [2048], P('tok')
- grad_query: float32 [2048, 2048], P('tok', 'tp')
- grad_key: float32 [2048, 512], P('tok', 'tp')
- grad_value: float32 [2048, 512], P('tok', 'tp')
- grad_out: float32 [2048, 2048], P('tp', 'tok')
- grad_gain_ffn: float32 [2048], P('tok')
- grad_gate: float32 [2048, 5632], P('tok', 'tp')
- grad_up: float32 [2048, 5632], P('tok', 'tp')
- grad_down: float32 [5632, 2048], P('tp', 'tok')
Inputs may be any that keep to these rules, and one draw needn't show every extreme that they name: `doc_lengths`: every length is a multiple of 128 and they sum to 6144; the kept documents hold exactly half of the tokens, and one kept document has 1024 tokens or more. `keep_flags`: half of the documents are kept.
All inputs are finite; a program needn't handle non-finite values.
Results may differ from a plain program's by a relative error of at most 0.015.
Values may be sent and summed in bfloat16 or wider, within the bound.
A program may use at most 256 MiB of HBM per device.

v0:
```python
import math

import jax
import jax.numpy as jnp
from jax import lax
from jax.sharding import PartitionSpec as P

HD = 128
BLOCK = 128


norm_eps = 1e-05
keep_scale = 2.0


def document_tables(doc_lengths, places):
    doc_ends = jnp.cumsum(doc_lengths, dtype=jnp.int32)
    doc_starts = doc_ends - doc_lengths
    doc_ids = jnp.sum(
        (places[:, None] >= doc_ends[None, :]).astype(jnp.int32), axis=1, dtype=jnp.int32
    )
    member = (
        doc_ids[:, None] == jnp.arange(doc_lengths.shape[0], dtype=jnp.int32)[None, :]
    ).astype(jnp.int32)
    positions = places - jnp.sum(member * doc_starts[None, :], axis=1, dtype=jnp.int32)
    return (doc_ids, positions, member)


def rotary_tables(positions, head_dim):
    half_dim = head_dim // 2
    freqs = jnp.exp(jnp.arange(half_dim, dtype=jnp.float32) * (-2.0 * math.log(10000.0) / head_dim))
    angles = positions.astype(jnp.float32)[:, None] * freqs[None, :]
    return (jnp.cos(angles), jnp.sin(angles))


def rotate(values, cosine, sine):
    half_dim = values.shape[-1] // 2
    former, latter = (values[..., :half_dim], values[..., half_dim:])
    cos_b, sin_b = (cosine[:, None, :], sine[:, None, :])
    return jnp.concatenate(
        [former * cos_b - latter * sin_b, latter * cos_b + former * sin_b], axis=-1
    )


def unrotate(values, cosine, sine):
    half_dim = values.shape[-1] // 2
    former, latter = (values[..., :half_dim], values[..., half_dim:])
    cos_b, sin_b = (cosine[:, None, :], sine[:, None, :])
    return jnp.concatenate(
        [former * cos_b + latter * sin_b, latter * cos_b - former * sin_b], axis=-1
    )


def over_rows(left, right):
    return lax.dot_general(
        left, right, (((0,), (0,)), ((), ())), preferred_element_type=jnp.float32
    )


def over_columns(left, right):
    return lax.dot_general(
        left, right, (((1,), (1,)), ((), ())), preferred_element_type=jnp.float32
    )


def pick_blocks(blocks, index, valid):
    picked = jnp.take(blocks, index, axis=0)
    return jnp.where(valid[:, None, None], picked, jnp.zeros((), blocks.dtype))


def on_device(
    tokens,
    gain_attn,
    w_query,
    w_key,
    w_value,
    w_out,
    gain_ffn,
    w_gate,
    w_up,
    w_down,
    cotangent,
    doc_lengths,
    keep_flags,
):
    length = tokens.shape[0]
    model_width = tokens.shape[1]
    devices = lax.axis_size("tok")
    own_index = lax.axis_index("tok")
    blocks_here = length // BLOCK
    kept_here = blocks_here // 2
    total_blocks = blocks_here * devices
    kept_total = kept_here * devices
    block_starts = jnp.arange(total_blocks, dtype=jnp.int32) * BLOCK
    block_docs, block_pos, block_member = document_tables(doc_lengths, block_starts)
    block_kept = jnp.sum(block_member * keep_flags[None, :], axis=1, dtype=jnp.int32)
    block_rank = jnp.cumsum(block_kept, dtype=jnp.int32) - block_kept
    rank_slots = jnp.arange(kept_total, dtype=jnp.int32)
    rank_match = ((block_rank[None, :] == rank_slots[:, None]) & (block_kept[None, :] == 1)).astype(
        jnp.int32
    )
    rank_block = jnp.sum(
        rank_match * jnp.arange(total_blocks, dtype=jnp.int32)[None, :], axis=1, dtype=jnp.int32
    )
    local_kept = lax.dynamic_slice_in_dim(block_kept, own_index * blocks_here, blocks_here)
    local_dest = (
        lax.dynamic_slice_in_dim(block_rank, own_index * blocks_here, blocks_here) % devices
    )
    peer_ids = jnp.arange(devices, dtype=jnp.int32)
    outgoing = (local_dest[None, :] == peer_ids[:, None]) & (local_kept[None, :] == 1)
    out_valid = jnp.any(outgoing, axis=1)
    out_index = jnp.sum(
        outgoing.astype(jnp.int32) * jnp.arange(blocks_here, dtype=jnp.int32)[None, :],
        axis=1,
        dtype=jnp.int32,
    )
    token_blocks = tokens.reshape(blocks_here, BLOCK, model_width)
    grad_blocks = cotangent.reshape(blocks_here, BLOCK, model_width)
    dealt_tokens, dealt_grads = (
        lax.all_to_all(
            pick_blocks(token_blocks, out_index, out_valid),
            "tok",
            split_axis=0,
            concat_axis=0,
            tiled=True,
        ),
        lax.all_to_all(
            pick_blocks(grad_blocks, out_index, out_valid),
            "tok",
            split_axis=0,
            concat_axis=0,
            tiled=True,
        ),
    )
    own_ranks = own_index + jnp.arange(kept_here, dtype=jnp.int32) * devices
    own_blocks = jnp.take(rank_block, own_ranks)
    sources = own_blocks // blocks_here
    rows = kept_here * BLOCK
    rows_x = jnp.take(dealt_tokens, sources, axis=0).reshape(rows, model_width)
    rows_dy = jnp.take(dealt_grads, sources, axis=0).reshape(rows, model_width)
    block_offsets = jnp.arange(BLOCK, dtype=jnp.int32)
    places = (own_blocks[:, None] * BLOCK + block_offsets[None, :]).reshape(rows)
    key_ranks = (
        peer_ids[:, None] + jnp.arange(kept_here, dtype=jnp.int32)[None, :] * devices
    ).reshape(kept_total)
    key_places = (
        jnp.take(rank_block, key_ranks)[:, None] * BLOCK + block_offsets[None, :]
    ).reshape(kept_total * BLOCK)
    doc_ids, positions, member = document_tables(doc_lengths, places)
    key_docs, key_pos, key_member = document_tables(doc_lengths, key_places)
    allowed = (doc_ids[:, None] == key_docs[None, :]) & (places[:, None] >= key_places[None, :])
    rate = keep_scale * jnp.sum(member * keep_flags[None, :], axis=1, dtype=jnp.int32).astype(
        jnp.float32
    )
    cosine, sine = rotary_tables(positions, HD)
    heads_here = w_query.shape[1] // HD
    groups_here = w_key.shape[1] // HD
    sharing = heads_here // groups_here
    score_scale = 1.0 / math.sqrt(HD)
    x_full = rows_x.astype(jnp.float32)
    inv_one = lax.rsqrt(jnp.mean(x_full * x_full, axis=1, keepdims=True) + norm_eps)
    normed_one = (x_full * inv_one * gain_attn).astype(jnp.bfloat16)
    query_pre = jnp.dot(normed_one, w_query, preferred_element_type=jnp.float32).reshape(
        rows, heads_here, HD
    )
    key_pre = jnp.dot(normed_one, w_key, preferred_element_type=jnp.float32).reshape(
        rows, groups_here, HD
    )
    value_pre = jnp.dot(normed_one, w_value, preferred_element_type=jnp.float32)
    queries = rotate(query_pre, cosine, sine).astype(jnp.bfloat16)
    keys_local = rotate(key_pre, cosine, sine).astype(jnp.bfloat16).reshape(rows, groups_here * HD)
    values_local = value_pre.astype(jnp.bfloat16)
    keys_all, values_all = (
        lax.all_gather(keys_local, "tok", axis=0, tiled=True),
        lax.all_gather(values_local, "tok", axis=0, tiled=True),
    )
    key_count = keys_all.shape[0]
    keys_heads = keys_all.reshape(key_count, groups_here, HD)
    values_heads = values_all.reshape(key_count, groups_here, HD)
    query_heads = queries.transpose(1, 0, 2)
    slot_of_head = jnp.arange(heads_here, dtype=jnp.int32) // sharing

    def head_scores(query, slot):
        keys_one = lax.dynamic_index_in_dim(keys_heads, slot, 1, keepdims=False)
        values_one = lax.dynamic_index_in_dim(values_heads, slot, 1, keepdims=False)
        scores = (
            jnp.einsum("qd,kd->qk", query, keys_one, preferred_element_type=jnp.float32)
            * score_scale
        )
        return (jnp.where(allowed, scores, -1e30), keys_one, values_one)

    def head_forward(pack):
        query, slot = pack
        scores, keys_one, values_one = head_scores(query, slot)
        peak = jnp.max(scores, axis=1, keepdims=True)
        weights = jnp.exp(scores - peak)
        totals = jnp.sum(weights, axis=1, keepdims=True)
        probs = (weights / totals).astype(jnp.bfloat16)
        return (jnp.dot(probs, values_one, preferred_element_type=jnp.float32), peak, totals)

    head_outs, peaks, totals = lax.map(head_forward, (query_heads, slot_of_head))
    attended = head_outs.transpose(1, 0, 2).reshape(rows, heads_here * HD).astype(jnp.bfloat16)
    branch_attn = lax.psum(jnp.dot(attended, w_out, preferred_element_type=jnp.float32), "tp")
    hidden_res = x_full + branch_attn
    inv_two = lax.rsqrt(jnp.mean(hidden_res * hidden_res, axis=1, keepdims=True) + norm_eps)
    normed_two = (hidden_res * inv_two * gain_ffn).astype(jnp.bfloat16)
    gate = jnp.dot(normed_two, w_gate, preferred_element_type=jnp.float32)
    upper = jnp.dot(normed_two, w_up, preferred_element_type=jnp.float32)
    sigma = jax.nn.sigmoid(gate)
    swish = gate * sigma
    inner = (swish * upper).astype(jnp.bfloat16)
    branch_ffn = lax.psum(
        jnp.dot(inner, w_down, preferred_element_type=jnp.float32).astype(jnp.bfloat16), "tp"
    ).astype(jnp.float32)
    mixed_rows = (x_full + rate[:, None] * (branch_attn + branch_ffn)).astype(jnp.bfloat16)
    grad_y = rows_dy.astype(jnp.float32)
    grad_branch = rate[:, None] * grad_y
    grad_m = grad_branch.astype(jnp.bfloat16)
    grad_down = over_rows(inner, grad_m)
    grad_inner = over_columns(grad_m, w_down)
    grad_gate_pre = (grad_inner * upper * sigma * (1.0 + gate * (1.0 - sigma))).astype(jnp.bfloat16)
    grad_up_pre = (grad_inner * swish).astype(jnp.bfloat16)
    grad_gate = over_rows(normed_two, grad_gate_pre)
    grad_up = over_rows(normed_two, grad_up_pre)
    grad_normed_two = lax.psum(
        over_columns(grad_gate_pre, w_gate) + over_columns(grad_up_pre, w_up), "tp"
    )
    gain_ffn_part = jnp.sum(grad_normed_two * hidden_res * inv_two, axis=0)
    ffn_sums = (
        lax.psum_scatter(gain_ffn_part, "tok", scatter_dimension=0, tiled=True),
        lax.psum_scatter(grad_gate, "tok", scatter_dimension=0, tiled=True),
        lax.psum_scatter(grad_up, "tok", scatter_dimension=0, tiled=True),
        lax.psum_scatter(grad_down, "tok", scatter_dimension=1, tiled=True),
    )
    weighted_two = gain_ffn * grad_normed_two
    grad_hidden = (
        grad_branch
        + inv_two * weighted_two
        - hidden_res * inv_two**3 * jnp.mean(weighted_two * hidden_res, axis=1, keepdims=True)
    )
    grad_a = grad_hidden.astype(jnp.bfloat16)
    grad_out = over_rows(attended, grad_a)
    grad_attended = over_columns(grad_a, w_out).astype(jnp.bfloat16)
    grad_heads = grad_attended.reshape(rows, heads_here, HD).transpose(1, 0, 2)

    def head_backward(pack):
        query, grad_head, peak, total, slot = pack
        scores, keys_one, values_one = head_scores(query, slot)
        probs = jnp.exp(scores - peak) / total
        probs_low = probs.astype(jnp.bfloat16)
        grad_probs = jnp.einsum(
            "qd,kd->qk", grad_head, values_one, preferred_element_type=jnp.float32
        )
        delta = jnp.sum(probs * grad_probs, axis=1, keepdims=True)
        grad_scores = (probs * (grad_probs - delta)).astype(jnp.bfloat16)
        grad_query_head = (
            jnp.dot(grad_scores, keys_one, preferred_element_type=jnp.float32) * score_scale
        )
        grad_keys_head = over_rows(grad_scores, query) * score_scale
        grad_values_head = over_rows(probs_low, grad_head)
        return (grad_query_head, grad_keys_head, grad_values_head)

    grad_q_heads, grad_k_heads, grad_v_heads = lax.map(
        head_backward, (query_heads, grad_heads, peaks, totals, slot_of_head)
    )
    grad_k_all = (
        grad_k_heads.reshape(groups_here, sharing, key_count, HD)
        .sum(axis=1)
        .transpose(1, 0, 2)
        .reshape(key_count, groups_here * HD)
    )
    grad_v_all = (
        grad_v_heads.reshape(groups_here, sharing, key_count, HD)
        .sum(axis=1)
        .transpose(1, 0, 2)
        .reshape(key_count, groups_here * HD)
    )
    grad_k_own, grad_v_own = (
        lax.psum_scatter(grad_k_all, "tok", scatter_dimension=0, tiled=True),
        lax.psum_scatter(grad_v_all, "tok", scatter_dimension=0, tiled=True),
    )
    grad_query_pre = (
        unrotate(grad_q_heads.transpose(1, 0, 2), cosine, sine)
        .reshape(rows, heads_here * HD)
        .astype(jnp.bfloat16)
    )
    grad_key_pre = (
        unrotate(grad_k_own.reshape(rows, groups_here, HD), cosine, sine)
        .reshape(rows, groups_here * HD)
        .astype(jnp.bfloat16)
    )
    grad_value_pre = grad_v_own.astype(jnp.bfloat16)
    grad_query = over_rows(normed_one, grad_query_pre)
    grad_key = over_rows(normed_one, grad_key_pre)
    grad_value = over_rows(normed_one, grad_value_pre)
    grad_normed_one = lax.psum(
        over_columns(grad_query_pre, w_query)
        + over_columns(grad_key_pre, w_key)
        + over_columns(grad_value_pre, w_value),
        "tp",
    )
    gain_attn_part = jnp.sum(grad_normed_one * x_full * inv_one, axis=0)
    weighted_one = gain_attn * grad_normed_one
    grad_rows = (
        (1.0 - rate)[:, None] * grad_y
        + grad_hidden
        + inv_one * weighted_one
        - x_full * inv_one**3 * jnp.mean(weighted_one * x_full, axis=1, keepdims=True)
    ).astype(jnp.bfloat16)
    incoming = sources[None, :] == peer_ids[:, None]
    back_valid = jnp.any(incoming, axis=1)
    back_index = jnp.sum(
        incoming.astype(jnp.int32) * jnp.arange(kept_here, dtype=jnp.int32)[None, :],
        axis=1,
        dtype=jnp.int32,
    )
    mixed_kept = mixed_rows.reshape(kept_here, BLOCK, model_width)
    grad_kept = grad_rows.reshape(kept_here, BLOCK, model_width)
    back_mixed, back_grads = (
        lax.all_to_all(
            pick_blocks(mixed_kept, back_index, back_valid),
            "tok",
            split_axis=0,
            concat_axis=0,
            tiled=True,
        ),
        lax.all_to_all(
            pick_blocks(grad_kept, back_index, back_valid),
            "tok",
            split_axis=0,
            concat_axis=0,
            tiled=True,
        ),
    )
    kept_mask = (local_kept == 1)[:, None, None]
    mixed = jnp.where(kept_mask, jnp.take(back_mixed, local_dest, axis=0), token_blocks).reshape(
        length, model_width
    )
    token_grad = jnp.where(
        kept_mask, jnp.take(back_grads, local_dest, axis=0), grad_blocks
    ).reshape(length, model_width)
    attn_sums = (
        lax.psum_scatter(gain_attn_part, "tok", scatter_dimension=0, tiled=True),
        lax.psum_scatter(grad_query, "tok", scatter_dimension=0, tiled=True),
        lax.psum_scatter(grad_key, "tok", scatter_dimension=0, tiled=True),
        lax.psum_scatter(grad_value, "tok", scatter_dimension=0, tiled=True),
        lax.psum_scatter(grad_out, "tok", scatter_dimension=1, tiled=True),
    )
    summed = (
        attn_sums[0],
        attn_sums[1],
        attn_sums[2],
        attn_sums[3],
        attn_sums[4],
        ffn_sums[0],
        ffn_sums[1],
        ffn_sums[2],
        ffn_sums[3],
    )
    return (
        mixed,
        token_grad,
        summed[0],
        summed[1],
        summed[2],
        summed[3],
        summed[4],
        summed[5],
        summed[6],
        summed[7],
        summed[8],
    )


def solution(mesh):
    placed = (
        P("tok", None),
        P(),
        P(None, "tp"),
        P(None, "tp"),
        P(None, "tp"),
        P("tp", None),
        P(),
        P(None, "tp"),
        P(None, "tp"),
        P("tp", None),
        P("tok", None),
        P(),
        P(),
    )
    return jax.shard_map(
        on_device,
        mesh=mesh,
        in_specs=placed,
        out_specs=(
            P("tok", None),
            P("tok", None),
            P("tok"),
            P("tok", "tp"),
            P("tok", "tp"),
            P("tok", "tp"),
            P("tp", "tok"),
            P("tok"),
            P("tok", "tp"),
            P("tok", "tp"),
            P("tp", "tok"),
        ),
        check_vma=False,
    )
```

profile of v0, /device:TPU:1, one launch (start us, length us, event | category | flops | bytes accessed | tf_op | source)
XLA Modules:
  0.0 1275.2 jit_solution(1295730691490040511)
XLA Ops:
  10.6 4.7 gather_fusion.2
  15.2 4.7 gather_fusion.6
  19.9 6.0 select_select_fusion.1
  25.9 5.2 all-to-all-start
  31.3 3.9 copy.63
  37.9 38.9 %all-to-all-done = bf16[8,128,2048]{2,1,0:T(8,128)(2,1)} async-done(((bf16[8,128,2048]{2,1,0:T(8,128)(2,1)}), bf16[8,128,2048]{2,1,0:T(8,128)(2,1)}, u32[]{:S(2)}, u32[]{:S(2)}) %all-to-all-start) | async-done | bytes 4194336 | tf_op jit(solution)/shard_map/all_to_all | solution.py:120
  76.8 8.0 all-to-all-start.2
  84.8 4.0 gather_fusion.3
  94.0 47.0 %all_gather.6 = bf16[3072,128]{0,1:T(8,128)(2,1)} all-gather(bf16[384,128]{0,1:T(8,128)(2,1)S(1)} %pad_maximum_fusion), channel_id=1, replica_groups=mesh['tok'=8,'tp'=4] {'tok'}, dimensions={0}, use_global_device_ids=true | all-gather | bytes 884736 | tf_op jit(solution)/shard_map/all_gather | solution.py:174
  142.6 2.2 convolution_convert_fusion.2
  144.9 11.4 all_gather.7
  160.9 18.6 %while.34 = (s32[]{:T(128)}, bf16[4,384,128]{1,2,0:T(8,128)(2,1)S(1)}, f32[4,384,1]{1,2,0:T(1,128)S(1)}, f32[4,384,1]{1,2,0:T(1,128)S(1)}, bf16[4,384,128]{2,1,0...) while((s32[]{:T(128)}, ...), condition=%wide.region_16.19_spmd.clone.clone, body=%wide.region_13.18_spmd.clone.sunk.clone | while | flops 616955136 | bytes 19213456 | solution.py:201
  160.9 2.3 fusion.181
  165.6 2.3 fusion.181
  170.3 2.3 fusion.181
  174.9 2.3 fusion.181
  179.6 2.7 fusion.100
  183.1 4.0 gather_fusion.7
  191.4 112.5 %all-reduce.8.cloned.1.call-done = f32[384,2048]{1,0:T(8,128)} async-done(((f32[384,2048]{1,0:T(8,128)}), f32[384,2048]{1,0:T(8,128)}) %all-reduce.8.cloned.1.call-update) | async-done | bytes 3145744 | tf_op jit(solution)/shard_map/psum | solution.py:203
  303.9 3.2 multiply_reduce_fusion.3
  308.4 6.1 fusion.101
  314.6 3.9 fusion.102
  318.6 6.5 multiply_convert_fusion.2
  325.1 2.6 fusion.103
  327.8 4.3 convolution_add_fusion
  332.2 6.7 convolution_convert_fusion
  339.2 113.1 %all-reduce.12.cloned.1.call-done = f32[384,2048]{1,0:T(8,128)} async-done(((f32[384,2048]{1,0:T(8,128)}), f32[384,2048]{1,0:T(8,128)}) %all-reduce.12.cloned.1.call-update) | async-done | bytes 3145744 | tf_op jit(solution)/shard_map/psum | solution.py:225
  452.4 5.0 multiply_reduce_fusion.1
  457.4 65.0 %all-reduce.10.cloned.1.call-done = bf16[384,2048]{1,0:T(8,128)(2,1)} async-done(((bf16[384,2048]{1,0:T(8,128)(2,1)}), bf16[384,2048]{1,0:T(8,128)(2,1)}) %all-reduce.10.cloned.1.call-update) | async-done | bytes 1572880 | tf_op jit(solution)/shard_map/psum | solution.py:212
  522.4 7.0 fusion.38
  531.0 44.1 %while.35 = (s32[]{:T(128)}, f32[4,384,128]{1,2,0:T(8,128)}, f32[4,3072,128]{2,1,0:T(8,128)}, f32[4,3072,128]{2,1,0:T(8,128)}, bf16[4,384,128]{2,1,0:T(8,128)(2,...) while((s32[]{:T(128)}, f32[4,384,128]{1,2,0:T(8,128)}, ...), condition=%wide.region_25.30_spmd.clone.clone, body=%wide.region_23.29_spmd.clone.sunk.clone | while | flops 1525726848 | bytes 42315408 | solution.py:263
  533.0 2.2 multiply_reduce_fusion.6
  544.0 2.2 multiply_reduce_fusion.6
  549.4 2.1 fusion.196
  555.1 2.2 multiply_reduce_fusion.6
  566.0 2.2 multiply_reduce_fusion.6
  575.1 3.3 reduce_sum.185
  580.2 4.6 reduce_sum.186
  585.4 33.4 %reduce-scatter.10.cloned.1.call-done = f32[384,128]{0,1:T(8,128)} async-done(((f32[3072,128]{0,1:T(8,128)}), f32[384,128]{0,1:T(8,128)}) %reduce-scatter.10.cloned.1.call-update) | async-done | bytes 196624 | tf_op jit(solution)/shard_map/reduce_scatter | solution.py:279
  620.3 2.3 fusion.74
  622.5 37.9 %reduce-scatter.12.cloned.1.call-done = f32[384,128]{1,0:T(8,128)} async-done(((f32[3072,128]{1,0:T(8,128)}), f32[384,128]{1,0:T(8,128)}) %reduce-scatter.12.cloned.1.call-update) | async-done | bytes 196624 | tf_op jit(solution)/shard_map/reduce_scatter | solution.py:280
  662.6 2.7 add_add_fusion
  665.4 3.1 fusion.77
  670.3 5.1 fusion.104
  676.4 5.1 fusion.55
  683.2 6.2 fusion.105
  690.6 6.1 fusion.106
  698.5 6.0 fusion.107
  705.3 4.4 gather_fusion.4
  709.8 76.8 %all-reduce.14.cloned.1.call-done = f32[384,2048]{1,0:T(8,128)} async-done(((f32[384,2048]{1,0:T(8,128)}), f32[384,2048]{1,0:T(8,128)}) %all-reduce.14.cloned.1.call-update) | async-done | bytes 3145744 | tf_op jit(solution)/shard_map/psum | solution.py:296
  786.6 3.0 fusion.52
  789.9 4.3 fusion.42
  794.2 4.3 gather_fusion.8
  798.6 5.5 select_select_fusion
  804.1 56.2 %all_to_all.20 = bf16[8,128,2048]{2,1,0:T(8,128)(2,1)} all-to-all(bf16[8,128,2048]{2,1,0:T(8,128)(2,1)S(1)} %get-tuple-element.428), channel_id=1, replica_groups=mesh['tok'=8,'tp'=4] {'tok'}, dimensions={0} | all-to-all | bytes 8388608 | tf_op jit(solution)/shard_map/all_to_all | solution.py:320
  860.3 5.9 all-to-all-start.3
  867.5 68.6 %all-reduce.2 = (f32[2048]{0:T(1024)S(1)}, f32[2048]{0:T(1024)S(1)}) all-reduce(f32[2048]{0:T(1024)S(1)} %get-tuple-element.334, f32[2048]{0:T(1024)S(1)} %copy-done.42), channel_id=4, replica_groups=mesh['tok'=8,'tp'=4] {'tok'}, use_global_device_ids=true, to_apply=%region_33.38.clone | all-reduce | flops 4096 | bytes 32768
  937.4 4.7 gather_fusion.5
  942.2 4.7 gather_fusion.9
  946.9 8.5 select_select_fusion.4
  955.4 40.5 %reduce-scatter.20.cloned.1.call-done = f32[512,256]{1,0:T(8,128)} async-done(((f32[512,2048]{1,0:T(8,128)}), f32[512,256]{1,0:T(8,128)}) %reduce-scatter.20.cloned.1.call-update) | async-done | bytes 524304 | tf_op jit(solution)/shard_map/reduce_scatter | solution.py:347
  996.0 90.9 %reduce-scatter.22.cloned.1.call-done = f32[256,1408]{1,0:T(8,128)} async-done(((f32[2048,1408]{1,0:T(8,128)}), f32[256,1408]{1,0:T(8,128)}) %reduce-scatter.22.cloned.1.call-update) | async-done | bytes 1441808 | tf_op jit(solution)/shard_map/reduce_scatter | solution.py:231
  1086.9 90.8 %reduce-scatter.24.cloned.1.call-done = f32[256,1408]{1,0:T(8,128)} async-done(((f32[2048,1408]{1,0:T(8,128)}), f32[256,1408]{1,0:T(8,128)}) %reduce-scatter.24.cloned.1.call-update) | async-done | bytes 1441808 | tf_op jit(solution)/shard_map/reduce_scatter | solution.py:232
  1177.6 90.9 %reduce-scatter.26.cloned.1.call-done = f32[1408,256]{1,0:T(8,128)} async-done(((f32[1408,2048]{1,0:T(8,128)}), f32[1408,256]{1,0:T(8,128)}) %reduce-scatter.26.cloned.1.call-update) | async-done | bytes 1441808 | tf_op jit(solution)/shard_map/reduce_scatter | solution.py:233
  (299 shorter events, 84.3 us)
Async XLA Ops:
  7.2 172.4 %copy-start = (bf16[512,2048]{1,0:T(8,128)(2,1)S(1)}, bf16[512,2048]{1,0:T(8,128)(2,1)}, u32[]{:S(2)}) copy-start(bf16[512,2048]{1,0:T(8,128)(2,1)} %param.30) | copy-start | bytes 6291460
  9.9 5.3 copy-start.54
  25.9 50.9 %all-to-all-start = ((bf16[8,128,2048]{2,1,0:T(8,128)(2,1)}), bf16[8,128,2048]{2,1,0:T(8,128)(2,1)}, u32[]{:S(2)}, u32[]{:S(2)}) async-start(bf16[8,128,2048]{2,1,0:T(8,128)(2,1)} %get-tuple-element.430), calls=%async_computation | async-start | bytes 8388608 | tf_op jit(solution)/shard_map/all_to_all | solution.py:120
  31.1 6.0 copy-start.56
  31.1 6.1 copy-start.53
  36.7 56.8 %copy-start.48 = (f32[64]{0:T(128)}, f32[64]{0:T(128)S(1)}, u32[]{:S(2)}) copy-start(f32[64]{0:T(128)S(1)} %multiply_exponential_fusion) | copy-start | bytes 772
  36.8 40.0 %copy-start.58 = (s32[3]{0:T(128)}, s32[3]{0:T(128)S(1)}, u32[]{:S(2)}) copy-start(s32[3]{0:T(128)S(1)} %get-tuple-element.395) | copy-start | bytes 40
  37.4 56.1 %copy-start.40 = (f32[384]{0:T(512)}, f32[384]{0:T(512)S(1)}, u32[]{:S(2)}) copy-start(f32[384]{0:T(512)S(1)} %subtract_convert_fusion.1) | copy-start | bytes 4612
  37.8 120.3 %copy-start.31 = (f32[384,64]{0,1:T(8,128)}, f32[384,64]{0,1:T(8,128)S(1)}, u32[]{:S(2)}) copy-start(f32[384,64]{0,1:T(8,128)S(1)} %get-tuple-element.417) | copy-start | bytes 294916
  37.8 120.3 %copy-start.33 = (f32[384,64]{0,1:T(8,128)}, f32[384,64]{0,1:T(8,128)S(1)}, u32[]{:S(2)}) copy-start(f32[384,64]{0,1:T(8,128)S(1)} %get-tuple-element.418) | copy-start | bytes 294916
  76.8 106.3 %all-to-all-start.2 = ((bf16[8,128,2048]{2,1,0:T(8,128)(2,1)}), bf16[8,128,2048]{2,1,0:T(8,128)(2,1)}, u32[]{:S(2)}, u32[]{:S(2)}) async-start(bf16[8,128,2048]{2,1,0:T(8,128)(2,1)} %get-tuple-element.429), calls=%async_computation.2 | async-start | bytes 8388608 | tf_op jit(solution)/shard_map/all_to_all | solution.py:127
  84.8 6.1 copy-start.37
  84.8 219.2 %all-reduce.8.cloned.1.call-start = ((), (), s32[]{:S(2)}) async-start(), calls=%async_computation.13 | async-start | bytes 6291456 | tf_op jit(solution)/shard_map/psum | solution.py:203
  88.8 4.1 copy-start.23
  90.8 50.2 %copy-start.45 = (f32[3,128]{1,0:T(4,128)}, f32[3,128]{1,0:T(4,128)S(1)}, u32[]{:S(2)}) copy-start(f32[3,128]{1,0:T(4,128)S(1)} %fusion.43) | copy-start | bytes 4612
  90.9 50.2 %copy-start.43 = (f32[384]{0:T(512)}, f32[384]{0:T(512)S(1)}, u32[]{:S(2)}) copy-start(f32[384]{0:T(512)S(1)} %get-tuple-element.423) | copy-start | bytes 4612
  92.9 48.1 %copy-start.9 = (bf16[384,2048]{1,0:T(8,128)(2,1)}, bf16[384,2048]{1,0:T(8,128)(2,1)S(1)}, u32[]{:S(2)}) copy-start(bf16[384,2048]{1,0:T(8,128)(2,1)S(1)} %fusion.47) | copy-start | bytes 4718596
  142.6 13.7 %copy-start.2 = (bf16[3,128,2048]{2,1,0:T(8,128)(2,1)S(1)}, bf16[3,128,2048]{2,1,0:T(8,128)(2,1)}, u32[]{:S(2)}) copy-start(bf16[3,128,2048]{2,1,0:T(8,128)(2,1)} %gather_fusion.3) | copy-start | bytes 4718596
  142.6 14.2 %copy-start.22 = (bf16[512,2048]{1,0:T(8,128)(2,1)S(1)}, bf16[512,2048]{1,0:T(8,128)(2,1)}, u32[]{:S(2)}) copy-start(bf16[512,2048]{1,0:T(8,128)(2,1)} %copy.63) | copy-start | bytes 6291460
  182.3 270.0 %all-reduce.12.cloned.1.call-start = ((), (), s32[]{:S(2)}) async-start(), calls=%async_computation.15 | async-start | bytes 6291456 | tf_op jit(solution)/shard_map/psum | solution.py:225
  191.4 115.7 %copy-start.39 = (f32[2048]{0:T(1024)S(1)}, f32[2048]{0:T(1024)}, u32[]{:S(2)}) copy-start(f32[2048]{0:T(1024)} %param.31) | copy-start | bytes 24580
  303.9 3.2 copy-start.3
  303.9 3.8 copy-start.5
  307.7 6.8 slice-start.2
  308.4 6.2 copy-start.14
  308.4 6.2 slice-start.3
  308.4 10.2 slice-start.4
  314.6 4.0 copy-start.18
  314.6 4.0 slice-start.5
  314.6 10.5 slice-start
  318.6 6.5 slice-start.1
  332.1 190.3 %all-reduce.10.cloned.1.call-start = ((), (), s32[]{:S(2)}) async-start(), calls=%async_computation.14 | async-start | bytes 3145728 | tf_op jit(solution)/shard_map/psum | solution.py:212
  338.9 279.9 %reduce-scatter.10.cloned.1.call-start = ((), (), s32[]{:S(2)}) async-start(), calls=%async_computation.16 | async-start | bytes 1769472 | tf_op jit(solution)/shard_map/reduce_scatter | solution.py:279
  580.1 80.4 %reduce-scatter.12.cloned.1.call-start = ((), (), s32[]{:S(2)}) async-start(), calls=%async_computation.17 | async-start | bytes 1769472 | tf_op jit(solution)/shard_map/reduce_scatter | solution.py:280
  580.1 5.1 copy-start.32
  580.1 5.1 copy-start.34
  580.2 5.1 copy-start.35
  584.8 34.1 %copy-start.41 = (f32[384]{0:T(512)S(1)}, f32[384]{0:T(512)}, u32[]{:S(2)}) copy-start(f32[384]{0:T(512)} %copy-done.40) | copy-start | bytes 4612
  584.8 34.1 %copy-start.49 = (f32[64]{0:T(128)S(1)}, f32[64]{0:T(128)}, u32[]{:S(2)}) copy-start(f32[64]{0:T(128)} %copy-done.48) | copy-start | bytes 772
  584.8 35.5 %copy-start.24 = (bf16[2048,128]{1,0:T(8,128)(2,1)S(1)}, bf16[2048,128]{1,0:T(8,128)(2,1)}, u32[]{:S(2)}) copy-start(bf16[2048,128]{1,0:T(8,128)(2,1)} %param.28) | copy-start | bytes 1572868
  584.8 201.8 %all-reduce.14.cloned.1.call-start = ((), (), s32[]{:S(2)}) async-start(), calls=%async_computation.18 | async-start | bytes 6291456 | tf_op jit(solution)/shard_map/psum | solution.py:296
  620.3 42.1 %copy-start.17 = (bf16[2048,512]{1,0:T(8,128)(2,1)S(1)}, bf16[2048,512]{1,0:T(8,128)(2,1)}, u32[]{:S(2)}) copy-start(bf16[2048,512]{1,0:T(8,128)(2,1)} %param.27) | copy-start | bytes 6291460
  665.3 3.3 copy-start.10
  665.3 3.3 copy-start.36
  665.4 290.0 %reduce-scatter.16.cloned.1.call-start = ((), (), s32[]{:S(2)}) async-start(), calls=%async_computation.20 | async-start | bytes 1179648 | tf_op jit(solution)/shard_map/reduce_scatter | solution.py:345
  668.5 286.9 %reduce-scatter.18.cloned.1.call-start = ((), (), s32[]{:S(2)}) async-start(), calls=%async_computation.21 | async-start | bytes 1179648 | tf_op jit(solution)/shard_map/reduce_scatter | solution.py:346
  670.3 285.2 %reduce-scatter.14.cloned.1.call-start = ((), (), s32[]{:S(2)}) async-start(), calls=%async_computation.19 | async-start | bytes 4718592 | tf_op jit(solution)/shard_map/reduce_scatter | solution.py:344
  675.4 320.6 %reduce-scatter.20.cloned.1.call-start = ((), (), s32[]{:S(2)}) async-start(), calls=%async_computation.22 | async-start | bytes 4718592 | tf_op jit(solution)/shard_map/reduce_scatter | solution.py:347
  681.5 405.3 %reduce-scatter.22.cloned.1.call-start = ((), (), s32[]{:S(2)}) async-start(), calls=%async_computation.23 | async-start | bytes 12976128 | tf_op jit(solution)/shard_map/reduce_scatter | solution.py:231
  689.4 488.2 %reduce-scatter.24.cloned.1.call-start = ((), (), s32[]{:S(2)}) async-start(), calls=%async_computation.24 | async-start | bytes 12976128 | tf_op jit(solution)/shard_map/reduce_scatter | solution.py:232
  696.7 571.8 %reduce-scatter.26.cloned.1.call-start = ((), (), s32[]{:S(2)}) async-start(), calls=%async_computation.25 | async-start | bytes 12976128 | tf_op jit(solution)/shard_map/reduce_scatter | solution.py:233
  705.3 81.3 %copy-start.4 = (bf16[3,128,2048]{2,1,0:T(8,128)(2,1)S(1)}, bf16[3,128,2048]{2,1,0:T(8,128)(2,1)}, u32[]{:S(2)}) copy-start(bf16[3,128,2048]{2,1,0:T(8,128)(2,1)} %gather_fusion.3) | copy-start | bytes 4718596
  705.3 81.3 %copy-start.38 = (f32[2048]{0:T(1024)S(1)}, f32[2048]{0:T(1024)}, u32[]{:S(2)}) copy-start(f32[2048]{0:T(1024)} %param.26) | copy-start | bytes 24580
  705.3 81.2 %copy-start.44 = (f32[384]{0:T(512)S(1)}, f32[384]{0:T(512)}, u32[]{:S(2)}) copy-start(f32[384]{0:T(512)} %copy-done.43) | copy-start | bytes 4612
  709.8 79.8 %copy-start.47 = (f32[384]{0:T(512)S(1)}, f32[384]{0:T(512)}, u32[]{:S(2)}) copy-start(f32[384]{0:T(512)} %get-tuple-element.419) | copy-start | bytes 4612
  786.6 3.0 copy-start.7
  786.6 3.3 copy-start.12
  860.3 6.0 copy-start.57
  860.3 7.2 copy-start.55
  860.3 7.2 copy-start.42
  860.3 81.9 %all-to-all-start.3 = ((bf16[8,128,2048]{2,1,0:T(8,128)(2,1)}), bf16[8,128,2048]{2,1,0:T(8,128)(2,1)}, u32[]{:S(2)}, u32[]{:S(2)}) async-start(bf16[8,128,2048]{2,1,0:T(8,128)(2,1)} %get-tuple-element.427), calls=%async_computation.5 | async-start | bytes 8388608 | tf_op jit(solution)/shard_map/all_to_all | solution.py:327
  942.2 4.7 copy-start.50
  942.2 4.7 copy-start.52
  946.9 321.6 %copy-start.1 = (bf16[512,2048]{1,0:T(8,128)(2,1)S(1)}, bf16[512,2048]{1,0:T(8,128)(2,1)}, u32[]{:S(2)}) copy-start(bf16[512,2048]{1,0:T(8,128)(2,1)} %param.30) | copy-start | bytes 6291460
  (21 other events, 31.2 us)
Sparse Core Ops, SparseCore 0:
  182.4 121.4 all-reduce.7
  332.2 120.0 all-reduce.11
  455.3 67.0 all-reduce.9
  580.2 38.6 reduce-scatter.9
  622.0 38.4 reduce-scatter.11
  665.5 121.0 all-reduce.13
  790.3 44.3 reduce-scatter.15
  838.4 37.2 reduce-scatter.17
  879.7 60.8 reduce-scatter.13
  944.7 51.2 reduce-scatter.19
  1000.1 86.7 reduce-scatter.21
  1090.8 86.7 reduce-scatter.23
  1181.7 86.7 reduce-scatter.25
where the time goes:
time: 1280 us
  waiting for transfers between devices  791 us (62%)
  blocking collectives  183 us (14%)
  matrix products  128 us (10%)
  other arithmetic  74.4 us (6%)
  local copies, waits for them, and re-layouts  62.1 us (5%)
  starting transfers between devices  20.6 us (2%)
  between operations  15.6 us (1%)
    psum x1, waiting for transfers between devices, on_device(): lax.psum(over_columns(grad_gate_pre, w_gate) + over_columns(grad_up_pre,...  113 us
    psum x1, waiting for transfers between devices, on_device(): lax.psum(jnp.dot(attended, w_out, preferred_element_type=jnp.float32), 'tp')  113 us
    reduce_scatter x1, waiting for transfers between devices, on_device(): lax.psum_scatter(grad_down, 'tok', scatter_dimension=1, tiled=True)  90.9 us
    reduce_scatter x1, waiting for transfers between devices, on_device(): lax.psum_scatter(grad_gate, 'tok', scatter_dimension=0, tiled=True)  90.9 us
    reduce_scatter x1, waiting for transfers between devices, on_device(): lax.psum_scatter(grad_up, 'tok', scatter_dimension=0, tiled=True)  90.8 us
    psum x1, waiting for transfers between devices, on_device(): lax.psum(over_columns(grad_query_pre, w_query) + over_columns(grad_key_pr...  76.8 us
    unnamed x1, blocking collectives  68.6 us
    psum x1, waiting for transfers between devices, on_device(): lax.psum(jnp.dot(inner, w_down, preferred_element_type=jnp.float32).astyp...  65 us
  transfers between devices with their start and end apart: 16, of which 11 were waited for; matrix products, arithmetic and copies ran while one was open for 11% of the time, Pallas kernels for 0%

commit v1 on v0

v1 whole, which is shorter than its diff:
```python
import functools
import math

import jax
import jax.numpy as jnp
from jax import lax
from jax.experimental import pallas as pl
from jax.experimental.pallas import tpu as pltpu
from jax.sharding import PartitionSpec as P

HD = 128
BLOCK = 128
SLOTS = 3
CHUNKS = 8
MESH = pl.DeviceIdType.MESH
VMEM_BYTES = 60 * 2**20

norm_eps = 1e-05
keep_scale = 2.0
F32 = jnp.float32
BF16 = jnp.bfloat16


def vmem():
    return pl.BlockSpec(memory_space=pltpu.VMEM)


def smem():
    return pl.BlockSpec(memory_space=pltpu.SMEM)


def params(collective_id):
    return pltpu.CompilerParams(
        collective_id=collective_id, has_side_effects=True, vmem_limit_bytes=VMEM_BYTES
    )


def cost(flops, moved):
    return pl.CostEstimate(flops=flops, bytes_accessed=moved, transcendentals=0)


def greet(peers):
    barrier = pltpu.get_barrier_semaphore()
    for peer in peers:
        pl.semaphore_signal(barrier, inc=1, device_id=peer, device_id_type=MESH)
    pl.semaphore_wait(barrier, len(peers))


def deal_tables(own, stages, blocks_here, lens_ref, flags_ref):
    def kept_before(place):
        total, start = jnp.int32(0), jnp.int32(0)
        for doc in range(lens_ref.shape[0]):
            blocks = lens_ref[doc] // BLOCK
            total = total + flags_ref[doc] * jnp.clip(place - start, 0, blocks)
            start = start + blocks
        return total

    def edges(stage):
        first = (own >> stage) << stage
        return (
            kept_before(first * blocks_here),
            kept_before((first + (1 << stage)) * blocks_here),
        )

    def located(stage):
        if stage == 0:
            ends = [kept_before(own * blocks_here + i + 1) for i in range(blocks_here)]

            def place(rank):
                index = jnp.int32(0)
                for end in ends:
                    index = index + (end <= rank).astype(jnp.int32)
                return index

            return place
        mine = (own >> (stage - 1)) << (stage - 1)
        low, high = edges(stage - 1)
        other = kept_before((mine ^ (1 << (stage - 1))) * blocks_here)

        def place(rank):
            inside = (rank >= low) & (rank < high)
            return jnp.where(inside, (rank - low) >> stage, SLOTS + ((rank - other) >> stage))

        return place

    keeps, sends = [], []
    for stage in range(stages):
        low, high = edges(stage)
        place = located(stage)
        period = 1 << (stage + 1)
        for table, target in ((keeps, own), (sends, own ^ (1 << stage))):
            first = low + ((target - low) & (period - 1))
            row = []
            for slot in range(SLOTS):
                rank = first + period * slot
                row.append(jnp.where(rank < high, place(rank), -1))
            table.append(row)
    place = located(stages)
    finals = [place(own + (slot << stages)) for slot in range(SLOTS)]
    return keeps, sends, finals


def choose(index, options, default=None):
    value = options[0] if default is None else default
    for number, option in enumerate(options):
        if number == 0 and default is None:
            continue
        value = jnp.where(index == number, option, value)
    return value


def deal_body(lens_ref, flags_ref, own_ref, out_ref, keep, send, recv, send_sem, recv_sem):
    stages = keep.shape[0]
    own = lax.axis_index("tok")
    plane = lax.axis_index("tp")
    blocks_here = own_ref.shape[0]
    rows = BLOCK // CHUNKS
    peers = [(own ^ (1 << stage), plane) for stage in range(stages)]
    greet(peers)
    keeps, sends, finals = deal_tables(own, stages, blocks_here, lens_ref, flags_ref)

    def copy(stage, chunk):
        return pltpu.make_async_remote_copy(
            src_ref=send.at[stage, chunk],
            dst_ref=recv.at[stage, chunk],
            send_sem=send_sem.at[stage, chunk],
            recv_sem=recv_sem.at[stage, chunk],
            device_id=peers[stage],
            device_id_type=MESH,
        )

    def held(stage, chunk):
        if stage == 0:
            span = pl.ds(pl.multiple_of(chunk * rows, rows), rows)
            return [own_ref[i, span, :] for i in range(blocks_here)]
        before = stage - 1
        return [keep[before, chunk, i] for i in range(SLOTS)] + [
            recv[before, chunk, i] for i in range(SLOTS)
        ]

    for stage in range(stages):

        def step(chunk, carry, stage=stage):
            if stage > 0:
                copy(stage - 1, chunk).wait_recv()
            options = held(stage, chunk)
            for slot in range(SLOTS):
                send[stage, chunk, slot] = choose(sends[stage][slot], options)
            copy(stage, chunk).start()
            for slot in range(SLOTS):
                keep[stage, chunk, slot] = choose(keeps[stage][slot], options)
            return carry

        lax.fori_loop(0, CHUNKS, step, 0)

    def finish(chunk, carry):
        copy(stages - 1, chunk).wait_recv()
        options = held(stages, chunk)
        span = pl.ds(pl.multiple_of(chunk * rows, rows), rows)
        for slot in range(SLOTS):
            out_ref[slot, span, :] = choose(finals[slot], options)
        return carry

    lax.fori_loop(0, CHUNKS, finish, 0)

    def drain(chunk, carry):
        for stage in range(stages):
            copy(stage, chunk).wait_send()
        return carry

    lax.fori_loop(0, CHUNKS, drain, 0)


def stages_of(axis):
    return int(math.log2(lax.axis_size(axis)))


def deal(doc_lengths, keep_flags, blocks, collective_id):
    stages = stages_of("tok")
    width = blocks.shape[2]
    rows = BLOCK // CHUNKS
    moved = (stages, CHUNKS, SLOTS, rows, width)
    return pl.pallas_call(
        deal_body,
        out_shape=jax.ShapeDtypeStruct((SLOTS, BLOCK, width), blocks.dtype),
        in_specs=[smem(), smem(), vmem()],
        out_specs=vmem(),
        scratch_shapes=[
            pltpu.VMEM(moved, blocks.dtype),
            pltpu.VMEM(moved, blocks.dtype),
            pltpu.VMEM(moved, blocks.dtype),
            pltpu.SemaphoreType.DMA((stages, CHUNKS)),
            pltpu.SemaphoreType.DMA((stages, CHUNKS)),
        ],
        compiler_params=params(collective_id),
        cost_estimate=cost(0, 40_000_000),
        name="deal",
    )(doc_lengths, keep_flags, blocks)


def undeal_body(
    lens_ref, flags_ref, kept_ref, home_ref, gains_ref, out_ref, sum_ref,
    hold, recv, gain_recv, send_sem, recv_sem, gain_send_sem, gain_recv_sem,
):
    stages = recv.shape[0]
    own = lax.axis_index("tok")
    plane = lax.axis_index("tp")
    devices = 1 << stages
    blocks_here = home_ref.shape[0]
    rows = BLOCK // CHUNKS
    share = sum_ref.shape[1]
    peers = [(own ^ (1 << stage), plane) for stage in range(stages)]
    greet([(own ^ step, plane) for step in range(1, devices)])

    def gain_copy(step):
        there = own ^ step
        return pltpu.make_async_remote_copy(
            src_ref=gains_ref.at[:, pl.ds(pl.multiple_of(there * share, share), share)]
            if share % 128 == 0
            else gains_ref,
            dst_ref=gain_recv.at[step],
            send_sem=gain_send_sem.at[step],
            recv_sem=gain_recv_sem.at[step],
            device_id=(there, plane),
            device_id_type=MESH,
        )

    for step in range(1, devices):
        gain_copy(step).start()
    keeps, sends, finals = deal_tables(own, stages, blocks_here, lens_ref, flags_ref)

    def copy(stage, chunk):
        return pltpu.make_async_remote_copy(
            src_ref=hold.at[stage, chunk, pl.ds(SLOTS, SLOTS)],
            dst_ref=recv.at[stage, chunk],
            send_sem=send_sem.at[stage, chunk],
            recv_sem=recv_sem.at[stage, chunk],
            device_id=peers[stage],
            device_id_type=MESH,
        )

    last = stages - 1

    def begin(chunk, carry):
        span = pl.ds(pl.multiple_of(chunk * rows, rows), rows)
        options = [kept_ref[slot, span, :] for slot in range(SLOTS)]
        for place in range(SLOTS, 2 * SLOTS):
            value = options[0]
            for slot in range(1, SLOTS):
                value = jnp.where(finals[slot] == place, options[slot], value)
            hold[last, chunk, place] = value
        copy(last, chunk).start()
        for place in range(SLOTS):
            value = options[0]
            for slot in range(1, SLOTS):
                value = jnp.where(finals[slot] == place, options[slot], value)
            hold[last, chunk, place] = value
        return carry

    lax.fori_loop(0, CHUNKS, begin, 0)
    for stage in range(last, -1, -1):

        def step(chunk, carry, stage=stage):
            copy(stage, chunk).wait_recv()
            options = [hold[stage, chunk, i] for i in range(SLOTS)] + [
                recv[stage, chunk, i] for i in range(SLOTS)
            ]
            places = keeps[stage] + sends[stage]

            def pick(place, value):
                for index, option in zip(places, options):
                    value = jnp.where(index == place, option, value)
                return value

            if stage == 0:
                span = pl.ds(pl.multiple_of(chunk * rows, rows), rows)
                for place in range(blocks_here):
                    out_ref[place, span, :] = pick(place, home_ref[place, span, :])
            else:
                for place in range(SLOTS, 2 * SLOTS):
                    hold[stage - 1, chunk, place] = pick(place, options[0])
                copy(stage - 1, chunk).start()
                for place in range(SLOTS):
                    hold[stage - 1, chunk, place] = pick(place, options[0])
            return carry

        lax.fori_loop(0, CHUNKS, step, 0)

    def drain(chunk, carry):
        for stage in range(stages):
            copy(stage, chunk).wait_send()
        return carry

    lax.fori_loop(0, CHUNKS, drain, 0)
    if share % 128 == 0:
        total = gains_ref[:, pl.ds(pl.multiple_of(own * share, share), share)]
    else:
        total = gains_ref[...]
    for step in range(1, devices):
        gain_copy(step).wait()
        total = total + gain_recv[step]
    sum_ref[...] = total


def undeal(doc_lengths, keep_flags, kept, home, gains, collective_id):
    stages = stages_of("tok")
    devices = 1 << stages
    width = kept.shape[2]
    rows = BLOCK // CHUNKS
    share = width // devices
    share = share if share % 128 == 0 else width
    return pl.pallas_call(
        undeal_body,
        out_shape=(
            jax.ShapeDtypeStruct(home.shape, home.dtype),
            jax.ShapeDtypeStruct((8, share), F32),
        ),
        in_specs=[smem(), smem(), vmem(), vmem(), vmem()],
        out_specs=(vmem(), vmem()),
        scratch_shapes=[
            pltpu.VMEM((stages, CHUNKS, 2 * SLOTS, rows, width), kept.dtype),
            pltpu.VMEM((stages, CHUNKS, SLOTS, rows, width), kept.dtype),
            pltpu.VMEM((devices, 8, share), F32),
            pltpu.SemaphoreType.DMA((stages, CHUNKS)),
            pltpu.SemaphoreType.DMA((stages, CHUNKS)),
            pltpu.SemaphoreType.DMA((devices,)),
            pltpu.SemaphoreType.DMA((devices,)),
        ],
        compiler_params=params(collective_id),
        cost_estimate=cost(0, 40_000_000),
        name="undeal",
    )(doc_lengths, keep_flags, kept, home, gains)


def gather_tok_body(mine_ref, out_ref, send_sem, recv_sem, relay_send_sem, relay_recv_sem):
    devices = out_ref.shape[0]
    chips = devices // 2
    own = lax.axis_index("tok")
    plane = lax.axis_index("tp")
    partner = (own ^ 1, plane)
    greet([partner] + [(own ^ (2 * step), plane) for step in range(1, chips)])

    def copy(step):
        return pltpu.make_async_remote_copy(
            src_ref=mine_ref,
            dst_ref=out_ref.at[own],
            send_sem=send_sem.at[step],
            recv_sem=recv_sem.at[step],
            device_id=(own ^ (2 * step), plane),
            device_id_type=MESH,
        )

    def relay(step):
        return pltpu.make_async_remote_copy(
            src_ref=mine_ref if step == 0 else out_ref.at[own ^ (2 * step)],
            dst_ref=out_ref.at[own ^ (2 * step)],
            send_sem=relay_send_sem.at[step],
            recv_sem=relay_recv_sem.at[step],
            device_id=partner,
            device_id_type=MESH,
        )

    for step in range(1, chips):
        copy(step).start()
    relay(0).start()
    out_ref[own] = mine_ref[...]
    for step in range(1, chips):
        copy(step).wait_recv()
        relay(step).start()
    for step in range(chips):
        relay(step).wait()
    for step in range(1, chips):
        copy(step).wait_send()


def gather_tok(mine, collective_id):
    devices = lax.axis_size("tok")
    chips = devices // 2
    return pl.pallas_call(
        gather_tok_body,
        out_shape=jax.ShapeDtypeStruct((devices,) + mine.shape, mine.dtype),
        in_specs=[vmem()],
        out_specs=vmem(),
        scratch_shapes=[pltpu.SemaphoreType.DMA((chips,))] * 4,
        compiler_params=params(collective_id),
        cost_estimate=cost(0, 10_000_000),
        name="gather_tok",
    )(mine)


def scatter_tok_body(
    part_ref, out_ref, core_recv, held, recv, core_send_sem, core_recv_sem, send_sem, recv_sem
):
    devices = part_ref.shape[0]
    chips = devices // 2
    own = lax.axis_index("tok")
    plane = lax.axis_index("tp")
    partner = (own ^ 1, plane)
    greet([partner] + [(own ^ (2 * step), plane) for step in range(1, chips)])

    def core_copy(step):
        return pltpu.make_async_remote_copy(
            src_ref=part_ref.at[own ^ (2 * step) ^ 1],
            dst_ref=core_recv.at[step],
            send_sem=core_send_sem.at[step],
            recv_sem=core_recv_sem.at[step],
            device_id=partner,
            device_id_type=MESH,
        )

    def copy(step):
        return pltpu.make_async_remote_copy(
            src_ref=held.at[step],
            dst_ref=recv.at[step],
            send_sem=send_sem.at[step],
            recv_sem=recv_sem.at[step],
            device_id=(own ^ (2 * step), plane),
            device_id_type=MESH,
        )

    order = list(range(chips - 1, -1, -1))
    for step in order:
        core_copy(step).start()
    for step in order:
        core_copy(step).wait_recv()
        total = part_ref[own ^ (2 * step)].astype(F32) + core_recv[step].astype(F32)
        if step > 0:
            held[step] = total.astype(held.dtype)
            copy(step).start()
        else:
            out_ref[...] = total
    for step in range(1, chips):
        copy(step).wait_recv()
        out_ref[...] += recv[step].astype(F32)
    for step in range(1, chips):
        copy(step).wait_send()
    for step in range(chips):
        core_copy(step).wait_send()


def scatter_tok(part, collective_id):
    devices = part.shape[0]
    chips = devices // 2
    shard = part.shape[1:]
    return pl.pallas_call(
        scatter_tok_body,
        out_shape=jax.ShapeDtypeStruct(shard, F32),
        in_specs=[vmem()],
        out_specs=vmem(),
        scratch_shapes=[
            pltpu.VMEM((chips,) + shard, part.dtype),
            pltpu.VMEM((chips,) + shard, part.dtype),
            pltpu.VMEM((chips,) + shard, part.dtype),
        ]
        + [pltpu.SemaphoreType.DMA((chips,))] * 4,
        compiler_params=params(collective_id),
        cost_estimate=cost(0, 10_000_000),
        name="scatter_tok",
    )(part)


def line_copies(own, plane, sources, targets, send_sem, recv_sem):
    def right(index):
        return pltpu.make_async_remote_copy(
            src_ref=sources.at[index],
            dst_ref=targets.at[index],
            send_sem=send_sem.at[0, index],
            recv_sem=recv_sem.at[0, index],
            device_id=(own, plane + 1),
            device_id_type=MESH,
        )

    def left(index):
        return pltpu.make_async_remote_copy(
            src_ref=sources.at[index],
            dst_ref=targets.at[index],
            send_sem=send_sem.at[1, index],
            recv_sem=recv_sem.at[1, index],
            device_id=(own, plane - 1),
            device_id_type=MESH,
        )

    return right, left


def line_greet(own, plane, planes):
    barrier = pltpu.get_barrier_semaphore()

    @pl.when(plane > 0)
    def _():
        pl.semaphore_signal(barrier, inc=1, device_id=(own, plane - 1), device_id_type=MESH)

    @pl.when(plane < planes - 1)
    def _():
        pl.semaphore_signal(barrier, inc=1, device_id=(own, plane + 1), device_id_type=MESH)

    end = (plane == 0) | (plane == planes - 1)

    @pl.when(end)
    def _():
        pl.semaphore_wait(barrier, 1)

    @pl.when(jnp.logical_not(end))
    def _():
        pl.semaphore_wait(barrier, 2)


def line_gather(own, plane, planes, out, send_sem, recv_sem):
    right, left = line_copies(own, plane, out, out, send_sem, recv_sem)
    last = planes - 1
    for step in range(1, planes + 1):
        before, after = plane - (step - 1), plane + (step - 1)

        @pl.when(before >= 0)
        def _():
            if step > 1:
                right(before).wait_recv()
            if step < planes:

                @pl.when(plane < last)
                def _():
                    right(before).start()

        @pl.when(after <= last)
        def _():
            if step > 1:
                left(after).wait_recv()
            if step < planes:

                @pl.when(plane > 0)
                def _():
                    left(after).start()

    for index in range(planes):

        @pl.when((index <= plane) & (plane < last))
        def _():
            right(index).wait_send()

        @pl.when((index >= plane) & (plane > 0))
        def _():
            left(index).wait_send()


def line_reduce(own, plane, planes, part, total, send, recv, send_sem, recv_sem):
    last = planes - 1
    right, _ = line_copies(own, plane, send.at[0], recv.at[0], send_sem, recv_sem)
    _, left = line_copies(own, plane, send.at[1], recv.at[1], send_sem, recv_sem)
    for step in range(1, planes):
        upper, lower = planes - step + plane, step - planes + plane

        @pl.when((upper <= last) & (plane < last))
        def _():
            @pl.when(plane == 0)
            def _():
                send[0, upper] = part[upper]

            @pl.when(plane > 0)
            def _():
                right(upper).wait_recv()
                send[0, upper] = (
                    part[upper].astype(F32) + recv[0, upper].astype(F32)
                ).astype(send.dtype)

            right(upper).start()

        @pl.when((lower >= 0) & (plane > 0))
        def _():
            @pl.when(plane == last)
            def _():
                send[1, lower] = part[lower]

            @pl.when(plane < last)
            def _():
                left(lower).wait_recv()
                send[1, lower] = (
                    part[lower].astype(F32) + recv[1, lower].astype(F32)
                ).astype(send.dtype)

            left(lower).start()

    total[...] = part[plane].astype(F32)

    @pl.when(plane > 0)
    def _():
        right(plane).wait_recv()
        total[...] += recv[0, plane].astype(F32)

    @pl.when(plane < last)
    def _():
        left(plane).wait_recv()
        total[...] += recv[1, plane].astype(F32)

    for index in range(planes):

        @pl.when((index > plane) & (plane < last))
        def _():
            right(index).wait_send()

        @pl.when((index < plane) & (plane > 0))
        def _():
            left(index).wait_send()


def gather_tp_body(mine_ref, out_ref, send_sem, recv_sem):
    planes = out_ref.shape[0]
    own, plane = lax.axis_index("tok"), lax.axis_index("tp")
    line_greet(own, plane, planes)
    out_ref[plane] = mine_ref[...]
    line_gather(own, plane, planes, out_ref, send_sem, recv_sem)


def gather_tp(mine, collective_id):
    planes = lax.axis_size("tp")
    return pl.pallas_call(
        gather_tp_body,
        out_shape=jax.ShapeDtypeStruct((planes,) + mine.shape, mine.dtype),
        in_specs=[vmem()],
        out_specs=vmem(),
        scratch_shapes=[
            pltpu.SemaphoreType.DMA((2, planes)),
            pltpu.SemaphoreType.DMA((2, planes)),
        ],
        compiler_params=params(collective_id),
        cost_estimate=cost(0, 30_000_000),
        name="gather_tp",
    )(mine)


def row_tiles(rows):
    tile = 16
    return [(start, tile) for start in range(0, rows, tile)]


def ffn_math(plane, total, inputs, outputs, gathered):
    hidden_ref, inv_ref, dy_ref, gain_ref = inputs
    grad_ref, gains_ref = outputs
    gains_ref[...] = jnp.zeros_like(gains_ref)

    def tile(index, carry):
        rows = pl.ds(pl.multiple_of(index * 16, 16), 16)
        dn = total[rows, :]
        hidden = hidden_ref[plane, rows, :]
        inv = inv_ref[plane, rows, :]
        weighted = gain_ref[...] * dn
        mean = jnp.mean(weighted * hidden, axis=1, keepdims=True)
        grad = (
            keep_scale * dy_ref[plane, rows, :].astype(F32)
            + inv * weighted
            - hidden * (inv * inv * inv * mean)
        )
        grad_ref[rows, :] = grad
        gathered[plane, rows, :] = grad.astype(BF16)
        gains_ref[0:1, :] += jnp.sum(dn * hidden * inv, axis=0, keepdims=True)
        return carry

    lax.fori_loop(0, total.shape[0] // 16, tile, 0)


def mixed_math(plane, total, inputs, outputs, gathered):
    hidden_ref, x_ref = inputs

    def tile(index, carry):
        rows = pl.ds(pl.multiple_of(index * 16, 16), 16)
        x = x_ref[plane, rows, :].astype(F32)
        branch = (hidden_ref[plane, rows, :] - x) + total[rows, :]
        gathered[plane, rows, :] = (x + keep_scale * branch).astype(BF16)
        return carry

    lax.fori_loop(0, total.shape[0] // 16, tile, 0)


def attn_math(plane, total, inputs, outputs, gathered):
    x_ref, inv_ref, dy_ref, grad_ref, gain_ref, ffn_gains_ref = inputs
    (gains_ref,) = outputs
    gains_ref[...] = ffn_gains_ref[...]

    def tile(index, carry):
        rows = pl.ds(pl.multiple_of(index * 16, 16), 16)
        dn = total[rows, :]
        x = x_ref[plane, rows, :].astype(F32)
        inv = inv_ref[plane, rows, :]
        weighted = gain_ref[...] * dn
        mean = jnp.mean(weighted * x, axis=1, keepdims=True)
        grad = (
            (1.0 - keep_scale) * dy_ref[plane, rows, :].astype(F32)
            + grad_ref[rows, :]
            + inv * weighted
            - x * (inv * inv * inv * mean)
        )
        gathered[plane, rows, :] = grad.astype(BF16)
        gains_ref[1:2, :] += jnp.sum(dn * x * inv, axis=0, keepdims=True)
        return carry

    lax.fori_loop(0, total.shape[0] // 16, tile, 0)


def sum_tp_body(math_rule, inputs, *refs):
    part_ref, ins = refs[0], refs[1 : 1 + inputs]
    outs, scratch = refs[1 + inputs : -7], refs[-7:]
    gathered, outs = outs[0], outs[1:]
    total, send, recv, send_sem, recv_sem, gather_send_sem, gather_recv_sem = scratch
    planes = part_ref.shape[0]
    own, plane = lax.axis_index("tok"), lax.axis_index("tp")
    line_greet(own, plane, planes)
    line_reduce(own, plane, planes, part_ref, total, send, recv, send_sem, recv_sem)
    math_rule(plane, total, ins, outs, gathered)
    line_gather(own, plane, planes, gathered, gather_send_sem, gather_recv_sem)


def sum_tp(math_rule, part, inputs, out_shapes, collective_id, name):
    planes = lax.axis_size("tp")
    rows, width = part.shape
    shard = rows // planes
    part = part.reshape(planes, shard, width)
    return pl.pallas_call(
        functools.partial(sum_tp_body, math_rule, len(inputs)),
        out_shape=[jax.ShapeDtypeStruct((planes, shard, width), BF16)] + out_shapes,
        in_specs=[vmem()] * (1 + len(inputs)),
        out_specs=[vmem()] * (1 + len(out_shapes)),
        scratch_shapes=[
            pltpu.VMEM((shard, width), F32),
            pltpu.VMEM((2, planes, shard, width), part.dtype),
            pltpu.VMEM((2, planes, shard, width), part.dtype),
        ]
        + [pltpu.SemaphoreType.DMA((2, planes))] * 4,
        compiler_params=params(collective_id),
        cost_estimate=cost(0, 60_000_000),
        name=name,
    )(part, *inputs)


def swap(values, bit):
    devices = lax.axis_size("tok")
    return lax.ppermute(values, "tok", [(i, i ^ bit) for i in range(devices)])


def pick(values, index):
    return lax.dynamic_index_in_dim(values, index, 0, keepdims=False)


def halve(values, bits, own):
    for position, bit in enumerate(bits):
        side = (own // bit) % 2
        shape = values.shape
        lead = 2 ** (len(bits) - position - 1)
        values = values.reshape((2, lead) + shape[1:])
        got = swap(pick(values, 1 - side), bit)
        summed = pick(values, side).astype(F32) + got.astype(F32)
        values = summed if position == len(bits) - 1 else summed.astype(BF16)
    return values[0]


def scatter_weights(grad):
    devices = lax.axis_size("tok")
    own = lax.axis_index("tok")
    stages = stages_of("tok")
    rows, columns = grad.shape
    share = rows // devices
    grad = grad.reshape(devices // 2, 2, share, columns)
    core = own % 2
    mine = lax.dynamic_index_in_dim(grad, core, 1, keepdims=False)
    other = lax.dynamic_index_in_dim(grad, 1 - core, 1, keepdims=False)
    both = (mine.astype(F32) + swap(other, 1).astype(F32)).astype(BF16)
    bits = [1 << stage for stage in range(stages - 1, 0, -1)]
    upper, lower = both[:, : share // 2], both[:, share // 2 :]
    sides = len(bits)
    flipped = lower.reshape((2,) * sides + lower.shape[1:])
    flipped = flipped.transpose(tuple(range(sides - 1, -1, -1)) + (sides, sides + 1))
    flipped = flipped.reshape(lower.shape)
    return jnp.concatenate([halve(upper, bits, own), halve(flipped, bits[::-1], own)], axis=0)


def document_tables(doc_lengths, places):
    doc_ends = jnp.cumsum(doc_lengths, dtype=jnp.int32)
    doc_starts = doc_ends - doc_lengths
    doc_ids = jnp.sum(
        (places[:, None] >= doc_ends[None, :]).astype(jnp.int32), axis=1, dtype=jnp.int32
    )
    member = (
        doc_ids[:, None] == jnp.arange(doc_lengths.shape[0], dtype=jnp.int32)[None, :]
    ).astype(jnp.int32)
    positions = places - jnp.sum(member * doc_starts[None, :], axis=1, dtype=jnp.int32)
    return (doc_ids, positions, member)


def rotary_tables(positions, head_dim):
    half_dim = head_dim // 2
    freqs = jnp.exp(jnp.arange(half_dim, dtype=jnp.float32) * (-2.0 * math.log(10000.0) / head_dim))
    angles = positions.astype(jnp.float32)[:, None] * freqs[None, :]
    return (jnp.cos(angles), jnp.sin(angles))


def rotate(values, cosine, sine):
    half_dim = values.shape[-1] // 2
    former, latter = (values[..., :half_dim], values[..., half_dim:])
    cos_b, sin_b = (cosine[:, None, :], sine[:, None, :])
    return jnp.concatenate(
        [former * cos_b - latter * sin_b, latter * cos_b + former * sin_b], axis=-1
    )


def unrotate(values, cosine, sine):
    half_dim = values.shape[-1] // 2
    former, latter = (values[..., :half_dim], values[..., half_dim:])
    cos_b, sin_b = (cosine[:, None, :], sine[:, None, :])
    return jnp.concatenate(
        [former * cos_b + latter * sin_b, latter * cos_b - former * sin_b], axis=-1
    )


def over_rows(left, right, kind=F32):
    return lax.dot_general(
        left, right, (((0,), (0,)), ((), ())), preferred_element_type=jnp.float32
    ).astype(kind)


def over_columns(left, right):
    return lax.dot_general(
        left, right, (((1,), (1,)), ((), ())), preferred_element_type=jnp.float32
    )


def on_device(
    tokens,
    gain_attn,
    w_query,
    w_key,
    w_value,
    w_out,
    gain_ffn,
    w_gate,
    w_up,
    w_down,
    cotangent,
    doc_lengths,
    keep_flags,
):
    length = tokens.shape[0]
    model_width = tokens.shape[1]
    devices = lax.axis_size("tok")
    planes = lax.axis_size("tp")
    own_index = lax.axis_index("tok")
    blocks_here = length // BLOCK
    kept_here = blocks_here // 2
    total_blocks = blocks_here * devices
    kept_total = kept_here * devices
    rows = kept_here * BLOCK
    token_blocks = tokens.reshape(blocks_here, BLOCK, model_width)
    grad_blocks = cotangent.reshape(blocks_here, BLOCK, model_width)

    half_columns = model_width // 2
    out_half = lax.dynamic_slice_in_dim(w_out, (own_index % 2) * half_columns, half_columns, 1)
    out_half = lax.all_gather(out_half, "tp", axis=0, tiled=True)
    out_other = swap(out_half, 1)
    first_core = own_index % 2 == 0

    rows_x = deal(doc_lengths, keep_flags, token_blocks, 0).reshape(rows, model_width)
    rows_dy = deal(doc_lengths, keep_flags, grad_blocks, 1).reshape(rows, model_width)

    block_starts = jnp.arange(total_blocks, dtype=jnp.int32) * BLOCK
    block_docs, block_pos, block_member = document_tables(doc_lengths, block_starts)
    block_kept = jnp.sum(block_member * keep_flags[None, :], axis=1, dtype=jnp.int32)
    block_rank = jnp.cumsum(block_kept, dtype=jnp.int32) - block_kept
    rank_slots = jnp.arange(kept_total, dtype=jnp.int32)
    rank_match = ((block_rank[None, :] == rank_slots[:, None]) & (block_kept[None, :] == 1)).astype(
        jnp.int32
    )
    rank_block = jnp.sum(
        rank_match * jnp.arange(total_blocks, dtype=jnp.int32)[None, :], axis=1, dtype=jnp.int32
    )
    peer_ids = jnp.arange(devices, dtype=jnp.int32)
    own_ranks = own_index + jnp.arange(kept_here, dtype=jnp.int32) * devices
    own_blocks = jnp.take(rank_block, own_ranks)
    block_offsets = jnp.arange(BLOCK, dtype=jnp.int32)
    places = (own_blocks[:, None] * BLOCK + block_offsets[None, :]).reshape(rows)
    key_ranks = (
        peer_ids[:, None] + jnp.arange(kept_here, dtype=jnp.int32)[None, :] * devices
    ).reshape(kept_total)
    key_places = (
        jnp.take(rank_block, key_ranks)[:, None] * BLOCK + block_offsets[None, :]
    ).reshape(kept_total * BLOCK)
    doc_ids, positions, member = document_tables(doc_lengths, places)
    key_docs, key_pos, key_member = document_tables(doc_lengths, key_places)
    allowed = (doc_ids[:, None] == key_docs[None, :]) & (places[:, None] >= key_places[None, :])
    cosine, sine = rotary_tables(positions, HD)
    heads_here = w_query.shape[1] // HD
    groups_here = w_key.shape[1] // HD
    sharing = heads_here // groups_here
    score_scale = 1.0 / math.sqrt(HD)

    x_full = rows_x.astype(jnp.float32)
    inv_one = lax.rsqrt(jnp.mean(x_full * x_full, axis=1, keepdims=True) + norm_eps)
    normed_one = (x_full * inv_one * gain_attn).astype(jnp.bfloat16)
    query_pre = jnp.dot(normed_one, w_query, preferred_element_type=jnp.float32).reshape(
        rows, heads_here, HD
    )
    key_pre = jnp.dot(normed_one, w_key, preferred_element_type=jnp.float32).reshape(
        rows, groups_here, HD
    )
    value_pre = jnp.dot(normed_one, w_value, preferred_element_type=jnp.float32)
    queries = rotate(query_pre, cosine, sine).astype(jnp.bfloat16)
    keys_local = rotate(key_pre, cosine, sine).astype(jnp.bfloat16).reshape(rows, groups_here * HD)
    values_local = value_pre.astype(jnp.bfloat16)
    kv_width = groups_here * HD
    key_count = kept_total * BLOCK
    both_all = gather_tok(jnp.concatenate([keys_local, values_local], axis=1), 2)
    both_all = both_all.reshape(key_count, 2, groups_here, HD)
    keys_heads, values_heads = both_all[:, 0], both_all[:, 1]
    query_heads = queries.transpose(1, 0, 2)
    slot_of_head = jnp.arange(heads_here, dtype=jnp.int32) // sharing

    def head_scores(query, slot):
        keys_one = lax.dynamic_index_in_dim(keys_heads, slot, 1, keepdims=False)
        values_one = lax.dynamic_index_in_dim(values_heads, slot, 1, keepdims=False)
        scores = (
            jnp.einsum("qd,kd->qk", query, keys_one, preferred_element_type=jnp.float32)
            * score_scale
        )
        return (jnp.where(allowed, scores, -1e30), keys_one, values_one)

    def head_forward(pack):
        query, slot = pack
        scores, keys_one, values_one = head_scores(query, slot)
        peak = jnp.max(scores, axis=1, keepdims=True)
        weights = jnp.exp(scores - peak)
        totals = jnp.sum(weights, axis=1, keepdims=True)
        probs = (weights / totals).astype(jnp.bfloat16)
        return (jnp.dot(probs, values_one, preferred_element_type=jnp.float32), peak, totals)

    head_outs, peaks, totals = lax.map(head_forward, (query_heads, slot_of_head))
    attended = head_outs.transpose(1, 0, 2).reshape(rows, heads_here * HD).astype(jnp.bfloat16)

    attended_all = gather_tp(attended, 3)
    attended_all = attended_all.transpose(1, 0, 2).reshape(rows, planes * heads_here * HD)
    mine = jnp.dot(attended_all, out_half, preferred_element_type=jnp.float32)
    other = jnp.dot(attended_all, out_other, preferred_element_type=jnp.float32)
    branch_attn = jnp.concatenate(
        [jnp.where(first_core, mine, other), jnp.where(first_core, other, mine)], axis=1
    )
    hidden_res = x_full + branch_attn
    inv_two = lax.rsqrt(jnp.mean(hidden_res * hidden_res, axis=1, keepdims=True) + norm_eps)
    normed_two = (hidden_res * inv_two * gain_ffn).astype(jnp.bfloat16)
    gate = jnp.dot(normed_two, w_gate, preferred_element_type=jnp.float32)
    upper = jnp.dot(normed_two, w_up, preferred_element_type=jnp.float32)
    sigma = jax.nn.sigmoid(gate)
    swish = gate * sigma
    inner = (swish * upper).astype(jnp.bfloat16)

    grad_m = (keep_scale * rows_dy.astype(jnp.float32)).astype(jnp.bfloat16)
    grad_inner = over_columns(grad_m, w_down)
    grad_gate_pre = (grad_inner * upper * sigma * (1.0 + gate * (1.0 - sigma))).astype(jnp.bfloat16)
    grad_up_pre = (grad_inner * swish).astype(jnp.bfloat16)
    part_two = (
        over_columns(grad_gate_pre, w_gate) + over_columns(grad_up_pre, w_up)
    ).astype(jnp.bfloat16)

    shard = rows // planes
    by_plane = lambda array: array.reshape(planes, shard, array.shape[1])
    x_planes, dy_planes = by_plane(rows_x), by_plane(rows_dy)
    hidden_planes = by_plane(hidden_res)
    grad_a, grad_hidden, gains_ffn = sum_tp(
        ffn_math,
        part_two,
        (hidden_planes, by_plane(inv_two), dy_planes, gain_ffn.reshape(1, -1)),
        [
            jax.ShapeDtypeStruct((shard, model_width), F32),
            jax.ShapeDtypeStruct((8, model_width), F32),
        ],
        4,
        "sum_ffn",
    )
    grad_a = grad_a.reshape(rows, model_width)

    grad_gate = scatter_weights(over_rows(normed_two, grad_gate_pre, BF16))
    grad_up = scatter_weights(over_rows(normed_two, grad_up_pre, BF16))
    grad_down = scatter_weights(over_rows(grad_m, inner, BF16)).T

    grad_attended = over_columns(grad_a, w_out).astype(jnp.bfloat16)
    grad_heads = grad_attended.reshape(rows, heads_here, HD).transpose(1, 0, 2)

    def head_backward(pack):
        query, grad_head, peak, total, slot = pack
        scores, keys_one, values_one = head_scores(query, slot)
        probs = jnp.exp(scores - peak) / total
        probs_low = probs.astype(jnp.bfloat16)
        grad_probs = jnp.einsum(
            "qd,kd->qk", grad_head, values_one, preferred_element_type=jnp.float32
        )
        delta = jnp.sum(probs * grad_probs, axis=1, keepdims=True)
        grad_scores = (probs * (grad_probs - delta)).astype(jnp.bfloat16)
        grad_query_head = (
            jnp.dot(grad_scores, keys_one, preferred_element_type=jnp.float32) * score_scale
        )
        grad_keys_head = over_rows(grad_scores, query) * score_scale
        grad_values_head = over_rows(probs_low, grad_head)
        return (grad_query_head, grad_keys_head, grad_values_head)

    grad_q_heads, grad_k_heads, grad_v_heads = lax.map(
        head_backward, (query_heads, grad_heads, peaks, totals, slot_of_head)
    )
    grad_k_all = (
        grad_k_heads.reshape(groups_here, sharing, key_count, HD)
        .sum(axis=1)
        .transpose(1, 0, 2)
        .reshape(key_count, kv_width)
    )
    grad_v_all = (
        grad_v_heads.reshape(groups_here, sharing, key_count, HD)
        .sum(axis=1)
        .transpose(1, 0, 2)
        .reshape(key_count, kv_width)
    )
    grad_kv = jnp.concatenate([grad_k_all, grad_v_all], axis=1).astype(BF16)
    grad_kv = scatter_tok(grad_kv.reshape(devices, rows, 2 * kv_width), 5)
    grad_k_own, grad_v_own = grad_kv[:, :kv_width], grad_kv[:, kv_width:]
    grad_query_pre = (
        unrotate(grad_q_heads.transpose(1, 0, 2), cosine, sine)
        .reshape(rows, heads_here * HD)
        .astype(jnp.bfloat16)
    )
    grad_key_pre = (
        unrotate(grad_k_own.reshape(rows, groups_here, HD), cosine, sine)
        .reshape(rows, kv_width)
        .astype(jnp.bfloat16)
    )
    grad_value_pre = grad_v_own.astype(jnp.bfloat16)
    part_one = (
        over_columns(grad_query_pre, w_query)
        + over_columns(grad_key_pre, w_key)
        + over_columns(grad_value_pre, w_value)
    ).astype(jnp.bfloat16)
    grad_rows, gains = sum_tp(
        attn_math,
        part_one,
        (x_planes, by_plane(inv_one), dy_planes, grad_hidden, gain_attn.reshape(1, -1), gains_ffn),
        [jax.ShapeDtypeStruct((8, model_width), F32)],
        6,
        "sum_attn",
    )
    gains = lax.psum(gains, "tp")

    mixed_rows = sum_tp(
        mixed_math,
        jnp.dot(inner, w_down, preferred_element_type=jnp.float32).astype(jnp.bfloat16),
        (hidden_planes, x_planes),
        [],
        7,
        "sum_mixed",
    )[0]
    mixed, _ = undeal(
        doc_lengths,
        keep_flags,
        mixed_rows.reshape(kept_here, BLOCK, model_width),
        token_blocks,
        gains_ffn,
        8,
    )
    token_grad, gain_sums = undeal(
        doc_lengths,
        keep_flags,
        grad_rows.reshape(kept_here, BLOCK, model_width),
        grad_blocks,
        gains,
        9,
    )
    own_share = model_width // devices
    if gain_sums.shape[1] != own_share:
        gain_sums = lax.dynamic_slice_in_dim(gain_sums, own_index * own_share, own_share, 1)

    attn_grads = jnp.concatenate(
        [
            over_rows(normed_one, grad_query_pre, BF16),
            over_rows(normed_one, grad_key_pre, BF16),
            over_rows(normed_one, grad_value_pre, BF16),
            over_rows(grad_a, attended, BF16),
        ],
        axis=1,
    )
    attn_grads = scatter_weights(attn_grads)
    wide, thin = w_query.shape[1], w_key.shape[1]
    grad_query = attn_grads[:, :wide]
    grad_key = attn_grads[:, wide : wide + thin]
    grad_value = attn_grads[:, wide + thin : wide + 2 * thin]
    grad_out = attn_grads[:, wide + 2 * thin :].T

    return (
        mixed.reshape(length, model_width),
        token_grad.reshape(length, model_width),
        gain_sums[1],
        grad_query,
        grad_key,
        grad_value,
        grad_out,
        gain_sums[0],
        grad_gate,
        grad_up,
        grad_down,
    )


def solution(mesh):
    placed = (
        P("tok", None),
        P(),
        P(None, "tp"),
        P(None, "tp"),
        P(None, "tp"),
        P("tp", None),
        P(),
        P(None, "tp"),
        P(None, "tp"),
        P("tp", None),
        P("tok", None),
        P(),
        P(),
    )
    return jax.shard_map(
        on_device,
        mesh=mesh,
        in_specs=placed,
        out_specs=(
            P("tok", None),
            P("tok", None),
            P("tok"),
            P("tok", "tp"),
            P("tok", "tp"),
            P("tok", "tp"),
            P("tp", "tok"),
            P("tok"),
            P("tok", "tp"),
            P("tok", "tp"),
            P("tp", "tok"),
        ),
        check_vma=False,
    )
```

time: 1280 us -> 869 us (0.68)
  waiting for transfers between devices: 791 us -> 66.9 us
  Pallas kernels: 0 us -> 440 us
  blocking collectives: 183 us -> 0 us
  local copies, waits for them, and re-layouts: 62.1 us -> 118 us
    pallas_call x0 -> x10, Pallas kernels: none -> 440 us  [the longest x3 173 us: sum_tp(): pl.pallas_call(functools.partial(sum_tp_body, math_rule, len(inputs)), ou...]
    reduce_scatter x9 -> x0, waiting for transfers between devices: 384 us -> none  [the longest x1 90.9 us: on_device(): lax.psum_scatter(grad_down, 'tok', scatter_dimension=1, tiled=True)]
    psum x4 -> x1, waiting for transfers between devices: 368 us -> 13.6 us  [on_device(): gains = lax.psum(gains, 'tp')]
    unnamed x1 -> x0, blocking collectives: 68.6 us -> none
    all_gather x2 -> x0, blocking collectives: 58.4 us -> none  [the longest x1 47 us: on_device(): lax.all_gather(keys_local, 'tok', axis=0, tiled=True)]
    all_to_all x1 -> x0, blocking collectives: 56.2 us -> none  [on_device(): lax.all_to_all(pick_blocks(mixed_kept, back_index, back_valid), 'tok', sp...]
    ppermute x0 -> x21, waiting for transfers between devices: none -> 53.2 us  [swap(): return lax.ppermute(values, 'tok', [(i, i ^ bit) for i in range(devices)])]
    all_to_all x3 -> x0, waiting for transfers between devices: 38.9 us -> none  [the longest x1 38.9 us: on_device(): lax.all_to_all(pick_blocks(token_blocks, out_index, out_valid), 'tok', sp...]
  transfers between devices with their start and end apart: 16 -> 23, of which waited for: 11 -> 9; matrix products, arithmetic and copies ran while one was open for 11% -> 14% of each run, Pallas kernels for 0% -> 43%
where the time goes in v1:
time: 869 us; the launch traced here: 857 us
  Pallas kernels  440 us (51%)
  matrix products  131 us (15%)
  local copies, waits for them, and re-layouts  118 us (14%)
  other arithmetic  68.9 us (8%)
  waiting for transfers between devices  66.9 us (8%)
  starting transfers between devices  15.8 us (2%)
  between operations  15.6 us (2%)
    pallas_call x3, Pallas kernels, sum_tp(): pl.pallas_call(functools.partial(sum_tp_body, math_rule, len(inputs)), ou...  173 us
    pallas_call x2, Pallas kernels, undeal(): pl.pallas_call(undeal_body, out_shape=(jax.ShapeDtypeStruct(home.shape, h...  105 us
    pallas_call x2, Pallas kernels, deal(): pl.pallas_call(deal_body, out_shape=jax.ShapeDtypeStruct((SLOTS, BLOCK, w...  97 us
    ppermute x21, waiting for transfers between devices, swap(): return lax.ppermute(values, 'tok', [(i, i ^ bit) for i in range(devices)])  53.2 us
    dot_general x15, matrix products, over_rows(): lax.dot_general(left, right, (((0,), (0,)), ((), ())), preferred_element_...  45.5 us
    unnamed x137, local copies, waits for them, and re-layouts  36.6 us
    pallas_call x1, Pallas kernels, gather_tp(): pl.pallas_call(gather_tp_body, out_shape=jax.ShapeDtypeStruct((planes,) +...  30.3 us
    dot_general x7, matrix products, over_columns(): lax.dot_general(left, right, (((1,), (1,)), ((), ())), preferred_element_...  24.3 us
  transfers between devices with their start and end apart: 23, of which 9 were waited for; matrix products, arithmetic and copies ran while one was open for 14% of the time, Pallas kernels for 43%

profile of v1, /device:TPU:1, one launch (start us, length us, event | category | flops | bytes accessed | tf_op | source)
XLA Modules:
  0.0 856.9 jit_solution(10723287245044398784)
XLA Ops:
  12.3 49.1 %deal.2 = bf16[3,128,2048]{2,1,0:T(8,128)(2,1)} custom-call(s32[6]{0:T(128)} %lens_ref.7, s32[6]{0:T(128)} %flags_ref.7, bf16[6,128,2048]{2,1,0:T(8,128)(2,1)} %bitcast.327), custom_call_target="tpu_custom_call" | custom-call | bytes 40000000 | tf_op jit(solution)/shard_map/deal/pallas_call | solution.py:183
  69.5 16.0 %gather_tok.1 = bf16[8,384,256]{2,1,0:T(8,128)(2,1)} custom-call(bf16[384,256]{1,0:T(8,128)(2,1)} %pad_maximum_fusion.5.mine_ref), custom_call_target="tpu_custom_call" | custom-call | bytes 10000000 | tf_op jit(solution)/shard_map/gather_tok/pallas_call | solution.py:379
  85.5 3.5 reshape.709
  89.0 3.9 copy.84
  97.9 4.5 fusion.103
  103.7 21.1 %while.32 = (s32[]{:T(128)}, bf16[4,384,128]{2,1,0:T(8,128)(2,1)}, f32[4,384,1]{1,2,0:T(1,128)}, f32[4,384,1]{1,2,0:T(1,128)}, bf16[4,384,128]{2,1,0:T(8,128)(2,...) while((s32[]{:T(128)}, bf16[4,384,128]{2,1,0:T(8,128)(2,1)}, ...), condition=%wide.region_12.13_spmd.clone, body=%wide.region_9.12_spmd.clone.sunk | while | flops 616955136 | bytes 19211968 | solution.py:931
  103.7 2.5 fusion.171
  109.0 2.5 fusion.171
  114.3 2.5 fusion.171
  119.5 2.5 fusion.171
  125.7 47.9 %deal.3 = bf16[3,128,2048]{2,1,0:T(8,128)(2,1)} custom-call(s32[6]{0:T(128)} %lens_ref.7, s32[6]{0:T(128)} %flags_ref.7, bf16[6,128,2048]{2,1,0:T(8,128)(2,1)} %bitcast.329), custom_call_target="tpu_custom_call" | custom-call | bytes 40000000 | tf_op jit(solution)/shard_map/deal/pallas_call | solution.py:183
  174.4 30.3 %gather_tp.1 = bf16[4,384,512]{2,1,0:T(8,128)(2,1)} custom-call(bf16[384,512]{1,0:T(8,128)(2,1)} %copy_bitcast_fusion.2.mine_ref), custom_call_target="tpu_custom_call" | custom-call | bytes 30000000 | tf_op jit(solution)/shard_map/gather_tp/pallas_call | solution.py:615
  204.7 3.0 copy.69
  209.7 4.2 fusion.106
  213.9 4.2 broadcast_select_fusion.1
  220.4 2.6 fusion.108
  223.0 2.6 fusion.107
  225.7 5.4 multiply_convert_fusion.2
  231.0 3.7 convolution_convert_fusion.5
  234.8 5.2 convolution_convert_fusion
  240.8 5.2 fusion.109
  246.1 7.8 add_convert_fusion.1
  256.0 55.7 %sum_ffn.1 = (bf16[4,96,2048]{2,1,0:T(8,128)(2,1)}, f32[96,2048]{1,0:T(8,128)}, f32[8,2048]{1,0:T(8,128)}) custom-call(bf16[4,96,2048]{2,1,0:T(8,128)(2,1)} %bitcast.376, f32[4,96,2048]{2,1,0:T(8,128)} %maximum_add_fusion.2.refs_1_, f32[4,96,1]{2,1,0:T(8,128)} %rsqrt.49.refs_2_, bf16[4,96,2048]{2,1,0:T(8,128)(2,1)} %bitcast.319, f32[1,2048]{1,0:T(1,128)} %bitcast.382), custom_call_target="tpu_custom_call" | custom-call | bytes 60000000 | tf_op jit(solution)/shard_map/sum_ffn/pallas_call | solution.py:716
  311.7 2.6 fusion.59
  314.3 2.6 convolution_convert_fusion.4
  316.9 5.2 convolution_convert_fusion.1
  322.9 73.3 %while.33 = (s32[]{:T(128)}, f32[4,384,128]{1,2,0:T(8,128)}, f32[4,3072,128]{2,1,0:T(8,128)}, f32[4,3072,128]{2,1,0:T(8,128)}, bf16[4,384,128]{2,1,0:T(8,128)(2,...) while((s32[]{:T(128)}, f32[4,384,128]{1,2,0:T(8,128)}, ...), condition=%wide.region_16.17_spmd.clone, body=%wide.region_14.16_spmd.clone.sunk | while | flops 1525726848 | bytes 64334072 | solution.py:999
  325.3 3.3 multiply_reduce_fusion.2
  334.8 4.4 fusion.186
  343.6 3.3 multiply_reduce_fusion.2
  353.1 4.4 fusion.186
  361.9 3.3 multiply_reduce_fusion.2
  371.4 4.4 fusion.186
  380.1 3.3 multiply_reduce_fusion.2
  389.6 4.4 fusion.186
  396.3 3.3 reduce_sum.119
  399.5 3.3 reduce_sum.118
  404.1 19.3 %scatter_tok.1 = f32[384,256]{1,0:T(8,128)} custom-call(bf16[8,384,256]{2,1,0:T(8,128)(2,1)} %pad_maximum_fusion.1.part_ref), custom_call_target="tpu_custom_call" | custom-call | bytes 10000000 | tf_op jit(solution)/shard_map/scatter_tok/pallas_call | solution.py:445
  429.0 10.1 %pad_maximum_fusion = bf16[2048,1280]{0,1:T(8,128)(2,1)} fusion(bf16[2048,512]{0,1:T(8,128)(2,1)S(1)} %copy-done.25, bf16[2048,128]{0,1:T(8,128)(2,1)S(1)} %convolution_convert_fusion.6, bf16[2048,128]{0,1:T(8,128)(2,1)S(1)} %convolution_convert_fusion.7, bf16[2048,512]{0,1:T(8,128)(2,1)S(1)} %convolution_convert_fusion.3), kind=kLoop, calls=%fused_computation.59 | loop fusion | flops 20971520 | bytes 10485760 | tf_op jit(solution)/shard_map/concatenate | solution.py:1071
  439.0 9.5 %reshape.723 = bf16[4,2,256,1280]{2,1,0,3:T(2,128)(2,1)} reshape(bf16[2048,1280]{0,1:T(8,128)(2,1)} %pad_maximum_fusion) | data formatting | bytes 10485760 | tf_op jit(solution)/shard_map/reshape | solution.py:760
  448.5 13.7 %constant_dynamic-slice_fusion.11 = (bf16[4,1,256,1280]{2,1,0,3:T(2,128)(2,1)}, bf16[4,1,256,1280]{2,1,0,3:T(2,128)(2,1)}) fusion(bf16[4,2,256,1280]{2,1,0,3:T(2,128)(2,1)} %reshape.723, s32[]{:T(128)S(6)} %select_n.229, s32[]{:T(128)S(6)} %select_n.230), kind=kLoop, calls=%fused_computation.208 | loop fusion | bytes 10485768 | tf_op jit(solution)/shard_map/jit(dynamic_index_in_dim)/dynamic_slice | solution.py:762
  462.2 11.1 %copy.90 = bf16[4,1,256,1280]{3,2,0,1:T(8,128)(2,1)} copy(bf16[4,1,256,1280]{2,1,0,3:T(2,128)(2,1)} %get-tuple-element.411) | data formatting | bytes 5242880
  473.7 3.6 dynamic-slice_bitcast_fusion
  477.4 58.3 %sum_mixed.1 = bf16[4,96,2048]{2,1,0:T(8,128)(2,1)} custom-call(bf16[4,96,2048]{2,1,0:T(8,128)(2,1)} %bitcast.377, f32[4,96,2048]{2,1,0:T(8,128)} %maximum_add_fusion.2.refs_1_, bf16[4,96,2048]{2,1,0:T(8,128)(2,1)} %bitcast.316), custom_call_target="tpu_custom_call" | custom-call | bytes 60000000 | tf_op jit(solution)/shard_map/sum_mixed/pallas_call | solution.py:716
  535.7 52.1 %undeal.2 = (bf16[6,128,2048]{2,1,0:T(8,128)(2,1)}, f32[8,256]{1,0:T(8,128)}) custom-call(s32[6]{0:T(128)} %lens_ref.7, s32[6]{0:T(128)} %flags_ref.7, bf16[3,128,2048]{2,1,0:T(8,128)(2,1)} %bitcast.337, bf16[6,128,2048]{2,1,0:T(8,128)(2,1)} %bitcast.328, f32[8,2048]{1,0:T(8,128)} %get-tuple-element.169.gains_ref.refs_6_), custom_call_target="tpu_custom_call" | custom-call | bytes 40000000 | tf_op jit(solution)/shard_map/undeal/pallas_call | solution.py:312
  587.8 3.7 dynamic-slice_bitcast_fusion.1
  596.3 58.6 %sum_attn.1 = (bf16[4,96,2048]{2,1,0:T(8,128)(2,1)}, f32[8,2048]{1,0:T(8,128)}) custom-call(bf16[4,96,2048]{2,1,0:T(8,128)(2,1)} %bitcast.332, bf16[4,96,2048]{2,1,0:T(8,128)(2,1)} %bitcast.317, f32[4,96,1]{2,1,0:T(8,128)} %rsqrt.50.refs_2_, bf16[4,96,2048]{2,1,0:T(8,128)(2,1)} %bitcast.320, f32[96,2048]{1,0:T(8,128)} %get-tuple-element.177.refs_4_, ...), custom_call_target="tpu_custom_call" | custom-call | bytes 60000000 | tf_op jit(solution)/shard_map/sum_attn/pallas_call | solution.py:716
  655.0 3.6 convolution_convert_fusion.2
  662.0 2.8 collective-permute-start.6
  664.8 9.6 %copy.89 = bf16[4,1,256,1280]{3,2,0,1:T(8,128)(2,1)S(1)} copy(bf16[4,1,256,1280]{2,1,0,3:T(2,128)(2,1)} %get-tuple-element.410) | data formatting | bytes 5242880
  674.4 13.6 %all-reduce.2.cloned.1.call-done.gains_ref = f32[8,2048]{1,0:T(8,128)} async-done(((f32[8,2048]{1,0:T(8,128)}), f32[8,2048]{1,0:T(8,128)}) %all-reduce.2.cloned.1.call-update) | async-done | bytes 65552 | tf_op jit(solution)/shard_map/psum | solution.py:1041
  688.1 52.4 %undeal.3 = (bf16[6,128,2048]{2,1,0:T(8,128)(2,1)}, f32[8,256]{1,0:T(8,128)}) custom-call(s32[6]{0:T(128)} %lens_ref.7, s32[6]{0:T(128)} %flags_ref.7, bf16[3,128,2048]{2,1,0:T(8,128)(2,1)} %bitcast.375, bf16[6,128,2048]{2,1,0:T(8,128)(2,1)} %bitcast.330, f32[8,2048]{1,0:T(8,128)} %all-reduce.2.cloned.1.call-done.gains_ref), custom_call_target="tpu_custom_call" | custom-call | bytes 40000000 | tf_op jit(solution)/shard_map/undeal/pallas_call | solution.py:312
  741.8 2.5 fusion.39
  747.3 2.6 fusion.36
  752.1 3.2 fusion.37
  755.8 2.5 fusion.38
  758.8 2.3 collective-permute-done.4
  764.1 13.6 %collective-permute-done.17 = bf16[2,128,1408]{2,1,0:T(8,128)(2,1)S(1)} collective-permute-done((bf16[2,128,1408]{2,1,0:T(8,128)(2,1)S(1)}, bf16[2,128,1408]{2,1,0:T(8,128)(2,1)S(1)}, u32[]{:S(2)}, u32[]{:S(2)}) %collective-permute-start.17) | collective-permute-done | bytes 720928 | tf_op jit(solution)/shard_map/ppermute | solution.py:735
  780.9 12.2 %collective-permute-done.12 = bf16[2,128,1408]{2,1,0:T(8,128)(2,1)S(1)} collective-permute-done((bf16[2,128,1408]{2,1,0:T(8,128)(2,1)S(1)}, bf16[2,128,1408]{2,1,0:T(8,128)(2,1)S(1)}, u32[]{:S(2)}, u32[]{:S(2)}) %collective-permute-start.12) | collective-permute-done | bytes 720928 | tf_op jit(solution)/shard_map/ppermute | solution.py:735
  795.9 12.7 %collective-permute-done.7 = bf16[2,128,1408]{2,1,0:T(8,128)(2,1)S(1)} collective-permute-done((bf16[2,128,1408]{2,1,0:T(8,128)(2,1)S(1)}, bf16[2,128,1408]{2,1,0:T(8,128)(2,1)S(1)}, u32[]{:S(2)}, u32[]{:S(2)}) %collective-permute-start.7) | collective-permute-done | bytes 720928 | tf_op jit(solution)/shard_map/ppermute | solution.py:735
  812.0 3.7 collective-permute-done.5
  826.0 4.0 collective-permute-done.13
  833.1 4.6 collective-permute-done.8
  840.4 2.4 pad_maximum_fusion.3
  (372 shorter events, 140.0 us)
Async XLA Ops:
  7.2 3.0 copy-start.51
  7.2 96.3 %all-gather.2.cloned.1.call-start = ((), (), s32[]{:S(2)}) async-start(), calls=%async_computation | async-start | bytes 5242880 | tf_op jit(solution)/shard_map/all_gather | solution.py:854
  9.9 678.2 %all-reduce.2.cloned.1.call-start = ((), (), s32[]{:S(2)}) async-start(), calls=%async_computation.1 | async-start | bytes 131072 | tf_op jit(solution)/shard_map/psum | solution.py:1041
  10.9 82.0 %copy-start.52 = (f32[64]{0:T(128)}, f32[64]{0:T(128)S(1)}, u32[]{:S(2)}) copy-start(f32[64]{0:T(128)S(1)} %multiply_exponential_fusion) | copy-start | bytes 772
  12.3 51.1 %copy-start.50 = (s32[6]{0:T(128)S(1)}, s32[6]{0:T(128)}, u32[]{:S(2)}) copy-start(s32[6]{0:T(128)} %lens_ref.7) | copy-start | bytes 76
  12.3 53.8 %copy-start.45 = (f32[2048]{0:T(1024)S(1)}, f32[2048]{0:T(1024)}, u32[]{:S(2)}) copy-start(f32[2048]{0:T(1024)} %param.18) | copy-start | bytes 24580
  61.4 4.6 copy-start.3
  67.2 25.7 %copy-start.47 = (f32[384]{0:T(512)}, f32[384]{0:T(512)S(1)}, u32[]{:S(2)}) copy-start(f32[384]{0:T(512)S(1)} %subtract_convert_fusion.1) | copy-start | bytes 4612
  93.3 3.4 copy-start.36
  93.4 3.4 copy-start.38
  103.6 110.4 %collective-permute-start = (bf16[2048,1024]{1,0:T(8,128)(2,1)}, bf16[2048,1024]{1,0:T(8,128)(2,1)}, u32[]{:S(2)}, u32[]{:S(2)}) collective-permute-start(bf16[2048,1024]{1,0:T(8,128)(2,1)} %all-gather.2.cloned.1.call-done), channel_id=1, source_target_pairs={{0,4},{4,0},{8,12},{12,8},{16,20},{20,16},{24,28},{28,24},{1,5},{5... | collective-permute-start | bytes 12582920 | tf_op jit(solution)/shard_map/ppermute | solution.py:735
  125.7 47.9 %copy-start.43 = (bf16[4,384,128]{2,1,0:T(8,128)(2,1)S(1)}, bf16[4,384,128]{2,1,0:T(8,128)(2,1)}, u32[]{:S(2)}) copy-start(bf16[4,384,128]{2,1,0:T(8,128)(2,1)} %get-tuple-element.168) | copy-start | bytes 1179652
  209.7 10.6 %slice-start.10 = ((s8[5767168]{0:T(1024)(128)(4,1)}), s8[4194304]{0:T(1024)(128)(4,1)S(1)}, s32[]{:S(2)}) async-start(s8[5767168]{0:T(1024)(128)(4,1)} %bitcast.394), calls=%async_computation.12 | async-start | bytes 8388608
  213.9 4.2 copy-start.4
  213.9 6.4 slice-start.11
  219.8 3.2 slice-start.8
  220.3 5.3 slice-start.6
  240.8 5.2 copy-start.56
  246.0 7.9 copy-start.5
  246.0 7.9 copy-start.9
  246.0 7.8 copy-start.11
  334.8 4.5 copy-start.32
  353.1 4.4 copy-start.32
  371.3 4.4 copy-start.32
  389.6 4.4 copy-start.32
  402.8 20.6 %copy-start.7 = (bf16[384,2048]{1,0:T(8,128)(2,1)S(1)}, bf16[384,2048]{1,0:T(8,128)(2,1)}, u32[]{:S(2)}) copy-start(bf16[384,2048]{1,0:T(8,128)(2,1)} %copy-done.6) | copy-start | bytes 4718596
  404.1 20.9 %copy-start.37 = (f32[384,64]{0,1:T(8,128)S(1)}, f32[384,64]{0,1:T(8,128)}, u32[]{:S(2)}) copy-start(f32[384,64]{0,1:T(8,128)} %copy-done.36) | copy-start | bytes 294916
  404.1 20.9 %copy-start.39 = (f32[384,64]{0,1:T(8,128)S(1)}, f32[384,64]{0,1:T(8,128)}, u32[]{:S(2)}) copy-start(f32[384,64]{0,1:T(8,128)} %copy-done.38) | copy-start | bytes 294916
  404.1 21.0 %copy-start.40 = (f32[4,384,128]{1,2,0:T(8,128)S(1)}, f32[4,384,128]{1,2,0:T(8,128)}, u32[]{:S(2)}) copy-start(f32[4,384,128]{1,2,0:T(8,128)} %get-tuple-element.174) | copy-start | bytes 2359300
  473.3 268.5 %collective-permute-start.1 = (bf16[4,256,1280]{2,1,0:T(8,128)(2,1)}, bf16[4,256,1280]{2,1,0:T(8,128)(2,1)}, u32[]{:S(2)}, u32[]{:S(2)}) collective-permute-start(bf16[4,256,1280]{2,1,0:T(8,128)(2,1)} %bitcast.53), channel_id=1, source_target_pairs={{0,4},{4,0},{8,12},{12,8},{16,20},{20,16},{24,28},{28,24},{1,5},{5... | collective-permute-start | bytes 7864328 | tf_op jit(solution)/shard_map/ppermute | solution.py:735
  477.3 270.0 %collective-permute-start.16 = (bf16[4,256,1408]{2,1,0:T(8,128)(2,1)}, bf16[4,256,1408]{2,1,0:T(8,128)(2,1)}, u32[]{:S(2)}, u32[]{:S(2)}) collective-permute-start(bf16[4,256,1408]{2,1,0:T(8,128)(2,1)} %dynamic-slice_bitcast_fusion), channel_id=1, source_target_pairs={{0,4},{4,0},{8,12},{12,8},{16,20},{20,16},{24,28},{28,24},{1,5},{5... | collective-permute-start | bytes 8650760 | tf_op jit(solution)/shard_map/ppermute | solution.py:735
  587.8 3.7 copy-start.28
  591.5 159.2 %collective-permute-start.11 = (bf16[4,256,1408]{2,1,0:T(8,128)(2,1)}, bf16[4,256,1408]{2,1,0:T(8,128)(2,1)}, u32[]{:S(2)}, u32[]{:S(2)}) collective-permute-start(bf16[4,256,1408]{2,1,0:T(8,128)(2,1)} %dynamic-slice_bitcast_fusion.1), channel_id=1, source_target_pairs={{0,4},{4,0},{8,12},{12,8},{16,20},{20,16},{24,28},{28,24},{1,5},{5... | collective-permute-start | bytes 8650760 | tf_op jit(solution)/shard_map/ppermute | solution.py:735
  596.3 58.7 %copy-start.35 = (bf16[384,2048]{1,0:T(8,128)(2,1)S(1)}, bf16[384,2048]{1,0:T(8,128)(2,1)}, u32[]{:S(2)}) copy-start(bf16[384,2048]{1,0:T(8,128)(2,1)} %copy-done.33) | copy-start | bytes 4718596
  596.3 58.7 %copy-start.55 = (bf16[384,1408]{1,0:T(8,128)(2,1)S(1)}, bf16[384,1408]{1,0:T(8,128)(2,1)}, u32[]{:S(2)}) copy-start(bf16[384,1408]{1,0:T(8,128)(2,1)} %get-tuple-element.413) | copy-start | bytes 3244036
  658.6 3.4 copy-start.16
  662.0 93.7 %collective-permute-start.6 = (bf16[4,256,1408]{2,1,0:T(8,128)(2,1)}, bf16[4,256,1408]{2,1,0:T(8,128)(2,1)}, u32[]{:S(2)}, u32[]{:S(2)}) collective-permute-start(bf16[4,256,1408]{2,1,0:T(8,128)(2,1)} %dynamic-slice_bitcast_fusion.2), channel_id=1, source_target_pairs={{0,4},{4,0},{8,12},{12,8},{16,20},{20,16},{24,28},{28,24},{1,5},{5... | collective-permute-start | bytes 8650760 | tf_op jit(solution)/shard_map/ppermute | solution.py:735
  741.8 5.5 slice-start
  744.3 3.0 slice-start.1
  744.6 16.5 %collective-permute-start.4 = (bf16[2,128,1280]{2,1,0:T(8,128)(2,1)S(1)}, bf16[2,128,1280]{2,1,0:T(8,128)(2,1)S(1)}, u32[]{:S(2)}, u32[]{:S(2)}) collective-permute-start(bf16[2,128,1280]{2,1,0:T(8,128)(2,1)S(1)} %dynamic-slice_bitcast_fusion.9), channel_id=1, source_target_pairs={{0,8},{4,12},{8,0},{12,4},{16,24},{20,28},{24,16},{28,20},{1,9},{5... | collective-permute-start | bytes 1966088 | tf_op jit(solution)/shard_map/ppermute | solution.py:735
  746.0 16.6 %collective-permute-start.2 = (bf16[2,128,1280]{2,1,0:T(8,128)(2,1)S(1)}, bf16[2,128,1280]{2,1,0:T(8,128)(2,1)S(1)}, u32[]{:S(2)}, u32[]{:S(2)}) collective-permute-start(bf16[2,128,1280]{2,1,0:T(8,128)(2,1)S(1)} %dynamic-slice_bitcast_fusion.10), channel_id=1, source_target_pairs={{0,16},{4,20},{8,24},{12,28},{16,0},{20,4},{24,8},{28,12},{1,17},{... | collective-permute-start | bytes 1966088 | tf_op jit(solution)/shard_map/ppermute | solution.py:735
  747.3 4.3 slice-start.2
  750.3 27.4 %collective-permute-start.17 = (bf16[2,128,1408]{2,1,0:T(8,128)(2,1)S(1)}, bf16[2,128,1408]{2,1,0:T(8,128)(2,1)S(1)}, u32[]{:S(2)}, u32[]{:S(2)}) collective-permute-start(bf16[2,128,1408]{2,1,0:T(8,128)(2,1)S(1)} %dynamic-slice_bitcast_fusion.4), channel_id=1, source_target_pairs={{0,16},{4,20},{8,24},{12,28},{16,0},{20,4},{24,8},{28,12},{1,17},{... | collective-permute-start | bytes 2162696 | tf_op jit(solution)/shard_map/ppermute | solution.py:735
  750.6 5.1 slice-start.4
  750.7 5.1 slice-start.5
  750.7 28.0 %collective-permute-start.19 = (bf16[2,128,1408]{2,1,0:T(8,128)(2,1)S(1)}, bf16[2,128,1408]{2,1,0:T(8,128)(2,1)S(1)}, u32[]{:S(2)}, u32[]{:S(2)}) collective-permute-start(bf16[2,128,1408]{2,1,0:T(8,128)(2,1)S(1)} %dynamic-slice_bitcast_fusion.3), channel_id=1, source_target_pairs={{0,8},{4,12},{8,0},{12,4},{16,24},{20,28},{24,16},{28,20},{1,9},{5... | collective-permute-start | bytes 2162696 | tf_op jit(solution)/shard_map/ppermute | solution.py:735
  755.7 37.4 %collective-permute-start.12 = (bf16[2,128,1408]{2,1,0:T(8,128)(2,1)S(1)}, bf16[2,128,1408]{2,1,0:T(8,128)(2,1)S(1)}, u32[]{:S(2)}, u32[]{:S(2)}) collective-permute-start(bf16[2,128,1408]{2,1,0:T(8,128)(2,1)S(1)} %dynamic-slice_bitcast_fusion.6), channel_id=1, source_target_pairs={{0,16},{4,20},{8,24},{12,28},{16,0},{20,4},{24,8},{28,12},{1,17},{... | collective-permute-start | bytes 2162696 | tf_op jit(solution)/shard_map/ppermute | solution.py:735
  761.1 32.3 %collective-permute-start.14 = (bf16[2,128,1408]{2,1,0:T(8,128)(2,1)S(1)}, bf16[2,128,1408]{2,1,0:T(8,128)(2,1)S(1)}, u32[]{:S(2)}, u32[]{:S(2)}) collective-permute-start(bf16[2,128,1408]{2,1,0:T(8,128)(2,1)S(1)} %dynamic-slice_bitcast_fusion.5), channel_id=1, source_target_pairs={{0,8},{4,12},{8,0},{12,4},{16,24},{20,28},{24,16},{28,20},{1,9},{5... | collective-permute-start | bytes 2162696 | tf_op jit(solution)/shard_map/ppermute | solution.py:735
  762.6 45.9 %collective-permute-start.7 = (bf16[2,128,1408]{2,1,0:T(8,128)(2,1)S(1)}, bf16[2,128,1408]{2,1,0:T(8,128)(2,1)S(1)}, u32[]{:S(2)}, u32[]{:S(2)}) collective-permute-start(bf16[2,128,1408]{2,1,0:T(8,128)(2,1)S(1)} %dynamic-slice_bitcast_fusion.8), channel_id=1, source_target_pairs={{0,16},{4,20},{8,24},{12,28},{16,0},{20,4},{24,8},{28,12},{1,17},{... | collective-permute-start | bytes 2162696 | tf_op jit(solution)/shard_map/ppermute | solution.py:735
  777.7 32.3 %collective-permute-start.9 = (bf16[2,128,1408]{2,1,0:T(8,128)(2,1)S(1)}, bf16[2,128,1408]{2,1,0:T(8,128)(2,1)S(1)}, u32[]{:S(2)}, u32[]{:S(2)}) collective-permute-start(bf16[2,128,1408]{2,1,0:T(8,128)(2,1)S(1)} %dynamic-slice_bitcast_fusion.7), channel_id=1, source_target_pairs={{0,8},{4,12},{8,0},{12,4},{16,24},{20,28},{24,16},{28,20},{1,9},{5... | collective-permute-start | bytes 2162696 | tf_op jit(solution)/shard_map/ppermute | solution.py:735
  778.7 37.0 %collective-permute-start.5 = (bf16[1,128,1280]{2,1,0:T(8,128)(2,1)S(1)}, bf16[1,128,1280]{2,1,0:T(8,128)(2,1)S(1)}, u32[]{:S(2)}, u32[]{:S(2)}) collective-permute-start(bf16[1,128,1280]{2,1,0:T(8,128)(2,1)S(1)} %constant_dynamic-slice_fusion.8), channel_id=1, source_target_pairs={{0,16},{4,20},{8,24},{12,28},{16,0},{20,4},{24,8},{28,12},{1,17},{... | collective-permute-start | bytes 983048 | tf_op jit(solution)/shard_map/ppermute | solution.py:735
  793.1 24.7 %collective-permute-start.3 = (bf16[1,128,1280]{2,1,0:T(8,128)(2,1)S(1)}, bf16[1,128,1280]{2,1,0:T(8,128)(2,1)S(1)}, u32[]{:S(2)}, u32[]{:S(2)}) collective-permute-start(bf16[1,128,1280]{2,1,0:T(8,128)(2,1)S(1)} %constant_dynamic-slice_fusion.9), channel_id=1, source_target_pairs={{0,8},{4,12},{8,0},{12,4},{16,24},{20,28},{24,16},{28,20},{1,9},{5... | collective-permute-start | bytes 983048 | tf_op jit(solution)/shard_map/ppermute | solution.py:735
  793.4 30.1 %collective-permute-start.18 = (bf16[1,128,1408]{2,1,0:T(8,128)(2,1)}, bf16[1,128,1408]{2,1,0:T(8,128)(2,1)}, u32[]{:S(2)}, u32[]{:S(2)}) collective-permute-start(bf16[1,128,1408]{2,1,0:T(8,128)(2,1)} %constant_dynamic-slice_fusion.3), channel_id=1, source_target_pairs={{0,8},{4,12},{8,0},{12,4},{16,24},{20,28},{24,16},{28,20},{1,9},{5... | collective-permute-start | bytes 1081352 | tf_op jit(solution)/shard_map/ppermute | solution.py:735
  795.0 16.2 %copy-start.20 = (bf16[2,128,1408]{2,1,0:T(8,128)(2,1)}, bf16[2,128,1408]{2,1,0:T(8,128)(2,1)S(1)}, u32[]{:S(2)}) copy-start(bf16[2,128,1408]{2,1,0:T(8,128)(2,1)S(1)} %fusion.53) | copy-start | bytes 2162692
  808.6 16.3 %collective-permute-start.20 = (bf16[1,128,1408]{2,1,0:T(8,128)(2,1)}, bf16[1,128,1408]{2,1,0:T(8,128)(2,1)}, u32[]{:S(2)}, u32[]{:S(2)}) collective-permute-start(bf16[1,128,1408]{2,1,0:T(8,128)(2,1)} %constant_dynamic-slice_fusion.2), channel_id=1, source_target_pairs={{0,16},{4,20},{8,24},{12,28},{16,0},{20,4},{24,8},{28,12},{1,17},{... | collective-permute-start | bytes 1081352 | tf_op jit(solution)/shard_map/ppermute | solution.py:735
  810.0 7.8 copy-start.22
  810.0 20.0 %collective-permute-start.13 = (bf16[1,128,1408]{2,1,0:T(8,128)(2,1)}, bf16[1,128,1408]{2,1,0:T(8,128)(2,1)}, u32[]{:S(2)}, u32[]{:S(2)}) collective-permute-start(bf16[1,128,1408]{2,1,0:T(8,128)(2,1)} %constant_dynamic-slice_fusion.5), channel_id=1, source_target_pairs={{0,8},{4,12},{8,0},{12,4},{16,24},{20,28},{24,16},{28,20},{1,9},{5... | collective-permute-start | bytes 1081352 | tf_op jit(solution)/shard_map/ppermute | solution.py:735
  815.7 15.4 %collective-permute-start.15 = (bf16[1,128,1408]{2,1,0:T(8,128)(2,1)}, bf16[1,128,1408]{2,1,0:T(8,128)(2,1)}, u32[]{:S(2)}, u32[]{:S(2)}) collective-permute-start(bf16[1,128,1408]{2,1,0:T(8,128)(2,1)} %constant_dynamic-slice_fusion.4), channel_id=1, source_target_pairs={{0,16},{4,20},{8,24},{12,28},{16,0},{20,4},{24,8},{28,12},{1,17},{... | collective-permute-start | bytes 1081352 | tf_op jit(solution)/shard_map/ppermute | solution.py:735
  817.8 19.9 %collective-permute-start.8 = (bf16[1,128,1408]{2,1,0:T(8,128)(2,1)}, bf16[1,128,1408]{2,1,0:T(8,128)(2,1)}, u32[]{:S(2)}, u32[]{:S(2)}) collective-permute-start(bf16[1,128,1408]{2,1,0:T(8,128)(2,1)} %constant_dynamic-slice_fusion.7), channel_id=1, source_target_pairs={{0,8},{4,12},{8,0},{12,4},{16,24},{20,28},{24,16},{28,20},{1,9},{5... | collective-permute-start | bytes 1081352 | tf_op jit(solution)/shard_map/ppermute | solution.py:735
  823.5 7.7 copy-start.21
  823.5 19.3 %collective-permute-start.10 = (bf16[1,128,1408]{2,1,0:T(8,128)(2,1)}, bf16[1,128,1408]{2,1,0:T(8,128)(2,1)}, u32[]{:S(2)}, u32[]{:S(2)}) collective-permute-start(bf16[1,128,1408]{2,1,0:T(8,128)(2,1)} %constant_dynamic-slice_fusion.6), channel_id=1, source_target_pairs={{0,16},{4,20},{8,24},{12,28},{16,0},{20,4},{24,8},{28,12},{1,17},{... | collective-permute-start | bytes 1081352 | tf_op jit(solution)/shard_map/ppermute | solution.py:735
  824.8 12.9 %copy-start.23 = (bf16[2,128,1408]{2,1,0:T(8,128)(2,1)S(1)}, bf16[2,128,1408]{2,1,0:T(8,128)(2,1)}, u32[]{:S(2)}) copy-start(bf16[2,128,1408]{2,1,0:T(8,128)(2,1)} %copy-done.22) | copy-start | bytes 2162692
  845.2 3.0 copy-start.18
  845.2 4.7 copy-start.1
  (44 other events, 83.4 us)
Sparse Core Ops, SparseCore 0:
  10.2 82.8 all-gather.1
  655.1 32.9 all-reduce.1

commit v2 on v1

--- a/solution.py
+++ b/solution.py
@@ -39,11 +39,44 @@
     return pl.CostEstimate(flops=flops, bytes_accessed=moved, transcendentals=0)
 
 
-def greet(peers):
+def greet(peers, line=False):
     barrier = pltpu.get_barrier_semaphore()
     for peer in peers:
         pl.semaphore_signal(barrier, inc=1, device_id=peer, device_id_type=MESH)
-    pl.semaphore_wait(barrier, len(peers))
+    if not line:
+        pl.semaphore_wait(barrier, len(peers))
+        return
+    own, plane = lax.axis_index("tok"), lax.axis_index("tp")
+    last = lax.axis_size("tp") - 1
+
+    @pl.when(plane > 0)
+    def _():
+        pl.semaphore_signal(barrier, inc=1, device_id=(own, plane - 1), device_id_type=MESH)
+
+    @pl.when(plane < last)
+    def _():
+        pl.semaphore_signal(barrier, inc=1, device_id=(own, plane + 1), device_id_type=MESH)
+
+    end = (plane == 0) | (plane == last)
+
+    @pl.when(end)
+    def _():
+        pl.semaphore_wait(barrier, len(peers) + 1)
+
+    @pl.when(jnp.logical_not(end))
+    def _():
+        pl.semaphore_wait(barrier, len(peers) + 2)
+
+
+def run(*flows):
+    waiting = [[next(flow), number, flow] for number, flow in enumerate(flows)]
+    while waiting:
+        waiting.sort(key=lambda entry: entry[:2])
+        entry = waiting[0]
+        try:
+            entry[0] = next(entry[2])
+        except StopIteration:
+            waiting.pop(0)
 
 
 def deal_tables(own, stages, blocks_here, lens_ref, flags_ref):
@@ -109,14 +142,18 @@
     return value
 
 
-def deal_body(lens_ref, flags_ref, own_ref, out_ref, keep, send, recv, send_sem, recv_sem):
+def bit_peers(stages):
+    own, plane = lax.axis_index("tok"), lax.axis_index("tp")
+    return [(own ^ (1 << stage), plane) for stage in range(stages)]
+
+
+def deal_flow(lens_ref, flags_ref, own_ref, out_ref, scratch, pace=4.3):
+    keep, send, recv, send_sem, recv_sem = scratch
     stages = keep.shape[0]
     own = lax.axis_index("tok")
-    plane = lax.axis_index("tp")
     blocks_here = own_ref.shape[0]
     rows = BLOCK // CHUNKS
-    peers = [(own ^ (1 << stage), plane) for stage in range(stages)]
-    greet(peers)
+    peers = bit_peers(stages)
     keeps, sends, finals = deal_tables(own, stages, blocks_here, lens_ref, flags_ref)
 
     def copy(stage, chunk):
@@ -131,16 +168,15 @@
 
     def held(stage, chunk):
         if stage == 0:
-            span = pl.ds(pl.multiple_of(chunk * rows, rows), rows)
-            return [own_ref[i, span, :] for i in range(blocks_here)]
+            return [own_ref[i, pl.ds(chunk * rows, rows), :] for i in range(blocks_here)]
         before = stage - 1
         return [keep[before, chunk, i] for i in range(SLOTS)] + [
             recv[before, chunk, i] for i in range(SLOTS)
         ]
 
     for stage in range(stages):
-
-        def step(chunk, carry, stage=stage):
+        for chunk in range(CHUNKS):
+            yield 0.0 if stage == 0 else 1 + 0.4 * chunk + pace * (stage - 1) * (chunk + 1)
             if stage > 0:
                 copy(stage - 1, chunk).wait_recv()
             options = held(stage, chunk)
@@ -149,19 +185,13 @@
             copy(stage, chunk).start()
             for slot in range(SLOTS):
                 keep[stage, chunk, slot] = choose(keeps[stage][slot], options)
-            return carry
-
-        lax.fori_loop(0, CHUNKS, step, 0)
-
-    def finish(chunk, carry):
+    for chunk in range(CHUNKS):
+        yield 3 + pace * (chunk + stages - 1)
         copy(stages - 1, chunk).wait_recv()
         options = held(stages, chunk)
-        span = pl.ds(pl.multiple_of(chunk * rows, rows), rows)
         for slot in range(SLOTS):
-            out_ref[slot, span, :] = choose(finals[slot], options)
-        return carry
-
-    lax.fori_loop(0, CHUNKS, finish, 0)
+            out_ref[slot, pl.ds(chunk * rows, rows), :] = choose(finals[slot], options)
+    yield 1e6
 
     def drain(chunk, carry):
         for stage in range(stages):
@@ -171,62 +201,70 @@
     lax.fori_loop(0, CHUNKS, drain, 0)
 
 
+def deal_scratch(stages, width, kind):
+    moved = (stages, CHUNKS, SLOTS, BLOCK // CHUNKS, width)
+    return [pltpu.VMEM(moved, kind)] * 3 + [pltpu.SemaphoreType.DMA((stages, CHUNKS))] * 2
+
+
 def stages_of(axis):
     return int(math.log2(lax.axis_size(axis)))
 
 
+def deal_body(lens_ref, flags_ref, own_ref, out_ref, *scratch):
+    greet(bit_peers(scratch[0].shape[0]))
+    run(deal_flow(lens_ref, flags_ref, own_ref, out_ref, scratch))
+
+
 def deal(doc_lengths, keep_flags, blocks, collective_id):
-    stages = stages_of("tok")
     width = blocks.shape[2]
-    rows = BLOCK // CHUNKS
-    moved = (stages, CHUNKS, SLOTS, rows, width)
     return pl.pallas_call(
         deal_body,
         out_shape=jax.ShapeDtypeStruct((SLOTS, BLOCK, width), blocks.dtype),
         in_specs=[smem(), smem(), vmem()],
         out_specs=vmem(),
-        scratch_shapes=[
-            pltpu.VMEM(moved, blocks.dtype),
-            pltpu.VMEM(moved, blocks.dtype),
-            pltpu.VMEM(moved, blocks.dtype),
-            pltpu.SemaphoreType.DMA((stages, CHUNKS)),
-            pltpu.SemaphoreType.DMA((stages, CHUNKS)),
-        ],
+        scratch_shapes=deal_scratch(stages_of("tok"), width, blocks.dtype),
         compiler_params=params(collective_id),
         cost_estimate=cost(0, 40_000_000),
         name="deal",
     )(doc_lengths, keep_flags, blocks)
 
 
-def undeal_body(
-    lens_ref, flags_ref, kept_ref, home_ref, gains_ref, out_ref, sum_ref,
-    hold, recv, gain_recv, send_sem, recv_sem, gain_send_sem, gain_recv_sem,
-):
+def deal_gather_body(lens_ref, flags_ref, own_ref, mine_ref, out_ref, all_ref, *scratch):
+    dealing, sems = scratch[:5], scratch[5:]
+    own, plane, planes = lax.axis_index("tok"), lax.axis_index("tp"), all_ref.shape[0]
+    greet(bit_peers(dealing[0].shape[0]), line=True)
+    all_ref[plane] = mine_ref[...]
+    run(
+        line_gather(own, plane, planes, [(all_ref,) + sems], 0.0, 8.5),
+        deal_flow(lens_ref, flags_ref, own_ref, out_ref, dealing),
+    )
+
+
+def deal_gather(doc_lengths, keep_flags, blocks, mine, collective_id):
+    width = blocks.shape[2]
+    planes = lax.axis_size("tp")
+    return pl.pallas_call(
+        deal_gather_body,
+        out_shape=(
+            jax.ShapeDtypeStruct((SLOTS, BLOCK, width), blocks.dtype),
+            jax.ShapeDtypeStruct((planes,) + mine.shape, mine.dtype),
+        ),
+        in_specs=[smem(), smem(), vmem(), vmem()],
+        out_specs=(vmem(), vmem()),
+        scratch_shapes=deal_scratch(stages_of("tok"), width, blocks.dtype) + line_sems(planes),
+        compiler_params=params(collective_id),
+        cost_estimate=cost(0, 40_000_000),
+        name="deal_gather",
+    )(doc_lengths, keep_flags, blocks, mine)
+
+
+def undeal_flow(lens_ref, flags_ref, kept_ref, home_ref, out_ref, scratch, pace=4.3):
+    hold, recv, send_sem, recv_sem = scratch
     stages = recv.shape[0]
     own = lax.axis_index("tok")
-    plane = lax.axis_index("tp")
-    devices = 1 << stages
     blocks_here = home_ref.shape[0]
     rows = BLOCK // CHUNKS
-    share = sum_ref.shape[1]
-    peers = [(own ^ (1 << stage), plane) for stage in range(stages)]
-    greet([(own ^ step, plane) for step in range(1, devices)])
-
-    def gain_copy(step):
-        there = own ^ step
-        return pltpu.make_async_remote_copy(
-            src_ref=gains_ref.at[:, pl.ds(pl.multiple_of(there * share, share), share)]
-            if share % 128 == 0
-            else gains_ref,
-            dst_ref=gain_recv.at[step],
-            send_sem=gain_send_sem.at[step],
-            recv_sem=gain_recv_sem.at[step],
-            device_id=(there, plane),
-            device_id_type=MESH,
-        )
-
-    for step in range(1, devices):
-        gain_copy(step).start()
+    peers = bit_peers(stages)
     keeps, sends, finals = deal_tables(own, stages, blocks_here, lens_ref, flags_ref)
 
     def copy(stage, chunk):
@@ -239,52 +277,36 @@
             device_id_type=MESH,
         )
 
+    def pick_place(places, options, place, value):
+        for index, option in zip(places, options):
+            value = jnp.where(index == place, option, value)
+        return value
+
     last = stages - 1
-
-    def begin(chunk, carry):
-        span = pl.ds(pl.multiple_of(chunk * rows, rows), rows)
-        options = [kept_ref[slot, span, :] for slot in range(SLOTS)]
-        for place in range(SLOTS, 2 * SLOTS):
-            value = options[0]
-            for slot in range(1, SLOTS):
-                value = jnp.where(finals[slot] == place, options[slot], value)
-            hold[last, chunk, place] = value
-        copy(last, chunk).start()
-        for place in range(SLOTS):
-            value = options[0]
-            for slot in range(1, SLOTS):
-                value = jnp.where(finals[slot] == place, options[slot], value)
-            hold[last, chunk, place] = value
-        return carry
-
-    lax.fori_loop(0, CHUNKS, begin, 0)
-    for stage in range(last, -1, -1):
-
-        def step(chunk, carry, stage=stage):
-            copy(stage, chunk).wait_recv()
-            options = [hold[stage, chunk, i] for i in range(SLOTS)] + [
-                recv[stage, chunk, i] for i in range(SLOTS)
-            ]
-            places = keeps[stage] + sends[stage]
-
-            def pick(place, value):
-                for index, option in zip(places, options):
-                    value = jnp.where(index == place, option, value)
-                return value
-
-            if stage == 0:
-                span = pl.ds(pl.multiple_of(chunk * rows, rows), rows)
+    for stage in range(last, -2, -1):
+        for chunk in range(CHUNKS):
+            yield 0.0 if stage == last else 1 + pace * (chunk + last - stage - (stage < 0))
+            span = pl.ds(chunk * rows, rows)
+            if stage == last:
+                options = [kept_ref[slot, span, :] for slot in range(SLOTS)]
+                places = finals
+            else:
+                copy(stage + 1, chunk).wait_recv()
+                options = [hold[stage + 1, chunk, i] for i in range(SLOTS)] + [
+                    recv[stage + 1, chunk, i] for i in range(SLOTS)
+                ]
+                places = keeps[stage + 1] + sends[stage + 1]
+            if stage < 0:
                 for place in range(blocks_here):
-                    out_ref[place, span, :] = pick(place, home_ref[place, span, :])
+                    home = home_ref[place, span, :]
+                    out_ref[place, span, :] = pick_place(places, options, place, home)
             else:
                 for place in range(SLOTS, 2 * SLOTS):
-                    hold[stage - 1, chunk, place] = pick(place, options[0])
-                copy(stage - 1, chunk).start()
+                    hold[stage, chunk, place] = pick_place(places, options, place, options[0])
+                copy(stage, chunk).start()
                 for place in range(SLOTS):
-                    hold[stage - 1, chunk, place] = pick(place, options[0])
-            return carry
-
-        lax.fori_loop(0, CHUNKS, step, 0)
+                    hold[stage, chunk, place] = pick_place(places, options, place, options[0])
+    yield 1e6
 
     def drain(chunk, carry):
         for stage in range(stages):
@@ -292,10 +314,44 @@
         return carry
 
     lax.fori_loop(0, CHUNKS, drain, 0)
-    if share % 128 == 0:
-        total = gains_ref[:, pl.ds(pl.multiple_of(own * share, share), share)]
-    else:
-        total = gains_ref[...]
+
+
+def undeal_scratch(stages, width, kind):
+    rows = BLOCK // CHUNKS
+    return [
+        pltpu.VMEM((stages, CHUNKS, 2 * SLOTS, rows, width), kind),
+        pltpu.VMEM((stages, CHUNKS, SLOTS, rows, width), kind),
+    ] + [pltpu.SemaphoreType.DMA((stages, CHUNKS))] * 2
+
+
+def undeal_body(lens_ref, flags_ref, kept_ref, home_ref, gains_ref, out_ref, sum_ref, *scratch):
+    undealing = scratch[:4]
+    gain_recv, gain_send_sem, gain_recv_sem = scratch[4:]
+    own, plane = lax.axis_index("tok"), lax.axis_index("tp")
+    devices = gain_recv.shape[0]
+    share = sum_ref.shape[1]
+    greet([(own ^ step, plane) for step in range(1, devices)])
+
+    def portion(there):
+        if share % 128 == 0 and share < gains_ref.shape[1]:
+            return gains_ref.at[:, pl.ds(pl.multiple_of(there * share, share), share)]
+        return gains_ref
+
+    def gain_copy(step):
+        there = own ^ step
+        return pltpu.make_async_remote_copy(
+            src_ref=portion(there),
+            dst_ref=gain_recv.at[step],
+            send_sem=gain_send_sem.at[step],
+            recv_sem=gain_recv_sem.at[step],
+            device_id=(there, plane),
+            device_id_type=MESH,
+        )
+
+    for step in range(1, devices):
+        gain_copy(step).start()
+    run(undeal_flow(lens_ref, flags_ref, kept_ref, home_ref, out_ref, undealing))
+    total = portion(own)[...]
     for step in range(1, devices):
         gain_copy(step).wait()
         total = total + gain_recv[step]
@@ -306,7 +362,6 @@
     stages = stages_of("tok")
     devices = 1 << stages
     width = kept.shape[2]
-    rows = BLOCK // CHUNKS
     share = width // devices
     share = share if share % 128 == 0 else width
     return pl.pallas_call(
@@ -317,12 +372,9 @@
         ),
         in_specs=[smem(), smem(), vmem(), vmem(), vmem()],
         out_specs=(vmem(), vmem()),
-        scratch_shapes=[
-            pltpu.VMEM((stages, CHUNKS, 2 * SLOTS, rows, width), kept.dtype),
-            pltpu.VMEM((stages, CHUNKS, SLOTS, rows, width), kept.dtype),
+        scratch_shapes=undeal_scratch(stages, width, kept.dtype)
+        + [
             pltpu.VMEM((devices, 8, share), F32),
-            pltpu.SemaphoreType.DMA((stages, CHUNKS)),
-            pltpu.SemaphoreType.DMA((stages, CHUNKS)),
             pltpu.SemaphoreType.DMA((devices,)),
             pltpu.SemaphoreType.DMA((devices,)),
         ],
@@ -459,108 +511,103 @@
     )(part)
 
 
-def line_copies(own, plane, sources, targets, send_sem, recv_sem):
-    def right(index):
-        return pltpu.make_async_remote_copy(
-            src_ref=sources.at[index],
-            dst_ref=targets.at[index],
-            send_sem=send_sem.at[0, index],
-            recv_sem=recv_sem.at[0, index],
-            device_id=(own, plane + 1),
-            device_id_type=MESH,
-        )
-
-    def left(index):
-        return pltpu.make_async_remote_copy(
-            src_ref=sources.at[index],
-            dst_ref=targets.at[index],
-            send_sem=send_sem.at[1, index],
-            recv_sem=recv_sem.at[1, index],
-            device_id=(own, plane - 1),
-            device_id_type=MESH,
-        )
-
-    return right, left
-
-
-def line_greet(own, plane, planes):
-    barrier = pltpu.get_barrier_semaphore()
-
-    @pl.when(plane > 0)
-    def _():
-        pl.semaphore_signal(barrier, inc=1, device_id=(own, plane - 1), device_id_type=MESH)
-
-    @pl.when(plane < planes - 1)
-    def _():
-        pl.semaphore_signal(barrier, inc=1, device_id=(own, plane + 1), device_id_type=MESH)
-
-    end = (plane == 0) | (plane == planes - 1)
-
-    @pl.when(end)
-    def _():
-        pl.semaphore_wait(barrier, 1)
-
-    @pl.when(jnp.logical_not(end))
-    def _():
-        pl.semaphore_wait(barrier, 2)
-
-
-def line_gather(own, plane, planes, out, send_sem, recv_sem):
-    right, left = line_copies(own, plane, out, out, send_sem, recv_sem)
+def line_sems(planes):
+    return [pltpu.SemaphoreType.DMA((2, planes))] * 2
+
+
+def line_copy(own, plane, step, source, target, send_sem, recv_sem, index):
+    side = 0 if step > 0 else 1
+    return pltpu.make_async_remote_copy(
+        src_ref=source,
+        dst_ref=target,
+        send_sem=send_sem.at[side, index],
+        recv_sem=recv_sem.at[side, index],
+        device_id=(own, plane + step),
+        device_id_type=MESH,
+    )
+
+
+def line_gather(own, plane, planes, arrays, start, pace):
     last = planes - 1
+
+    def right(array, index):
+        out, send_sem, recv_sem = array
+        return line_copy(own, plane, 1, out.at[index], out.at[index], send_sem, recv_sem, index)
+
+    def left(array, index):
+        out, send_sem, recv_sem = array
+        return line_copy(own, plane, -1, out.at[index], out.at[index], send_sem, recv_sem, index)
+
     for step in range(1, planes + 1):
+        yield start + pace * (step - 1)
         before, after = plane - (step - 1), plane + (step - 1)
 
         @pl.when(before >= 0)
         def _():
-            if step > 1:
-                right(before).wait_recv()
-            if step < planes:
-
-                @pl.when(plane < last)
-                def _():
-                    right(before).start()
+            for array in arrays:
+                if step > 1:
+                    right(array, before).wait_recv()
+                if step < planes:
+
+                    @pl.when(plane < last)
+                    def _():
+                        right(array, before).start()
 
         @pl.when(after <= last)
         def _():
-            if step > 1:
-                left(after).wait_recv()
-            if step < planes:
-
-                @pl.when(plane > 0)
-                def _():
-                    left(after).start()
+            for array in arrays:
+                if step > 1:
+                    left(array, after).wait_recv()
+                if step < planes:
+
+                    @pl.when(plane > 0)
+                    def _():
+                        left(array, after).start()
 
     for index in range(planes):
 
         @pl.when((index <= plane) & (plane < last))
         def _():
-            right(index).wait_send()
+            for array in arrays:
+                right(array, index).wait_send()
 
         @pl.when((index >= plane) & (plane > 0))
         def _():
-            left(index).wait_send()
-
-
-def line_reduce(own, plane, planes, part, total, send, recv, send_sem, recv_sem):
+            for array in arrays:
+                left(array, index).wait_send()
+
+
+def line_reduce(own, plane, planes, part, total, send, recv, send_sem, recv_sem, start, pace):
     last = planes - 1
-    right, _ = line_copies(own, plane, send.at[0], recv.at[0], send_sem, recv_sem)
-    _, left = line_copies(own, plane, send.at[1], recv.at[1], send_sem, recv_sem)
+
+    def right(index):
+        return line_copy(
+            own, plane, 1, send.at[index], recv.at[index], send_sem, recv_sem, index
+        )
+
+    def left(index):
+        slot = jnp.where(index == plane - 1, planes, index)
+        return line_copy(
+            own, plane, -1, send.at[index], recv.at[slot], send_sem, recv_sem, index
+        )
+
+    def add(index):
+        send[index] = (part[index].astype(F32) + recv[index].astype(F32)).astype(send.dtype)
+
     for step in range(1, planes):
+        yield start + pace * (step - 1)
         upper, lower = planes - step + plane, step - planes + plane
 
         @pl.when((upper <= last) & (plane < last))
         def _():
             @pl.when(plane == 0)
             def _():
-                send[0, upper] = part[upper]
+                send[upper] = part[upper]
 
             @pl.when(plane > 0)
             def _():
                 right(upper).wait_recv()
-                send[0, upper] = (
-                    part[upper].astype(F32) + recv[0, upper].astype(F32)
-                ).astype(send.dtype)
+                add(upper)
 
             right(upper).start()
 
@@ -568,28 +615,27 @@
         def _():
             @pl.when(plane == last)
             def _():
-                send[1, lower] = part[lower]
+                send[lower] = part[lower]
 
             @pl.when(plane < last)
             def _():
                 left(lower).wait_recv()
-                send[1, lower] = (
-                    part[lower].astype(F32) + recv[1, lower].astype(F32)
-                ).astype(send.dtype)
+                add(lower)
 
             left(lower).start()
 
+    yield start + pace * (planes - 1)
     total[...] = part[plane].astype(F32)
 
     @pl.when(plane > 0)
     def _():
         right(plane).wait_recv()
-        total[...] += recv[0, plane].astype(F32)
+        total[...] += recv[plane].astype(F32)
 
     @pl.when(plane < last)
     def _():
         left(plane).wait_recv()
-        total[...] += recv[1, plane].astype(F32)
+        total[...] += recv[planes].astype(F32)
 
     for index in range(planes):
 
@@ -602,173 +648,384 @@
             left(index).wait_send()
 
 
-def gather_tp_body(mine_ref, out_ref, send_sem, recv_sem):
-    planes = out_ref.shape[0]
-    own, plane = lax.axis_index("tok"), lax.axis_index("tp")
-    line_greet(own, plane, planes)
-    out_ref[plane] = mine_ref[...]
-    line_gather(own, plane, planes, out_ref, send_sem, recv_sem)
-
-
-def gather_tp(mine, collective_id):
-    planes = lax.axis_size("tp")
-    return pl.pallas_call(
-        gather_tp_body,
-        out_shape=jax.ShapeDtypeStruct((planes,) + mine.shape, mine.dtype),
-        in_specs=[vmem()],
-        out_specs=vmem(),
-        scratch_shapes=[
-            pltpu.SemaphoreType.DMA((2, planes)),
-            pltpu.SemaphoreType.DMA((2, planes)),
-        ],
-        compiler_params=params(collective_id),
-        cost_estimate=cost(0, 30_000_000),
-        name="gather_tp",
-    )(mine)
-
-
-def row_tiles(rows):
-    tile = 16
-    return [(start, tile) for start in range(0, rows, tile)]
-
-
-def ffn_math(plane, total, inputs, outputs, gathered):
-    hidden_ref, inv_ref, dy_ref, gain_ref = inputs
-    grad_ref, gains_ref = outputs
-    gains_ref[...] = jnp.zeros_like(gains_ref)
-
-    def tile(index, carry):
-        rows = pl.ds(pl.multiple_of(index * 16, 16), 16)
-        dn = total[rows, :]
-        hidden = hidden_ref[plane, rows, :]
-        inv = inv_ref[plane, rows, :]
-        weighted = gain_ref[...] * dn
-        mean = jnp.mean(weighted * hidden, axis=1, keepdims=True)
-        grad = (
-            keep_scale * dy_ref[plane, rows, :].astype(F32)
-            + inv * weighted
-            - hidden * (inv * inv * inv * mean)
-        )
-        grad_ref[rows, :] = grad
-        gathered[plane, rows, :] = grad.astype(BF16)
-        gains_ref[0:1, :] += jnp.sum(dn * hidden * inv, axis=0, keepdims=True)
-        return carry
-
-    lax.fori_loop(0, total.shape[0] // 16, tile, 0)
-
-
-def mixed_math(plane, total, inputs, outputs, gathered):
-    hidden_ref, x_ref = inputs
-
-    def tile(index, carry):
-        rows = pl.ds(pl.multiple_of(index * 16, 16), 16)
-        x = x_ref[plane, rows, :].astype(F32)
-        branch = (hidden_ref[plane, rows, :] - x) + total[rows, :]
-        gathered[plane, rows, :] = (x + keep_scale * branch).astype(BF16)
-        return carry
-
-    lax.fori_loop(0, total.shape[0] // 16, tile, 0)
-
-
-def attn_math(plane, total, inputs, outputs, gathered):
-    x_ref, inv_ref, dy_ref, grad_ref, gain_ref, ffn_gains_ref = inputs
-    (gains_ref,) = outputs
-    gains_ref[...] = ffn_gains_ref[...]
-
-    def tile(index, carry):
-        rows = pl.ds(pl.multiple_of(index * 16, 16), 16)
-        dn = total[rows, :]
-        x = x_ref[plane, rows, :].astype(F32)
-        inv = inv_ref[plane, rows, :]
-        weighted = gain_ref[...] * dn
-        mean = jnp.mean(weighted * x, axis=1, keepdims=True)
-        grad = (
-            (1.0 - keep_scale) * dy_ref[plane, rows, :].astype(F32)
-            + grad_ref[rows, :]
-            + inv * weighted
-            - x * (inv * inv * inv * mean)
-        )
-        gathered[plane, rows, :] = grad.astype(BF16)
-        gains_ref[1:2, :] += jnp.sum(dn * x * inv, axis=0, keepdims=True)
-        return carry
-
-    lax.fori_loop(0, total.shape[0] // 16, tile, 0)
-
-
-def sum_tp_body(math_rule, inputs, *refs):
-    part_ref, ins = refs[0], refs[1 : 1 + inputs]
-    outs, scratch = refs[1 + inputs : -7], refs[-7:]
-    gathered, outs = outs[0], outs[1:]
+def sum_flow(part_ref, gathered, scratch, math_rule, start=0.0, pace=8.7, extra=None):
     total, send, recv, send_sem, recv_sem, gather_send_sem, gather_recv_sem = scratch
     planes = part_ref.shape[0]
     own, plane = lax.axis_index("tok"), lax.axis_index("tp")
-    line_greet(own, plane, planes)
-    line_reduce(own, plane, planes, part_ref, total, send, recv, send_sem, recv_sem)
-    math_rule(plane, total, ins, outs, gathered)
-    line_gather(own, plane, planes, gathered, gather_send_sem, gather_recv_sem)
-
-
-def sum_tp(math_rule, part, inputs, out_shapes, collective_id, name):
-    planes = lax.axis_size("tp")
-    rows, width = part.shape
-    shard = rows // planes
-    part = part.reshape(planes, shard, width)
+    yield from line_reduce(
+        own, plane, planes, part_ref, total, send, recv, send_sem, recv_sem, start, pace
+    )
+    math_rule(plane, total, gathered)
+    arrays = [(gathered, gather_send_sem, gather_recv_sem)] + ([] if extra is None else [extra])
+    yield from line_gather(
+        own, plane, planes, arrays, start + pace * (planes - 1), pace
+    )
+
+
+def sum_scratch(planes, shard, width, kind):
+    return [
+        pltpu.VMEM((shard, width), F32),
+        pltpu.VMEM((planes, shard, width), kind),
+        pltpu.VMEM((planes + 1, shard, width), kind),
+    ] + line_sems(planes) * 2
+
+
+def ffn_math(hidden_ref, inv_ref, dy_ref, gain_ref, grad_ref, gains_ref):
+    def rule(plane, total, gathered):
+        gains_ref[...] = jnp.zeros_like(gains_ref)
+
+        def tile(index, carry):
+            rows = pl.ds(pl.multiple_of(index * 16, 16), 16)
+            dn = total[rows, :]
+            hidden = hidden_ref[plane, rows, :]
+            inv = inv_ref[plane, rows, :]
+            weighted = gain_ref[...] * dn
+            mean = jnp.mean(weighted * hidden, axis=1, keepdims=True)
+            grad = (
+                keep_scale * dy_ref[plane, rows, :].astype(F32)
+                + inv * weighted
+                - hidden * (inv * inv * inv * mean)
+            )
+            grad_ref[rows, :] = grad
+            gathered[plane, rows, :] = grad.astype(BF16)
+            gains_ref[0:1, :] += jnp.sum(dn * hidden * inv, axis=0, keepdims=True)
+            return carry
+
+        lax.fori_loop(0, total.shape[0] // 16, tile, 0)
+
+    return rule
+
+
+def mixed_math(hidden_ref, x_ref):
+    def rule(plane, total, gathered):
+        def tile(index, carry):
+            rows = pl.ds(pl.multiple_of(index * 16, 16), 16)
+            x = x_ref[plane, rows, :].astype(F32)
+            branch = (hidden_ref[plane, rows, :] - x) + total[rows, :]
+            gathered[plane, rows, :] = (x + keep_scale * branch).astype(BF16)
+            return carry
+
+        lax.fori_loop(0, total.shape[0] // 16, tile, 0)
+
+    return rule
+
+
+def attn_math(x_ref, inv_ref, dy_ref, grad_ref, gain_ref, ffn_gains_ref, gains_all):
+    def rule(plane, total, gathered):
+        gains_all[plane] = ffn_gains_ref[...]
+
+        def tile(index, carry):
+            rows = pl.ds(pl.multiple_of(index * 16, 16), 16)
+            dn = total[rows, :]
+            x = x_ref[plane, rows, :].astype(F32)
+            inv = inv_ref[plane, rows, :]
+            weighted = gain_ref[...] * dn
+            mean = jnp.mean(weighted * x, axis=1, keepdims=True)
+            grad = (
+                (1.0 - keep_scale) * dy_ref[plane, rows, :].astype(F32)
+                + grad_ref[rows, :]
+                + inv * weighted
+                - x * (inv * inv * inv * mean)
+            )
+            gathered[plane, rows, :] = grad.astype(BF16)
+            gains_all[plane, 1:2, :] += jnp.sum(dn * x * inv, axis=0, keepdims=True)
+            return carry
+
+        lax.fori_loop(0, total.shape[0] // 16, tile, 0)
+
+    return rule
+
+
+def spread_flow(units, outs, scratch, pace):
+    own, plane = lax.axis_index("tok"), lax.axis_index("tp")
+    count = len(units)
+    boxes, inboxes, core_inboxes = scratch[:count], scratch[count : 2 * count], scratch[2 * count : 3 * count]
+    core_send_sem, core_recv_sem, send_sem, recv_sem = scratch[3 * count :]
+    chips = boxes[0].shape[0]
+    bits = [1 << i for i in range(int(math.log2(chips)))]
+    orders = (bits, bits[::-1])
+    stages = len(bits)
+
+    def core_copy(unit, chip):
+        return pltpu.make_async_remote_copy(
+            src_ref=boxes[unit].at[chip],
+            dst_ref=core_inboxes[unit].at[chip],
+            send_sem=core_send_sem.at[unit, chip],
+            recv_sem=core_recv_sem.at[unit, chip],
+            device_id=(own ^ 1, plane),
+            device_id_type=MESH,
+        )
+
+    def active(half, stage):
+        gone = orders[half][:stage]
+        return [chip for chip in range(chips) if all(chip & bit == 0 for bit in gone)]
+
+    def slot(stage, half, chip):
+        before = sum(chips >> (earlier + 1) for earlier in range(stage))
+        return before + active(half, stage + 1).index(chip)
+
+    def copy(unit, half, stage, chip):
+        bit = orders[half][stage]
+        there = slot(stage, half, chip)
+        return pltpu.make_async_remote_copy(
+            src_ref=boxes[unit].at[chip ^ bit, half],
+            dst_ref=inboxes[unit].at[there, half],
+            send_sem=send_sem.at[unit, half, there],
+            recv_sem=recv_sem.at[unit, half, there],
+            device_id=(own ^ (2 * bit), plane),
+            device_id_type=MESH,
+        )
+
+    def offer(unit):
+        def step(chip, carry):
+            for half in range(2):
+                term = units[unit]((own ^ (2 * chip)) ^ 1, half)
+                boxes[unit][chip, half] = term.astype(BF16)
+            core_copy(unit, chip).start()
+            return carry
+
+        lax.fori_loop(0, chips, step, 0)
+
+    def collect(unit):
+        def step(chip, carry):
+            core_copy(unit, chip).wait()
+            for half in range(2):
+                term = units[unit](own ^ (2 * chip), half)
+                term = term + core_inboxes[unit][chip, half].astype(F32)
+                boxes[unit][chip, half] = term.astype(BF16)
+            return carry
+
+        lax.fori_loop(0, chips, step, 0)
+        send(unit, 0)
+
+    def send(unit, stage):
+        for half in range(2):
+            for chip in active(half, stage + 1):
+                copy(unit, half, stage, chip).start()
+
+    def take(unit, stage):
+        for half in range(2):
+            for chip in active(half, stage + 1):
+                copy(unit, half, stage, chip).wait_recv()
+                got = inboxes[unit][slot(stage, half, chip), half].astype(F32)
+                total = boxes[unit][chip, half].astype(F32) + got
+                if stage < stages - 1:
+                    boxes[unit][chip, half] = total.astype(BF16)
+                else:
+                    rows = total.shape[0]
+                    outs[unit][half * rows : (half + 1) * rows, :] = total
+        if stage < stages - 1:
+            send(unit, stage + 1)
+
+    yield 0.1
+    offer(0)
+    for unit in range(count):
+        if unit + 1 < count:
+            yield 1.0 + 2 * unit
+            offer(unit + 1)
+        yield 2.0 + 2 * unit
+        collect(unit)
+    for stage in range(stages):
+        for unit in range(count):
+            yield 6.0 + pace * (unit + 1 + count * stage)
+            take(unit, stage)
+    for unit in range(count):
+        for half in range(2):
+            for stage in range(stages):
+                for chip in active(half, stage + 1):
+                    copy(unit, half, stage, chip).wait_send()
+
+
+def spread_scratch(shapes, devices):
+    chips = devices // 2
+    boxes = [pltpu.VMEM((chips, 2, rows // 2, columns), BF16) for rows, columns in shapes]
+    inboxes = [pltpu.VMEM((chips - 1, 2, rows // 2, columns), BF16) for rows, columns in shapes]
+    return (
+        boxes
+        + inboxes
+        + boxes
+        + [pltpu.SemaphoreType.DMA((len(shapes), chips))] * 2
+        + [pltpu.SemaphoreType.DMA((len(shapes), 2, chips - 1))] * 2
+    )
+
+
+def window(ref, number, size):
+    if size % 128 == 0:
+        return ref[:, pl.ds(pl.multiple_of(number * size, size), size)]
+    parts = 128 // size
+    tile = ref[:, pl.ds(pl.multiple_of(number // parts * 128, 128), 128)].astype(F32)
+    return choose(
+        number % parts, [tile[:, i * size : (i + 1) * size] for i in range(parts)]
+    ).astype(ref.dtype)
+
+
+def rows_by_owner(left_ref, right_ref, rows):
+    def term(owner, half):
+        return lax.dot_general(
+            window(left_ref, owner * 2 + half, rows // 2),
+            right_ref[...],
+            (((0,), (0,)), ((), ())),
+            preferred_element_type=F32,
+        )
+
+    return term
+
+
+def columns_by_owner(left_ref, right_ref, columns):
+    def term(owner, half):
+        rows = left_ref.shape[1] // 2
+        return lax.dot_general(
+            left_ref[:, half * rows : (half + 1) * rows],
+            window(right_ref, owner, columns),
+            (((0,), (0,)), ((), ())),
+            preferred_element_type=F32,
+        )
+
+    return term
+
+
+def ffn_sums_body(
+    part_ref, hidden_ref, inv_ref, dy_ref, gain_ref, normed_ref, dgate_ref, dup_ref, inner_ref, dm_ref,
+    gathered, grad_ref, gains_ref, gate_out, up_out, down_out, *scratch,
+):
+    summing, spreading = scratch[:7], scratch[7:]
+    own, plane = lax.axis_index("tok"), lax.axis_index("tp")
+    devices = lax.axis_size("tok")
+    share = normed_ref.shape[1] // devices
+    chips = devices // 2
+    greet([(own ^ 1, plane)] + [(own ^ (2 << i), plane) for i in range(stages_of("tok") - 1)], True)
+    run(
+        sum_flow(
+            part_ref,
+            gathered,
+            summing,
+            ffn_math(hidden_ref, inv_ref, dy_ref, gain_ref, grad_ref, gains_ref),
+        ),
+        spread_flow(
+            [
+                rows_by_owner(normed_ref, dgate_ref, share),
+                rows_by_owner(normed_ref, dup_ref, share),
+                columns_by_owner(inner_ref, dm_ref, share),
+            ],
+            [gate_out, up_out, down_out],
+            spreading,
+            15.6,
+        ),
+    )
+
+
+def ffn_sums(part, hidden, inv, dy, gain, normed, dgate, dup, inner, dm, collective_id):
+    planes, shard, width = part.shape
+    devices = lax.axis_size("tok")
+    share = width // devices
+    wide = dgate.shape[1]
+    shapes = [(share, wide), (share, wide), (wide, share)]
     return pl.pallas_call(
-        functools.partial(sum_tp_body, math_rule, len(inputs)),
-        out_shape=[jax.ShapeDtypeStruct((planes, shard, width), BF16)] + out_shapes,
-        in_specs=[vmem()] * (1 + len(inputs)),
-        out_specs=[vmem()] * (1 + len(out_shapes)),
-        scratch_shapes=[
-            pltpu.VMEM((shard, width), F32),
-            pltpu.VMEM((2, planes, shard, width), part.dtype),
-            pltpu.VMEM((2, planes, shard, width), part.dtype),
+        ffn_sums_body,
+        out_shape=[
+            jax.ShapeDtypeStruct((planes, shard, width), BF16),
+            jax.ShapeDtypeStruct((shard, width), F32),
+            jax.ShapeDtypeStruct((8, width), F32),
         ]
-        + [pltpu.SemaphoreType.DMA((2, planes))] * 4,
+        + [jax.ShapeDtypeStruct(shape, F32) for shape in shapes],
+        in_specs=[vmem()] * 10,
+        out_specs=[vmem()] * 6,
+        scratch_shapes=sum_scratch(planes, shard, width, BF16) + spread_scratch(shapes, devices),
+        compiler_params=params(collective_id),
+        cost_estimate=cost(0, 80_000_000),
+        name="ffn_sums",
+    )(part, hidden, inv, dy, gain, normed, dgate, dup, inner, dm)
+
+
+def attn_sums_body(
+    lens_ref, flags_ref, part_ref, x_ref, inv_ref, dy_ref, grad_ref, gain_ref, ffn_gains_ref,
+    kept_ref, home_ref, normed_ref, dqkv_ref, attended_ref, da_ref,
+    gathered, gains_ref, mixed_ref, qkv_out, out_out, *scratch,
+):
+    summing, undealing, scratch = scratch[:7], scratch[7:11], scratch[11:]
+    gains_all, gains_sems, spreading = scratch[0], scratch[1:3], scratch[3:]
+    planes = part_ref.shape[0]
+    share = normed_ref.shape[1] // lax.axis_size("tok")
+    greet(bit_peers(stages_of("tok")), True)
+    run(
+        sum_flow(
+            part_ref,
+            gathered,
+            summing,
+            attn_math(x_ref, inv_ref, dy_ref, grad_ref, gain_ref, ffn_gains_ref, gains_all),
+            extra=(gains_all,) + gains_sems,
+        ),
+        undeal_flow(lens_ref, flags_ref, kept_ref, home_ref, mixed_ref, undealing, 7.0),
+        spread_flow(
+            [
+                rows_by_owner(normed_ref, dqkv_ref, share),
+                columns_by_owner(attended_ref, da_ref, share),
+            ],
+            [qkv_out, out_out],
+            spreading,
+            15.0,
+        ),
+    )
+    total = gains_all[0]
+    for index in range(1, planes):
+        total = total + gains_all[index]
+    gains_ref[...] = total
+
+
+def attn_sums(
+    doc_lengths, keep_flags, part, x, inv, dy, grad, gain, ffn_gains, kept, home, normed, dqkv,
+    attended, da, collective_id,
+):
+    planes, shard, width = part.shape
+    devices = lax.axis_size("tok")
+    share = width // devices
+    shapes = [(share, dqkv.shape[1]), (attended.shape[1], share)]
+    return pl.pallas_call(
+        attn_sums_body,
+        out_shape=[
+            jax.ShapeDtypeStruct((planes, shard, width), BF16),
+            jax.ShapeDtypeStruct((8, width), F32),
+            jax.ShapeDtypeStruct(home.shape, BF16),
+        ]
+        + [jax.ShapeDtypeStruct(shape, F32) for shape in shapes],
+        in_specs=[smem(), smem()] + [vmem()] * 13,
+        out_specs=[vmem()] * 5,
+        scratch_shapes=sum_scratch(planes, shard, width, BF16)
+        + undeal_scratch(stages_of("tok"), width, BF16)
+        + [pltpu.VMEM((planes, 8, width), F32)]
+        + line_sems(planes)
+        + spread_scratch(shapes, devices),
+        compiler_params=params(collective_id),
+        cost_estimate=cost(0, 80_000_000),
+        name="attn_sums",
+    )(
+        doc_lengths, keep_flags, part, x, inv, dy, grad, gain, ffn_gains, kept, home, normed, dqkv,
+        attended, da,
+    )
+
+
+def mixed_sum_body(part_ref, hidden_ref, x_ref, gathered, *scratch):
+    greet([], True)
+    run(sum_flow(part_ref, gathered, scratch, mixed_math(hidden_ref, x_ref)))
+
+
+def mixed_sum(part, hidden, x, collective_id):
+    planes, shard, width = part.shape
+    return pl.pallas_call(
+        mixed_sum_body,
+        out_shape=jax.ShapeDtypeStruct((planes, shard, width), BF16),
+        in_specs=[vmem()] * 3,
+        out_specs=vmem(),
+        scratch_shapes=sum_scratch(planes, shard, width, BF16),
         compiler_params=params(collective_id),
         cost_estimate=cost(0, 60_000_000),
-        name=name,
-    )(part, *inputs)
+        name="mixed_sum",
+    )(part, hidden, x)
 
 
 def swap(values, bit):
     devices = lax.axis_size("tok")
     return lax.ppermute(values, "tok", [(i, i ^ bit) for i in range(devices)])
-
-
-def pick(values, index):
-    return lax.dynamic_index_in_dim(values, index, 0, keepdims=False)
-
-
-def halve(values, bits, own):
-    for position, bit in enumerate(bits):
-        side = (own // bit) % 2
-        shape = values.shape
-        lead = 2 ** (len(bits) - position - 1)
-        values = values.reshape((2, lead) + shape[1:])
-        got = swap(pick(values, 1 - side), bit)
-        summed = pick(values, side).astype(F32) + got.astype(F32)
-        values = summed if position == len(bits) - 1 else summed.astype(BF16)
-    return values[0]
-
-
-def scatter_weights(grad):
-    devices = lax.axis_size("tok")
-    own = lax.axis_index("tok")
-    stages = stages_of("tok")
-    rows, columns = grad.shape
-    share = rows // devices
-    grad = grad.reshape(devices // 2, 2, share, columns)
-    core = own % 2
-    mine = lax.dynamic_index_in_dim(grad, core, 1, keepdims=False)
-    other = lax.dynamic_index_in_dim(grad, 1 - core, 1, keepdims=False)
-    both = (mine.astype(F32) + swap(other, 1).astype(F32)).astype(BF16)
-    bits = [1 << stage for stage in range(stages - 1, 0, -1)]
-    upper, lower = both[:, : share // 2], both[:, share // 2 :]
-    sides = len(bits)
-    flipped = lower.reshape((2,) * sides + lower.shape[1:])
-    flipped = flipped.transpose(tuple(range(sides - 1, -1, -1)) + (sides, sides + 1))
-    flipped = flipped.reshape(lower.shape)
-    return jnp.concatenate([halve(upper, bits, own), halve(flipped, bits[::-1], own)], axis=0)
 
 
 def document_tables(doc_lengths, places):
@@ -809,10 +1066,10 @@
     )
 
 
-def over_rows(left, right, kind=F32):
+def over_rows(left, right):
     return lax.dot_general(
         left, right, (((0,), (0,)), ((), ())), preferred_element_type=jnp.float32
-    ).astype(kind)
+    )
 
 
 def over_columns(left, right):
@@ -856,7 +1113,6 @@
     first_core = own_index % 2 == 0
 
     rows_x = deal(doc_lengths, keep_flags, token_blocks, 0).reshape(rows, model_width)
-    rows_dy = deal(doc_lengths, keep_flags, grad_blocks, 1).reshape(rows, model_width)
 
     block_starts = jnp.arange(total_blocks, dtype=jnp.int32) * BLOCK
     block_docs, block_pos, block_member = document_tables(doc_lengths, block_starts)
@@ -931,7 +1187,8 @@
     head_outs, peaks, totals = lax.map(head_forward, (query_heads, slot_of_head))
     attended = head_outs.transpose(1, 0, 2).reshape(rows, heads_here * HD).astype(jnp.bfloat16)
 
-    attended_all = gather_tp(attended, 3)
+    rows_dy, attended_all = deal_gather(doc_lengths, keep_flags, grad_blocks, attended, 1)
+    rows_dy = rows_dy.reshape(rows, model_width)
     attended_all = attended_all.transpose(1, 0, 2).reshape(rows, planes * heads_here * HD)
     mine = jnp.dot(attended_all, out_half, preferred_element_type=jnp.float32)
     other = jnp.dot(attended_all, out_other, preferred_element_type=jnp.float32)
@@ -959,22 +1216,20 @@
     by_plane = lambda array: array.reshape(planes, shard, array.shape[1])
     x_planes, dy_planes = by_plane(rows_x), by_plane(rows_dy)
     hidden_planes = by_plane(hidden_res)
-    grad_a, grad_hidden, gains_ffn = sum_tp(
-        ffn_math,
-        part_two,
-        (hidden_planes, by_plane(inv_two), dy_planes, gain_ffn.reshape(1, -1)),
-        [
-            jax.ShapeDtypeStruct((shard, model_width), F32),
-            jax.ShapeDtypeStruct((8, model_width), F32),
-        ],
+    grad_a, grad_hidden, gains_ffn, grad_gate, grad_up, grad_down = ffn_sums(
+        by_plane(part_two),
+        hidden_planes,
+        by_plane(inv_two),
+        dy_planes,
+        gain_ffn.reshape(1, -1),
+        normed_two,
+        grad_gate_pre,
+        grad_up_pre,
+        inner,
+        grad_m,
         4,
-        "sum_ffn",
     )
     grad_a = grad_a.reshape(rows, model_width)
-
-    grad_gate = scatter_weights(over_rows(normed_two, grad_gate_pre, BF16))
-    grad_up = scatter_weights(over_rows(normed_two, grad_up_pre, BF16))
-    grad_down = scatter_weights(over_rows(grad_m, inner, BF16)).T
 
     grad_attended = over_columns(grad_a, w_out).astype(jnp.bfloat16)
     grad_heads = grad_attended.reshape(rows, heads_here, HD).transpose(1, 0, 2)
@@ -1030,31 +1285,29 @@
         + over_columns(grad_key_pre, w_key)
         + over_columns(grad_value_pre, w_value)
     ).astype(jnp.bfloat16)
-    grad_rows, gains = sum_tp(
-        attn_math,
-        part_one,
-        (x_planes, by_plane(inv_one), dy_planes, grad_hidden, gain_attn.reshape(1, -1), gains_ffn),
-        [jax.ShapeDtypeStruct((8, model_width), F32)],
-        6,
-        "sum_attn",
-    )
-    gains = lax.psum(gains, "tp")
-
-    mixed_rows = sum_tp(
-        mixed_math,
-        jnp.dot(inner, w_down, preferred_element_type=jnp.float32).astype(jnp.bfloat16),
-        (hidden_planes, x_planes),
-        [],
+    mixed_rows = mixed_sum(
+        by_plane(jnp.dot(inner, w_down, preferred_element_type=jnp.float32).astype(jnp.bfloat16)),
+        hidden_planes,
+        x_planes,
         7,
-        "sum_mixed",
-    )[0]
-    mixed, _ = undeal(
+    )
+    grad_rows, gains, mixed, grad_qkv, grad_out = attn_sums(
         doc_lengths,
         keep_flags,
+        by_plane(part_one),
+        x_planes,
+        by_plane(inv_one),
+        dy_planes,
+        grad_hidden,
+        gain_attn.reshape(1, -1),
+        gains_ffn,
         mixed_rows.reshape(kept_here, BLOCK, model_width),
         token_blocks,
-        gains_ffn,
-        8,
+        normed_one,
+        jnp.concatenate([grad_query_pre, grad_key_pre, grad_value_pre], axis=1),
+        attended,
+        grad_a,
+        6,
     )
     token_grad, gain_sums = undeal(
         doc_lengths,
@@ -1067,22 +1320,10 @@
     own_share = model_width // devices
     if gain_sums.shape[1] != own_share:
         gain_sums = lax.dynamic_slice_in_dim(gain_sums, own_index * own_share, own_share, 1)
-
-    attn_grads = jnp.concatenate(
-        [
-            over_rows(normed_one, grad_query_pre, BF16),
-            over_rows(normed_one, grad_key_pre, BF16),
-            over_rows(normed_one, grad_value_pre, BF16),
-            over_rows(grad_a, attended, BF16),
-        ],
-        axis=1,
-    )
-    attn_grads = scatter_weights(attn_grads)
     wide, thin = w_query.shape[1], w_key.shape[1]
-    grad_query = attn_grads[:, :wide]
-    grad_key = attn_grads[:, wide : wide + thin]
-    grad_value = attn_grads[:, wide + thin : wide + 2 * thin]
-    grad_out = attn_grads[:, wide + 2 * thin :].T
+    grad_query = grad_qkv[:, :wide]
+    grad_key = grad_qkv[:, wide : wide + thin]
+    grad_value = grad_qkv[:, wide + thin :]
 
     return (
         mixed.reshape(length, model_width),

time: 869 us -> 649 us (0.75)
  waiting for transfers between devices: 66.9 us -> 0.02 us
  local copies, waits for them, and re-layouts: 118 us -> 62 us
  other arithmetic: 68.9 us -> 38.7 us
  matrix products: 131 us -> 104 us
  Pallas kernels: 440 us -> 423 us
  starting transfers between devices: 15.8 us -> 0.18 us
    pallas_call x4, Pallas kernels: 203 us -> 292 us  [the longest x1 95.8 us: attn_sums(): pl.pallas_call(attn_sums_body, out_shape=[jax.ShapeDtypeStruct((planes, s...]
    pallas_call x2 -> x1, Pallas kernels: 105 us -> 49.7 us  [undeal(): pl.pallas_call(undeal_body, out_shape=(jax.ShapeDtypeStruct(home.shape, h...]
    ppermute x21 -> x1, waiting for transfers between devices: 53.2 us -> 0.01 us  [swap(): return lax.ppermute(values, 'tok', [(i, i ^ bit) for i in range(devices)])]
    pallas_call x2 -> x1, Pallas kernels: 97 us -> 49.5 us  [deal(): pl.pallas_call(deal_body, out_shape=jax.ShapeDtypeStruct((SLOTS, BLOCK, w...]
    unnamed x137 -> x107, local copies, waits for them, and re-layouts: 36.6 us -> 12.2 us
    dot_general x15 -> x8, matrix products: 45.5 us -> 25.5 us  [over_rows(): lax.dot_general(left, right, (((0,), (0,)), ((), ())), preferred_element_...]
    ppermute x21 -> x1, starting transfers between devices: 15.7 us -> 0.14 us  [swap(): return lax.ppermute(values, 'tok', [(i, i ^ bit) for i in range(devices)])]
    squeeze x19 -> x0, local copies, waits for them, and re-layouts: 15.5 us -> none  [the longest x3 9.21 us: scatter_weights(): other = lax.dynamic_index_in_dim(grad, 1 - core, 1, keepdims=False)]
  transfers between devices with their start and end apart: 23 -> 2, of which waited for: 9 -> 0; matrix products, arithmetic and copies ran while one was open for 14% -> 10% of each run, Pallas kernels for 43% -> 18%
where the time goes in v2:
time: 649 us; the launch traced here: 644 us
  Pallas kernels  423 us (65%)
  matrix products  104 us (16%)
  local copies, waits for them, and re-layouts  62 us (10%)
  other arithmetic  38.7 us (6%)
  between operations  15.4 us (2%)
    pallas_call x1, Pallas kernels, attn_sums(): pl.pallas_call(attn_sums_body, out_shape=[jax.ShapeDtypeStruct((planes, s...  95.8 us
    pallas_call x1, Pallas kernels, ffn_sums(): pl.pallas_call(ffn_sums_body, out_shape=[jax.ShapeDtypeStruct((planes, sh...  87.8 us
    pallas_call x1, Pallas kernels, mixed_sum(): pl.pallas_call(mixed_sum_body, out_shape=jax.ShapeDtypeStruct((planes, sh...  58.6 us
    pallas_call x1, Pallas kernels, undeal(): pl.pallas_call(undeal_body, out_shape=(jax.ShapeDtypeStruct(home.shape, h...  49.7 us
    pallas_call x1, Pallas kernels, deal(): pl.pallas_call(deal_body, out_shape=jax.ShapeDtypeStruct((SLOTS, BLOCK, w...  49.5 us
    pallas_call x1, Pallas kernels, deal_gather(): pl.pallas_call(deal_gather_body, out_shape=(jax.ShapeDtypeStruct((SLOTS,...  49.4 us
    dot_general x8, matrix products, over_rows(): lax.dot_general(left, right, (((0,), (0,)), ((), ())), preferred_element_...  25.5 us
    dot_general x8, matrix products, head_scores(): jnp.einsum('qd,kd->qk', query, keys_one, preferred_element_type=jnp.float32)  21.8 us
  transfers between devices with their start and end apart: 2, of which 0 were waited for; matrix products, arithmetic and copies ran while one was open for 10% of the time, Pallas kernels for 18%

profile of v2, /device:TPU:1, one launch (start us, length us, event | category | flops | bytes accessed | tf_op | source)
XLA Modules:
  0.0 643.6 jit_solution(163295769974563958)
XLA Ops:
  12.3 49.5 %deal.1 = bf16[3,128,2048]{2,1,0:T(8,128)(2,1)} custom-call(s32[6]{0:T(128)} %lens_ref.7, s32[6]{0:T(128)} %flags_ref.7, bf16[6,128,2048]{2,1,0:T(8,128)(2,1)} %bitcast.212), custom_call_target="tpu_custom_call" | custom-call | bytes 40000000 | tf_op jit(solution)/shard_map/deal/pallas_call | solution.py:220
  64.6 1.9 fusion.41
  69.8 16.2 %gather_tok.1 = bf16[8,384,256]{2,1,0:T(8,128)(2,1)} custom-call(bf16[384,256]{1,0:T(8,128)(2,1)} %pad_maximum_fusion.3.mine_ref), custom_call_target="tpu_custom_call" | custom-call | bytes 10000000 | tf_op jit(solution)/shard_map/gather_tok/pallas_call | solution.py:431
  86.0 3.5 reshape.535
  89.5 3.9 copy.68
  93.9 2.1 fusion.43
  98.5 4.6 fusion.74
  104.3 21.1 %while.32 = (s32[]{:T(128)}, bf16[4,384,128]{2,1,0:T(8,128)(2,1)}, f32[4,384,1]{1,2,0:T(1,128)}, f32[4,384,1]{1,2,0:T(1,128)}, bf16[4,384,128]{2,1,0:T(8,128)(2,...) while((s32[]{:T(128)}, bf16[4,384,128]{2,1,0:T(8,128)(2,1)}, ...), condition=%wide.region_12.13_spmd.clone, body=%wide.region_9.12_spmd.clone.sunk | while | flops 616955136 | bytes 19211968 | solution.py:1187
  104.3 2.5 fusion.135
  109.5 2.5 fusion.135
  114.8 2.5 fusion.135
  120.1 2.5 fusion.135
  126.3 1.8 copy_bitcast_fusion.2.mine_ref.attended_ref
  128.0 49.4 %deal_gather.1 = (bf16[3,128,2048]{2,1,0:T(8,128)(2,1)}, bf16[4,384,512]{2,1,0:T(8,128)(2,1)}) custom-call(s32[6]{0:T(128)} %lens_ref.7, s32[6]{0:T(128)} %flags_ref.7, bf16[6,128,2048]{2,1,0:T(8,128)(2,1)} %bitcast.214, bf16[384,512]{1,0:T(8,128)(2,1)} %copy_bitcast_fusion.2.mine_ref.attended_ref), custom_call_target="tpu_custom_call" | custom-call | bytes 40000000 | tf_op jit(solution)/shard_map/deal_gather/pallas_call | solution.py:246
  177.5 2.6 copy.59
  180.0 1.7 multiply_convert_fusion.1
  181.8 7.2 %fusion.80 = f32[384,1408]{1,0:T(8,128)} fusion(bf16[384,2048]{1,0:T(8,128)(2,1)S(1)} %bitcast.219, bf16[1408,2048]{1,0:T(8,128)(2,1)} %param.26), kind=kOutput, calls=%fused_computation.163 | convolution fusion | flops 2214592512 | bytes 9502720 | tf_op jit(solution)/shard_map/dot_general | solution.py:1076
  189.0 1.8 fusion.81
  190.9 4.1 broadcast_select_fusion.1
  197.6 3.0 fusion.38.normed_ref
  200.6 5.8 fusion.82
  206.5 3.3 multiply_convert_fusion.2
  209.9 3.9 convolution_convert_fusion
  213.9 2.6 fusion.83
  216.6 3.8 add_convert_fusion.1
  220.4 2.1 maximum_add_fusion.2.hidden_ref
  222.5 87.8 %ffn_sums.1 = (bf16[4,96,2048]{2,1,0:T(8,128)(2,1)}, f32[96,2048]{1,0:T(8,128)}, f32[8,2048]{1,0:T(8,128)}, f32[256,1408]{1,0:T(8,128)}, f32[256,1408]{1,0:T(8,128)}, /*index=5*/f32[1408,256]{1,0:T(8,128)}) custom-call(bf16[4,96,2048]{2,1,0:T(8,128)(2,1)} %bitcast.234, f32[4,96,2048]{2,1,0:T(8,128)} %maximum_add_fusion.2.hidden_ref, ...), custom_call_target="tpu_custom_call" | custom-call | bytes 80000000 | tf_op jit(solution)/shard_map/ffn_sums/pallas_call | solution.py:923
  310.3 2.4 fusion.47
  313.5 67.2 %while.33 = (s32[]{:T(128)}, f32[4,384,128]{1,2,0:T(8,128)}, f32[4,3072,128]{2,1,0:T(8,128)}, f32[4,3072,128]{2,1,0:T(8,128)}, bf16[4,384,128]{2,1,0:T(8,128)(2,...) while((s32[]{:T(128)}, f32[4,384,128]{1,2,0:T(8,128)}, ...), condition=%wide.region_16.17_spmd.clone, body=%wide.region_14.16_spmd.clone.sunk | while | flops 1525726848 | bytes 67479824 | solution.py:1254
  314.2 1.7 fusion.146
  316.0 2.9 multiply_reduce_fusion.2
  318.9 2.2 copy-done.2
  323.9 4.4 fusion.150
  328.3 2.0 fusion.149
  331.0 1.7 fusion.146
  332.7 2.9 multiply_reduce_fusion.2
  335.7 2.2 copy-done.2
  340.7 4.4 fusion.150
  345.1 2.0 fusion.149
  347.8 1.7 fusion.146
  349.5 2.9 multiply_reduce_fusion.2
  352.5 2.2 copy-done.2
  357.5 4.4 fusion.150
  361.9 2.0 fusion.149
  364.6 1.7 fusion.146
  366.3 2.9 multiply_reduce_fusion.2
  369.3 2.2 copy-done.2
  374.3 4.4 fusion.150
  378.7 2.0 fusion.149
  380.7 3.2 reduce_sum.119
  383.9 3.3 reduce_sum.118
  388.5 15.8 %scatter_tok.1 = f32[384,256]{1,0:T(8,128)} custom-call(bf16[8,384,256]{2,1,0:T(8,128)(2,1)} %pad_maximum_fusion.part_ref), custom_call_target="tpu_custom_call" | custom-call | bytes 10000000 | tf_op jit(solution)/shard_map/scatter_tok/pallas_call | solution.py:497
  404.4 1.6 slice.110
  406.9 1.5 fusion.77
  408.4 58.6 %mixed_sum.1 = bf16[4,96,2048]{2,1,0:T(8,128)(2,1)} custom-call(bf16[4,96,2048]{2,1,0:T(8,128)(2,1)} %bitcast.233, f32[4,96,2048]{2,1,0:T(8,128)} %maximum_add_fusion.2.hidden_ref, bf16[4,96,2048]{2,1,0:T(8,128)(2,1)} %bitcast.201), custom_call_target="tpu_custom_call" | custom-call | bytes 60000000 | tf_op jit(solution)/shard_map/mixed_sum/pallas_call | solution.py:1014
  468.3 1.5 fusion.61
  471.9 1.8 fusion.84
  474.6 2.2 add_convert_fusion
  476.8 95.8 %attn_sums.1 = (bf16[4,96,2048]{2,1,0:T(8,128)(2,1)}, f32[8,2048]{1,0:T(8,128)}, bf16[6,128,2048]{2,1,0:T(8,128)(2,1)}, f32[256,768]{1,0:T(8,128)}, f32[512,256]{1,0:T(8,128)}) custom-call(s32[6]{0:T(128)} %lens_ref.7, s32[6]{0:T(128)} %flags_ref.7, bf16[4,96,2048]{2,1,0:T(8,128)(2,1)} %bitcast.217, bf16[4,96,2048]{2,1,0:T(8,128)(2,1)} %bitcast.202, ...), custom_call_target="tpu_custom_call" | custom-call | bytes 80000000 | tf_op jit(solution)/shard_map/attn_sums/pallas_call | solution.py:983
  572.5 1.7 fusion.75
  574.2 1.9 slice.65
  576.1 49.7 %undeal.1 = (bf16[6,128,2048]{2,1,0:T(8,128)(2,1)}, f32[8,256]{1,0:T(8,128)}) custom-call(s32[6]{0:T(128)} %lens_ref.7, s32[6]{0:T(128)} %flags_ref.7, bf16[3,128,2048]{2,1,0:T(8,128)(2,1)} %bitcast.231, bf16[6,128,2048]{2,1,0:T(8,128)(2,1)} %bitcast.215, f32[8,2048]{1,0:T(8,128)} %get-tuple-element.188.gains_ref), custom_call_target="tpu_custom_call" | custom-call | bytes 40000000 | tf_op jit(solution)/shard_map/undeal/pallas_call | solution.py:367
  627.2 1.7 copy.125
  630.2 1.7 copy.126
  (250 shorter events, 58.0 us)
Async XLA Ops:
  7.2 2.7 copy-start.43
  7.2 3.0 copy-start.45
  7.2 96.9 %all-gather.2.cloned.1.call-start = ((), (), s32[]{:S(2)}) async-start(), calls=%async_computation | async-start | bytes 5242880 | tf_op jit(solution)/shard_map/all_gather | solution.py:1111
  10.8 82.6 %copy-start.46 = (f32[64]{0:T(128)}, f32[64]{0:T(128)S(1)}, u32[]{:S(2)}) copy-start(f32[64]{0:T(128)S(1)} %multiply_exponential_fusion) | copy-start | bytes 772
  12.3 51.5 %copy-start.44 = (s32[6]{0:T(128)S(1)}, s32[6]{0:T(128)}, u32[]{:S(2)}) copy-start(s32[6]{0:T(128)} %lens_ref.7) | copy-start | bytes 76
  12.3 54.2 %copy-start.39 = (f32[2048]{0:T(1024)S(1)}, f32[2048]{0:T(1024)}, u32[]{:S(2)}) copy-start(f32[2048]{0:T(1024)} %param.18) | copy-start | bytes 24580
  61.8 4.7 copy-start.3
  64.6 2.3 copy-start.19
  66.5 2.0 copy-start.20
  66.9 2.1 copy-start.7
  67.6 25.9 %copy-start.40 = (f32[384]{0:T(512)}, f32[384]{0:T(512)S(1)}, u32[]{:S(2)}) copy-start(f32[384]{0:T(512)S(1)} %subtract_convert_fusion.2) | copy-start | bytes 4612
  93.4 2.5 copy-start.18
  93.9 3.4 copy-start.31
  93.9 3.4 copy-start.33
  104.1 86.7 %collective-permute-start = (bf16[2048,1024]{1,0:T(8,128)(2,1)}, bf16[2048,1024]{1,0:T(8,128)(2,1)}, u32[]{:S(2)}, u32[]{:S(2)}) collective-permute-start(bf16[2048,1024]{1,0:T(8,128)(2,1)} %all-gather.2.cloned.1.call-done), channel_id=1, source_target_pairs={{0,4},{4,0},{8,12},{12,8},{16,20},{20,16},{24,28},{28,24},{1,5},{5... | collective-permute-start | bytes 12582920 | tf_op jit(solution)/shard_map/ppermute | solution.py:1028
  181.8 7.2 %copy-start.14 = (bf16[3,128,2048]{2,1,0:T(8,128)(2,1)}, bf16[3,128,2048]{2,1,0:T(8,128)(2,1)S(1)}, u32[]{:S(2)}) copy-start(bf16[3,128,2048]{2,1,0:T(8,128)(2,1)S(1)} %multiply_convert_fusion.1) | copy-start | bytes 4718596
  181.8 7.2 %copy-start.12 = (bf16[384,4,512]{0,2,1:T(8,128)(2,1)S(1)}, bf16[384,4,512]{0,2,1:T(8,128)(2,1)}, u32[]{:S(2)}) copy-start(bf16[384,4,512]{0,2,1:T(8,128)(2,1)} %copy.59) | copy-start | bytes 4718596
  181.8 7.2 %copy-start.48 = (bf16[2048,1024]{1,0:T(8,128)(2,1)S(1)}, bf16[2048,1024]{1,0:T(8,128)(2,1)}, u32[]{:S(2)}) copy-start(bf16[2048,1024]{1,0:T(8,128)(2,1)} %all-gather.2.cloned.1.call-done) | copy-start | bytes 12582916
  190.8 4.2 copy-start.4
  195.0 2.5 copy-start.42
  197.6 8.9 %slice-start.4 = ((s8[5767168]{0:T(1024)(128)(4,1)}), s8[4194304]{0:T(1024)(128)(4,1)S(1)}, s32[]{:S(2)}) async-start(s8[5767168]{0:T(1024)(128)(4,1)} %bitcast.249), calls=%async_computation.5 | async-start | bytes 8388608
  200.6 5.9 copy-start.15
  200.6 5.9 slice-start.5
  200.6 5.9 copy-start.49
  200.6 9.3 %slice-start = ((s8[5767168]{0:T(1024)(128)(4,1)}), s8[4194304]{0:T(1024)(128)(4,1)S(1)}, s32[]{:S(2)}) async-start(s8[5767168]{0:T(1024)(128)(4,1)} %bitcast.245), calls=%async_computation.1 | async-start | bytes 8388608
  200.6 13.3 %slice-start.2 = ((s8[5767168]{0:T(1024)(128)(4,1)}), s8[4194304]{0:T(1024)(128)(4,1)S(1)}, s32[]{:S(2)}) async-start(s8[5767168]{0:T(1024)(128)(4,1)} %bitcast.247), calls=%async_computation.3 | async-start | bytes 8388608
  206.5 3.4 slice-start.1
  206.5 7.4 %slice-start.3 = ((s8[5767168]{0:T(1024)(128)(4,1)}), s8[1572864]{0:T(1024)(128)(4,1)S(1)}, s32[]{:S(2)}) async-start(s8[5767168]{0:T(1024)(128)(4,1)} %bitcast.247), calls=%async_computation.4 | async-start | bytes 3145728
  209.8 4.0 copy-start.28
  209.8 4.0 copy-start.29
  209.9 6.7 %copy-start.30 = (bf16[384,1408]{1,0:T(8,128)(2,1)}, bf16[384,1408]{1,0:T(8,128)(2,1)S(1)}, u32[]{:S(2)}) copy-start(bf16[384,1408]{1,0:T(8,128)(2,1)S(1)} %get-tuple-element.393.dup_ref) | copy-start | bytes 3244036
  216.5 3.8 copy-start.5
  216.6 3.8 copy-start.9
  216.6 3.8 copy-start.11
  313.5 2.4 copy-start.22
  314.2 1.8 copy-start.6
  318.9 2.2 copy-start.2
  323.9 4.4 copy-start.23
  330.3 2.5 copy-start.22
  331.0 1.8 copy-start.6
  335.7 2.2 copy-start.2
  340.7 4.4 copy-start.23
  347.1 2.5 copy-start.22
  347.8 1.8 copy-start.6
  352.5 2.2 copy-start.2
  357.5 4.4 copy-start.23
  363.9 2.5 copy-start.22
  364.6 1.8 copy-start.6
  369.3 2.2 copy-start.2
  374.3 4.4 copy-start.23
  387.2 19.7 %copy-start.21 = (bf16[2048,128]{1,0:T(8,128)(2,1)S(1)}, bf16[2048,128]{1,0:T(8,128)(2,1)}, u32[]{:S(2)}) copy-start(bf16[2048,128]{1,0:T(8,128)(2,1)} %param.21) | copy-start | bytes 1572868
  408.4 58.7 %copy-start.32 = (f32[384,64]{0,1:T(8,128)S(1)}, f32[384,64]{0,1:T(8,128)}, u32[]{:S(2)}) copy-start(f32[384,64]{0,1:T(8,128)} %copy-done.31) | copy-start | bytes 294916
  408.4 58.7 %copy-start.34 = (f32[384,64]{0,1:T(8,128)S(1)}, f32[384,64]{0,1:T(8,128)}, u32[]{:S(2)}) copy-start(f32[384,64]{0,1:T(8,128)} %copy-done.33) | copy-start | bytes 294916
  408.4 59.9 %copy-start.41 = (f32[384]{0:T(512)S(1)}, f32[384]{0:T(512)}, u32[]{:S(2)}) copy-start(f32[384]{0:T(512)} %copy-done.40) | copy-start | bytes 4612
  408.4 59.9 %copy-start.47 = (f32[64]{0:T(128)S(1)}, f32[64]{0:T(128)}, u32[]{:S(2)}) copy-start(f32[64]{0:T(128)} %copy-done.46) | copy-start | bytes 772
  470.8 2.9 copy-start.24
  470.8 2.9 copy-start.38
  471.9 2.7 copy-start.13
  576.1 51.1 %copy-start.16 = (bf16[6,128,2048]{2,1,0:T(8,128)(2,1)S(1)}, bf16[6,128,2048]{2,1,0:T(8,128)(2,1)}, u32[]{:S(2)}) copy-start(bf16[6,128,2048]{2,1,0:T(8,128)(2,1)} %get-tuple-element.186) | copy-start | bytes 9437188
  627.2 3.0 copy-start.17
  630.2 2.8 copy-start.27
  631.9 2.2 copy-start.26
  633.0 2.2 copy-start.25
  633.0 3.3 copy-start.1
  (12 other events, 13.1 us)
Sparse Core Ops, SparseCore 0:
  10.2 82.8 all-gather.1

commit v3 on v2

v3 whole, which is shorter than its diff:
```python
import functools
import math

import jax
import jax.numpy as jnp
from jax import lax
from jax.experimental import pallas as pl
from jax.experimental.pallas import tpu as pltpu
from jax.sharding import PartitionSpec as P

HD = 128
BLOCK = 128
SLOTS = 3
CHUNKS = 8
HALVES = 2
MESH = pl.DeviceIdType.MESH
VMEM_BYTES = 60 * 2**20

norm_eps = 1e-05
keep_scale = 2.0
F32 = jnp.float32
BF16 = jnp.bfloat16


def vmem():
    return pl.BlockSpec(memory_space=pltpu.VMEM)


def smem():
    return pl.BlockSpec(memory_space=pltpu.SMEM)


def params(collective_id):
    return pltpu.CompilerParams(
        collective_id=collective_id, has_side_effects=True, vmem_limit_bytes=VMEM_BYTES
    )


def cost(flops, moved):
    return pl.CostEstimate(flops=flops, bytes_accessed=moved, transcendentals=0)


def greet(peers, line=False):
    barrier = pltpu.get_barrier_semaphore()
    for peer in peers:
        pl.semaphore_signal(barrier, inc=1, device_id=peer, device_id_type=MESH)
    if not line:
        pl.semaphore_wait(barrier, len(peers))
        return
    own, plane = lax.axis_index("tok"), lax.axis_index("tp")
    last = lax.axis_size("tp") - 1

    @pl.when(plane > 0)
    def _():
        pl.semaphore_signal(barrier, inc=1, device_id=(own, plane - 1), device_id_type=MESH)

    @pl.when(plane < last)
    def _():
        pl.semaphore_signal(barrier, inc=1, device_id=(own, plane + 1), device_id_type=MESH)

    end = (plane == 0) | (plane == last)

    @pl.when(end)
    def _():
        pl.semaphore_wait(barrier, len(peers) + 1)

    @pl.when(jnp.logical_not(end))
    def _():
        pl.semaphore_wait(barrier, len(peers) + 2)


def run(*flows):
    waiting = [[next(flow), number, flow] for number, flow in enumerate(flows)]
    while waiting:
        waiting.sort(key=lambda entry: entry[:2])
        entry = waiting[0]
        try:
            entry[0] = next(entry[2])
        except StopIteration:
            waiting.pop(0)


def deal_tables(own, stages, blocks_here, lens_ref, flags_ref):
    def kept_before(place):
        total, start = jnp.int32(0), jnp.int32(0)
        for doc in range(lens_ref.shape[0]):
            blocks = lens_ref[doc] // BLOCK
            total = total + flags_ref[doc] * jnp.clip(place - start, 0, blocks)
            start = start + blocks
        return total

    def edges(stage):
        first = (own >> stage) << stage
        return (
            kept_before(first * blocks_here),
            kept_before((first + (1 << stage)) * blocks_here),
        )

    def located(stage):
        if stage == 0:
            ends = [kept_before(own * blocks_here + i + 1) for i in range(blocks_here)]

            def place(rank):
                index = jnp.int32(0)
                for end in ends:
                    index = index + (end <= rank).astype(jnp.int32)
                return index

            return place
        mine = (own >> (stage - 1)) << (stage - 1)
        low, high = edges(stage - 1)
        other = kept_before((mine ^ (1 << (stage - 1))) * blocks_here)

        def place(rank):
            inside = (rank >= low) & (rank < high)
            return jnp.where(inside, (rank - low) >> stage, SLOTS + ((rank - other) >> stage))

        return place

    keeps, sends = [], []
    for stage in range(stages):
        low, high = edges(stage)
        place = located(stage)
        period = 1 << (stage + 1)
        for table, target in ((keeps, own), (sends, own ^ (1 << stage))):
            first = low + ((target - low) & (period - 1))
            row = []
            for slot in range(SLOTS):
                rank = first + period * slot
                row.append(jnp.where(rank < high, place(rank), -1))
            table.append(row)
    place = located(stages)
    finals = [place(own + (slot << stages)) for slot in range(SLOTS)]
    return keeps, sends, finals


def choose(index, options, default=None):
    value = options[0] if default is None else default
    for number, option in enumerate(options):
        if number == 0 and default is None:
            continue
        value = jnp.where(index == number, option, value)
    return value


def bit_peers(stages):
    own, plane = lax.axis_index("tok"), lax.axis_index("tp")
    return [(own ^ (1 << stage), plane) for stage in range(stages)]


def deal_flow(lens_ref, flags_ref, own_ref, out_ref, scratch, pace=4.3):
    keep, send, recv, send_sem, recv_sem = scratch
    stages = send.shape[0]
    own = lax.axis_index("tok")
    blocks_here = own_ref.shape[0]
    rows = BLOCK // CHUNKS
    peers = bit_peers(stages)
    keeps, sends, finals = deal_tables(own, stages, blocks_here, lens_ref, flags_ref)

    def copy(stage, chunk):
        return pltpu.make_async_remote_copy(
            src_ref=send.at[stage, chunk],
            dst_ref=recv.at[stage, chunk],
            send_sem=send_sem.at[stage, chunk],
            recv_sem=recv_sem.at[stage, chunk],
            device_id=peers[stage],
            device_id_type=MESH,
        )

    def held(stage, chunk):
        if stage == 0:
            return [own_ref[i, pl.ds(chunk * rows, rows), :] for i in range(blocks_here)]
        return [keep[chunk, i] for i in range(SLOTS)] + [
            recv[stage - 1, chunk, i] for i in range(SLOTS)
        ]

    for stage in range(stages + 1):
        for chunk in range(CHUNKS):
            yield 0.0 if stage == 0 else 1 + 0.4 * chunk + pace * (stage - 1) * (chunk + 1)
            if stage > 0:
                copy(stage - 1, chunk).wait_recv()
            options = held(stage, chunk)
            if stage == stages:
                for slot in range(SLOTS):
                    out_ref[slot, pl.ds(chunk * rows, rows), :] = choose(finals[slot], options)
            else:
                for slot in range(SLOTS):
                    send[stage, chunk, slot] = choose(sends[stage][slot], options)
                copy(stage, chunk).start()
                for slot in range(SLOTS):
                    keep[chunk, slot] = choose(keeps[stage][slot], options)
    yield 1e6

    def drain(chunk, carry):
        for stage in range(stages):
            copy(stage, chunk).wait_send()
        return carry

    lax.fori_loop(0, CHUNKS, drain, 0)


def deal_scratch(stages, width, kind):
    moved = (CHUNKS, SLOTS, BLOCK // CHUNKS, width)
    return (
        [pltpu.VMEM(moved, kind)]
        + [pltpu.VMEM((stages,) + moved, kind)] * 2
        + [pltpu.SemaphoreType.DMA((stages, CHUNKS))] * 2
    )


def stages_of(axis):
    return int(math.log2(lax.axis_size(axis)))


def deal_body(lens_ref, flags_ref, own_ref, out_ref, *scratch):
    greet(bit_peers(scratch[1].shape[0]))
    run(deal_flow(lens_ref, flags_ref, own_ref, out_ref, scratch))


def deal(doc_lengths, keep_flags, blocks, collective_id):
    width = blocks.shape[2]
    return pl.pallas_call(
        deal_body,
        out_shape=jax.ShapeDtypeStruct((SLOTS, BLOCK, width), blocks.dtype),
        in_specs=[smem(), smem(), vmem()],
        out_specs=vmem(),
        scratch_shapes=deal_scratch(stages_of("tok"), width, blocks.dtype),
        compiler_params=params(collective_id),
        cost_estimate=cost(0, 40_000_000),
        name="deal",
    )(doc_lengths, keep_flags, blocks)


def undeal_flow(lens_ref, flags_ref, kept_ref, home_ref, out_ref, scratch, pace=4.3):
    keep, send, recv, send_sem, recv_sem = scratch
    stages = recv.shape[0]
    own = lax.axis_index("tok")
    blocks_here = home_ref.shape[0]
    rows = BLOCK // CHUNKS
    peers = bit_peers(stages)
    keeps, sends, finals = deal_tables(own, stages, blocks_here, lens_ref, flags_ref)

    def copy(stage, chunk):
        return pltpu.make_async_remote_copy(
            src_ref=send.at[stage, chunk],
            dst_ref=recv.at[stage, chunk],
            send_sem=send_sem.at[stage, chunk],
            recv_sem=recv_sem.at[stage, chunk],
            device_id=peers[stage],
            device_id_type=MESH,
        )

    def pick_place(places, options, place, value):
        for index, option in zip(places, options):
            value = jnp.where(index == place, option, value)
        return value

    last = stages - 1
    for stage in range(last, -2, -1):
        for chunk in range(CHUNKS):
            yield 0.0 if stage == last else 1 + pace * (chunk + last - stage - (stage < 0))
            span = pl.ds(chunk * rows, rows)
            if stage == last:
                options = [kept_ref[slot, span, :] for slot in range(SLOTS)]
                places = finals
            else:
                copy(stage + 1, chunk).wait_recv()
                options = [keep[chunk, i] for i in range(SLOTS)] + [
                    recv[stage + 1, chunk, i] for i in range(SLOTS)
                ]
                places = keeps[stage + 1] + sends[stage + 1]
            if stage < 0:
                for place in range(blocks_here):
                    home = home_ref[place, span, :]
                    out_ref[place, span, :] = pick_place(places, options, place, home)
            else:
                for slot in range(SLOTS):
                    send[stage, chunk, slot] = pick_place(
                        places, options, SLOTS + slot, options[0]
                    )
                copy(stage, chunk).start()
                for slot in range(SLOTS):
                    keep[chunk, slot] = pick_place(places, options, slot, options[0])
    yield 1e6

    def drain(chunk, carry):
        for stage in range(stages):
            copy(stage, chunk).wait_send()
        return carry

    lax.fori_loop(0, CHUNKS, drain, 0)


def undeal_body(lens_ref, flags_ref, kept_ref, home_ref, gains_ref, out_ref, sum_ref, *scratch):
    undealing = scratch[:5]
    gain_recv, gain_send_sem, gain_recv_sem = scratch[5:]
    own, plane = lax.axis_index("tok"), lax.axis_index("tp")
    devices = gain_recv.shape[0]
    share = sum_ref.shape[1]
    greet([(own ^ step, plane) for step in range(1, devices)])

    def portion(there):
        if share % 128 == 0 and share < gains_ref.shape[1]:
            return gains_ref.at[:, pl.ds(pl.multiple_of(there * share, share), share)]
        return gains_ref

    def gain_copy(step):
        there = own ^ step
        return pltpu.make_async_remote_copy(
            src_ref=portion(there),
            dst_ref=gain_recv.at[step],
            send_sem=gain_send_sem.at[step],
            recv_sem=gain_recv_sem.at[step],
            device_id=(there, plane),
            device_id_type=MESH,
        )

    for step in range(1, devices):
        gain_copy(step).start()
    run(undeal_flow(lens_ref, flags_ref, kept_ref, home_ref, out_ref, undealing))
    total = portion(own)[...]
    for step in range(1, devices):
        gain_copy(step).wait()
        total = total + gain_recv[step]
    sum_ref[...] = total


def undeal(doc_lengths, keep_flags, kept, home, gains, collective_id):
    stages = stages_of("tok")
    devices = 1 << stages
    width = kept.shape[2]
    share = width // devices
    share = share if share % 128 == 0 else width
    return pl.pallas_call(
        undeal_body,
        out_shape=(
            jax.ShapeDtypeStruct(home.shape, home.dtype),
            jax.ShapeDtypeStruct((8, share), F32),
        ),
        in_specs=[smem(), smem(), vmem(), vmem(), vmem()],
        out_specs=(vmem(), vmem()),
        scratch_shapes=deal_scratch(stages, width, kept.dtype)
        + [
            pltpu.VMEM((devices, 8, share), F32),
            pltpu.SemaphoreType.DMA((devices,)),
            pltpu.SemaphoreType.DMA((devices,)),
        ],
        compiler_params=params(collective_id),
        cost_estimate=cost(0, 40_000_000),
        name="undeal",
    )(doc_lengths, keep_flags, kept, home, gains)


def project_body(
    x_ref, gain_ref, w_query_ref, w_key_ref, w_value_ref, cos_ref, sin_ref,
    normed_ref, inv_ref, query_ref, out_ref,
    mine_ref, send_sem, recv_sem, relay_send_sem, relay_recv_sem,
):
    devices = out_ref.shape[0]
    chips = devices // 2
    own = lax.axis_index("tok")
    plane = lax.axis_index("tp")
    partner = (own ^ 1, plane)
    rows = x_ref.shape[0]
    thin = w_key_ref.shape[1]
    greet([partner] + [(own ^ (2 * step), plane) for step in range(1, chips)])

    def copy(step):
        return pltpu.make_async_remote_copy(
            src_ref=mine_ref,
            dst_ref=out_ref.at[own],
            send_sem=send_sem.at[step],
            recv_sem=recv_sem.at[step],
            device_id=(own ^ (2 * step), plane),
            device_id_type=MESH,
        )

    def relay(step):
        return pltpu.make_async_remote_copy(
            src_ref=mine_ref if step == 0 else out_ref.at[own ^ (2 * step)],
            dst_ref=out_ref.at[own ^ (2 * step)],
            send_sem=relay_send_sem.at[step],
            recv_sem=relay_recv_sem.at[step],
            device_id=partner,
            device_id_type=MESH,
        )

    def norm(index, carry):
        span = pl.ds(pl.multiple_of(index * 16, 16), 16)
        x = x_ref[span, :].astype(F32)
        inv = lax.rsqrt(jnp.mean(x * x, axis=1, keepdims=True) + norm_eps)
        inv_ref[span, :] = inv
        normed_ref[span, :] = (x * inv * gain_ref[...]).astype(BF16)
        return carry

    lax.fori_loop(0, rows // 16, norm, 0)

    def product(w_ref):
        return lax.dot_general(
            normed_ref[...], w_ref[...], (((1,), (0,)), ((), ())), preferred_element_type=F32
        )

    keys = product(w_key_ref)
    for group in range(thin // HD):
        one = keys[:, group * HD : (group + 1) * HD]
        mine_ref[:, group * HD : (group + 1) * HD] = turn(one, cos_ref, sin_ref, -1.0).astype(BF16)
    mine_ref[:, thin:] = product(w_value_ref).astype(BF16)
    for step in range(1, chips):
        copy(step).start()
    relay(0).start()
    out_ref[own] = mine_ref[...]
    queries = product(w_query_ref)
    for head in range(w_query_ref.shape[1] // HD):
        one = queries[:, head * HD : (head + 1) * HD]
        query_ref[:, head * HD : (head + 1) * HD] = turn(one, cos_ref, sin_ref, -1.0).astype(BF16)
    for step in range(1, chips):
        copy(step).wait_recv()
        relay(step).start()
    for step in range(chips):
        relay(step).wait()
    for step in range(1, chips):
        copy(step).wait_send()


def turn(values, cos_ref, sin_ref, sign):
    return values * cos_ref[...] + pltpu.roll(values, HD // 2, 1) * (sin_ref[...] * sign)


def project(x, gain, w_query, w_key, w_value, cosine, sine, collective_id):
    devices = lax.axis_size("tok")
    chips = devices // 2
    rows = x.shape[0]
    both = w_key.shape[1] + w_value.shape[1]
    return pl.pallas_call(
        project_body,
        out_shape=(
            jax.ShapeDtypeStruct(x.shape, BF16),
            jax.ShapeDtypeStruct((rows, 1), F32),
            jax.ShapeDtypeStruct((rows, w_query.shape[1]), BF16),
            jax.ShapeDtypeStruct((devices, rows, both), BF16),
        ),
        in_specs=[vmem()] * 7,
        out_specs=(vmem(),) * 4,
        scratch_shapes=[pltpu.VMEM((rows, both), BF16)] + [pltpu.SemaphoreType.DMA((chips,))] * 4,
        compiler_params=params(collective_id),
        cost_estimate=cost(0, 30_000_000),
        name="project",
    )(x, gain, w_query, w_key, w_value, cosine, sine)


def first_rank(lens_ref, flags_ref, rank):
    first, start = jnp.int32(0), jnp.int32(0)
    for doc in range(lens_ref.shape[0]):
        blocks = flags_ref[doc] * (lens_ref[doc] // BLOCK)
        first = jnp.where((rank >= start) & (rank < start + blocks), start, first)
        start = start + blocks
    return first


def stack_heads(ref, slot):
    heads = ref.shape[1] // HD
    return jnp.concatenate(
        [ref[slot * BLOCK : (slot + 1) * BLOCK, i * HD : (i + 1) * HD] for i in range(heads)], axis=0
    )


def dot(left, right, dims):
    return lax.dot_general(left, right, ((dims[:1], dims[1:]), ((), ())), preferred_element_type=F32)


def key_block(kv_ref, rank):
    devices = kv_ref.shape[0]
    device, slot = lax.rem(rank, devices), lax.div(rank, devices)
    span = pl.ds(pl.multiple_of(slot * BLOCK, BLOCK), BLOCK)
    return device, span


def causal(scores):
    keys = lax.broadcasted_iota(jnp.int32, scores.shape, 0)
    queries = lax.rem(lax.broadcasted_iota(jnp.int32, scores.shape, 1), BLOCK)
    return jnp.where(keys <= queries, scores, -1e30)


def attend_body(lens_ref, flags_ref, own_ref, query_ref, kv_ref, out_ref, wide_ref, log_ref, total):
    devices = kv_ref.shape[0]
    scale = 1.0 / math.sqrt(HD)
    for slot in range(SLOTS):
        rank = own_ref[0] + devices * slot
        query = stack_heads(query_ref, slot)
        count = query.shape[0]
        total[...] = jnp.zeros_like(total)

        def visit(key_rank, state, masked):
            peak, weight = state
            device, span = key_block(kv_ref, key_rank)
            scores = dot(kv_ref[device, span, :HD], query, (1, 1)) * scale
            if masked:
                scores = causal(scores)
            higher = jnp.maximum(peak, jnp.max(scores, axis=0, keepdims=True))
            shrink = jnp.exp(peak - higher)
            probs = jnp.exp(scores - higher)
            weight = weight * shrink + jnp.sum(probs, axis=0, keepdims=True)
            values = kv_ref[device, span, HD:]
            total[...] = total[...] * shrink + dot(values, probs.astype(BF16), (0, 0))
            return higher, weight

        start = (jnp.full((1, count), -1e30, F32), jnp.zeros((1, count), F32))
        first = first_rank(lens_ref, flags_ref, rank)
        state = lax.fori_loop(first, rank, lambda r, s: visit(r, s, False), start)
        peak, weight = visit(rank, state, True)
        result = total[...] / weight
        wide_ref[slot] = result
        log_ref[slot] = jnp.broadcast_to(peak + jnp.log(weight), log_ref.shape[1:])
        turned = result.T.astype(BF16)
        for head in range(count // BLOCK):
            out_ref[slot * BLOCK : (slot + 1) * BLOCK, head * HD : (head + 1) * HD] = turned[
                head * BLOCK : (head + 1) * BLOCK
            ]


def attend(doc_lengths, keep_flags, own, query, kv):
    count = query.shape[1] // HD * BLOCK
    return pl.pallas_call(
        attend_body,
        out_shape=(
            jax.ShapeDtypeStruct(query.shape, BF16),
            jax.ShapeDtypeStruct((SLOTS, HD, count), F32),
            jax.ShapeDtypeStruct((SLOTS, 8, count), F32),
        ),
        in_specs=[smem()] * 3 + [vmem()] * 2,
        out_specs=(vmem(),) * 3,
        scratch_shapes=[pltpu.VMEM((HD, count), F32)],
        compiler_params=pltpu.CompilerParams(vmem_limit_bytes=VMEM_BYTES),
        cost_estimate=cost(1_000_000_000, 10_000_000),
        name="attend",
    )(doc_lengths, keep_flags, own, query, kv)


def attend_back_body(
    lens_ref, flags_ref, own_ref, query_ref, grad_ref, kv_ref, wide_ref, log_ref, cos_ref, sin_ref,
    grad_query_ref, grad_kv_ref, grad_kv, total,
):
    devices = kv_ref.shape[0]
    scale = 1.0 / math.sqrt(HD)
    grad_kv[...] = jnp.zeros_like(grad_kv)
    for slot in range(SLOTS):
        rank = own_ref[0] + devices * slot
        query = stack_heads(query_ref, slot)
        grad = stack_heads(grad_ref, slot)
        delta = jnp.sum(grad.astype(F32).T * wide_ref[slot], axis=0, keepdims=True)
        log_total = log_ref[slot, 0:1, :]
        total[...] = jnp.zeros_like(total)

        def visit(key_rank, masked):
            device, span = key_block(kv_ref, key_rank)
            keys, values = kv_ref[device, span, :HD], kv_ref[device, span, HD:]
            scores = dot(keys, query, (1, 1)) * scale
            if masked:
                scores = causal(scores)
            probs = jnp.exp(scores - log_total)
            grad_probs = dot(values, grad, (1, 1))
            grad_scores = (probs * (grad_probs - delta)).astype(BF16)
            grad_kv[device, span, HD:] += dot(probs.astype(BF16), grad, (1, 0))
            grad_kv[device, span, :HD] += dot(grad_scores, query, (1, 0)) * scale
            total[...] += dot(keys, grad_scores, (0, 0))

        def step(key_rank, carry):
            visit(key_rank, False)
            return carry

        lax.fori_loop(first_rank(lens_ref, flags_ref, rank), rank, step, 0)
        visit(rank, True)
        turned = (total[...] * scale).T
        span = pl.ds(slot * BLOCK, BLOCK)
        for head in range(turned.shape[0] // BLOCK):
            one = turned[head * BLOCK : (head + 1) * BLOCK]
            grad_query_ref[span, head * HD : (head + 1) * HD] = turn(
                one, cos_ref.at[span], sin_ref.at[span], 1.0
            ).astype(BF16)
    grad_kv_ref[...] = grad_kv[...].astype(BF16)


def attend_back(doc_lengths, keep_flags, own, query, grad, kv, wide, log_total, cosine, sine):
    count = query.shape[1] // HD * BLOCK
    return pl.pallas_call(
        attend_back_body,
        out_shape=(
            jax.ShapeDtypeStruct(query.shape, BF16),
            jax.ShapeDtypeStruct(kv.shape, BF16),
        ),
        in_specs=[smem()] * 3 + [vmem()] * 7,
        out_specs=(vmem(),) * 2,
        scratch_shapes=[pltpu.VMEM(kv.shape, F32), pltpu.VMEM((HD, count), F32)],
        compiler_params=pltpu.CompilerParams(vmem_limit_bytes=VMEM_BYTES),
        cost_estimate=cost(3_000_000_000, 20_000_000),
        name="attend_back",
    )(doc_lengths, keep_flags, own, query, grad, kv, wide, log_total, cosine, sine)


def scatter_tok_body(
    part_ref, out_ref, core_recv, held, recv, core_send_sem, core_recv_sem, send_sem, recv_sem
):
    devices = part_ref.shape[0]
    chips = devices // 2
    own = lax.axis_index("tok")
    plane = lax.axis_index("tp")
    partner = (own ^ 1, plane)
    greet([partner] + [(own ^ (2 * step), plane) for step in range(1, chips)])

    def core_copy(step):
        return pltpu.make_async_remote_copy(
            src_ref=part_ref.at[own ^ (2 * step) ^ 1],
            dst_ref=core_recv.at[step],
            send_sem=core_send_sem.at[step],
            recv_sem=core_recv_sem.at[step],
            device_id=partner,
            device_id_type=MESH,
        )

    def copy(step):
        return pltpu.make_async_remote_copy(
            src_ref=held.at[step],
            dst_ref=recv.at[step],
            send_sem=send_sem.at[step],
            recv_sem=recv_sem.at[step],
            device_id=(own ^ (2 * step), plane),
            device_id_type=MESH,
        )

    order = list(range(chips - 1, -1, -1))
    for step in order:
        core_copy(step).start()
    for step in order:
        core_copy(step).wait_recv()
        total = part_ref[own ^ (2 * step)].astype(F32) + core_recv[step].astype(F32)
        if step > 0:
            held[step] = total.astype(held.dtype)
            copy(step).start()
        else:
            out_ref[...] = total
    for step in range(1, chips):
        copy(step).wait_recv()
        out_ref[...] += recv[step].astype(F32)
    for step in range(1, chips):
        copy(step).wait_send()
    for step in range(chips):
        core_copy(step).wait_send()


def scatter_tok(part, collective_id):
    devices = part.shape[0]
    chips = devices // 2
    shard = part.shape[1:]
    return pl.pallas_call(
        scatter_tok_body,
        out_shape=jax.ShapeDtypeStruct(shard, F32),
        in_specs=[vmem()],
        out_specs=vmem(),
        scratch_shapes=[
            pltpu.VMEM((chips,) + shard, part.dtype),
            pltpu.VMEM((chips,) + shard, part.dtype),
            pltpu.VMEM((chips,) + shard, part.dtype),
        ]
        + [pltpu.SemaphoreType.DMA((chips,))] * 4,
        compiler_params=params(collective_id),
        cost_estimate=cost(0, 10_000_000),
        name="scatter_tok",
    )(part)


def line_sems(planes):
    return [pltpu.SemaphoreType.DMA((2, planes))] * 2


def line_copy(own, plane, step, source, target, send_sem, recv_sem, index):
    side = 0 if step > 0 else 1
    return pltpu.make_async_remote_copy(
        src_ref=source,
        dst_ref=target,
        send_sem=send_sem.at[side, index],
        recv_sem=recv_sem.at[side, index],
        device_id=(own, plane + step),
        device_id_type=MESH,
    )


def line_gather(own, plane, planes, arrays, start, pace):
    last = planes - 1

    def move(array, index, step):
        out, rest, send_sem, recv_sem = array
        shard = out.at[(index,) + rest]
        return line_copy(own, plane, step, shard, shard, send_sem, recv_sem, index)

    for step in range(1, planes + 1):
        yield start + pace * (step - 1)
        before, after = plane - (step - 1), plane + (step - 1)

        @pl.when(before >= 0)
        def _():
            for array in arrays:
                if step > 1:
                    move(array, before, 1).wait_recv()
                if step < planes:

                    @pl.when(plane < last)
                    def _():
                        move(array, before, 1).start()

        @pl.when(after <= last)
        def _():
            for array in arrays:
                if step > 1:
                    move(array, after, -1).wait_recv()
                if step < planes:

                    @pl.when(plane > 0)
                    def _():
                        move(array, after, -1).start()

    for index in range(planes):

        @pl.when((index <= plane) & (plane < last))
        def _():
            for array in arrays:
                move(array, index, 1).wait_send()

        @pl.when((index >= plane) & (plane > 0))
        def _():
            for array in arrays:
                move(array, index, -1).wait_send()


def line_reduce(own, plane, planes, half, part, total, send, recv, send_sem, recv_sem, start, pace):
    last = planes - 1

    def right(index):
        return line_copy(
            own, plane, 1, send.at[index, half], recv.at[index, half], send_sem, recv_sem, index
        )

    def left(index):
        slot = jnp.where(index == plane - 1, planes, index)
        return line_copy(
            own, plane, -1, send.at[index, half], recv.at[slot, half], send_sem, recv_sem, index
        )

    def add(index):
        send[index, half] = (
            part[index, half].astype(F32) + recv[index, half].astype(F32)
        ).astype(send.dtype)

    for step in range(1, planes):
        yield start + pace * (step - 1)
        upper, lower = planes - step + plane, step - planes + plane

        @pl.when((upper <= last) & (plane < last))
        def _():
            @pl.when(plane == 0)
            def _():
                send[upper, half] = part[upper, half]

            @pl.when(plane > 0)
            def _():
                right(upper).wait_recv()
                add(upper)

            right(upper).start()

        @pl.when((lower >= 0) & (plane > 0))
        def _():
            @pl.when(plane == last)
            def _():
                send[lower, half] = part[lower, half]

            @pl.when(plane < last)
            def _():
                left(lower).wait_recv()
                add(lower)

            left(lower).start()

    yield start + pace * (planes - 1)
    total[half] = part[plane, half].astype(F32)

    @pl.when(plane > 0)
    def _():
        right(plane).wait_recv()
        total[half] += recv[plane, half].astype(F32)

    @pl.when(plane < last)
    def _():
        left(plane).wait_recv()
        total[half] += recv[planes, half].astype(F32)

    yield start + pace * (2 * planes)
    for index in range(planes):

        @pl.when((index > plane) & (plane < last))
        def _():
            right(index).wait_send()

        @pl.when((index < plane) & (plane > 0))
        def _():
            left(index).wait_send()


def sum_flows(part_ref, gathered, scratch, math_rule, start=0.0, pace=8.7, extra=None):
    total, send, recv, send_sem, recv_sem, gather_send_sem, gather_recv_sem = scratch
    planes = part_ref.shape[0]
    own, plane = lax.axis_index("tok"), lax.axis_index("tp")
    lag = pace / 2

    def flow(half):
        begin = start + lag * half
        reducing = line_reduce(
            own, plane, planes, half, part_ref, total, send, recv,
            send_sem.at[half], recv_sem.at[half], begin, pace,
        )
        for number in range(planes):
            yield next(reducing)
        next(reducing)
        math_rule(plane, half, total, gathered)
        arrays = [(gathered, (half,), gather_send_sem.at[half], gather_recv_sem.at[half])]
        if extra is not None and half == HALVES - 1:
            arrays.append(extra)
        yield from line_gather(own, plane, planes, arrays, begin + pace * (planes - 1), pace)
        for _ in reducing:
            pass

    return [flow(half) for half in range(HALVES)]


def sum_scratch(planes, shard, width, kind):
    rows = shard // HALVES
    return [
        pltpu.VMEM((HALVES, rows, width), F32),
        pltpu.VMEM((planes, HALVES, rows, width), kind),
        pltpu.VMEM((planes + 1, HALVES, rows, width), kind),
    ] + [pltpu.SemaphoreType.DMA((HALVES, 2, planes))] * 4


def by_tiles(rows, step):
    lax.fori_loop(0, rows // 16, lambda i, c: (step(pl.ds(pl.multiple_of(i * 16, 16), 16)), c)[1], 0)


def norm_math(x_ref, gain_ref, hidden_ref, inv_ref):
    def rule(plane, half, total, gathered):
        def tile(rows):
            hidden = x_ref[plane, half, rows, :].astype(F32) + total[half, rows, :]
            inv = lax.rsqrt(jnp.mean(hidden * hidden, axis=1, keepdims=True) + norm_eps)
            hidden_ref[half, rows, :] = hidden
            inv_ref[half, rows, :] = inv
            gathered[plane, half, rows, :] = (hidden * inv * gain_ref[...]).astype(BF16)

        by_tiles(total.shape[1], tile)

    return rule


def ffn_math(hidden_ref, inv_ref, dy_ref, gain_ref, grad_ref, gains_ref):
    def rule(plane, half, total, gathered):
        if half == 0:
            gains_ref[...] = jnp.zeros_like(gains_ref)

        def tile(rows):
            dn = total[half, rows, :]
            hidden = hidden_ref[half, rows, :]
            inv = inv_ref[half, rows, :]
            weighted = gain_ref[...] * dn
            mean = jnp.mean(weighted * hidden, axis=1, keepdims=True)
            grad = (
                keep_scale * dy_ref[plane, half, rows, :].astype(F32)
                + inv * weighted
                - hidden * (inv * inv * inv * mean)
            )
            grad_ref[half, rows, :] = grad
            gathered[plane, half, rows, :] = grad.astype(BF16)
            gains_ref[0:1, :] += jnp.sum(dn * hidden * inv, axis=0, keepdims=True)

        by_tiles(total.shape[1], tile)

    return rule


def mixed_math(hidden_ref, x_ref):
    def rule(plane, half, total, gathered):
        def tile(rows):
            x = x_ref[plane, half, rows, :].astype(F32)
            branch = (hidden_ref[half, rows, :] - x) + total[half, rows, :]
            gathered[plane, half, rows, :] = (x + keep_scale * branch).astype(BF16)

        by_tiles(total.shape[1], tile)

    return rule


def attn_math(x_ref, inv_ref, dy_ref, grad_ref, gain_ref, ffn_gains_ref, gains_all):
    def rule(plane, half, total, gathered):
        if half == 0:
            gains_all[plane] = ffn_gains_ref[...]

        def tile(rows):
            dn = total[half, rows, :]
            x = x_ref[plane, half, rows, :].astype(F32)
            inv = inv_ref[plane, half, rows, :]
            weighted = gain_ref[...] * dn
            mean = jnp.mean(weighted * x, axis=1, keepdims=True)
            grad = (
                (1.0 - keep_scale) * dy_ref[plane, half, rows, :].astype(F32)
                + grad_ref[half, rows, :]
                + inv * weighted
                - x * (inv * inv * inv * mean)
            )
            gathered[plane, half, rows, :] = grad.astype(BF16)
            gains_all[plane, 1:2, :] += jnp.sum(dn * x * inv, axis=0, keepdims=True)

        by_tiles(total.shape[1], tile)

    return rule


def deal_sum_body(
    lens_ref, flags_ref, own_ref, part_ref, x_ref, gain_ref,
    out_ref, gathered, hidden_ref, inv_ref, *scratch,
):
    dealing, summing = scratch[:5], scratch[5:]
    greet(bit_peers(dealing[1].shape[0]), line=True)
    run(
        *sum_flows(part_ref, gathered, summing, norm_math(x_ref, gain_ref, hidden_ref, inv_ref)),
        deal_flow(lens_ref, flags_ref, own_ref, out_ref, dealing),
    )


def deal_sum(doc_lengths, keep_flags, blocks, part, x, gain, collective_id):
    planes, halves, rows, width = part.shape
    return pl.pallas_call(
        deal_sum_body,
        out_shape=(
            jax.ShapeDtypeStruct((SLOTS, BLOCK, width), blocks.dtype),
            jax.ShapeDtypeStruct(part.shape, BF16),
            jax.ShapeDtypeStruct((halves, rows, width), F32),
            jax.ShapeDtypeStruct((halves, rows, 1), F32),
        ),
        in_specs=[smem(), smem()] + [vmem()] * 4,
        out_specs=(vmem(),) * 4,
        scratch_shapes=deal_scratch(stages_of("tok"), width, blocks.dtype)
        + sum_scratch(planes, halves * rows, width, BF16),
        compiler_params=params(collective_id),
        cost_estimate=cost(0, 60_000_000),
        name="deal_sum",
    )(doc_lengths, keep_flags, blocks, part, x, gain)


def spread_flow(units, outs, scratch, pace):
    own, plane = lax.axis_index("tok"), lax.axis_index("tp")
    count = len(units)
    boxes, inboxes, core_inboxes = scratch[:count], scratch[count : 2 * count], scratch[2 * count : 3 * count]
    core_send_sem, core_recv_sem, send_sem, recv_sem = scratch[3 * count :]
    chips = boxes[0].shape[0]
    bits = [1 << i for i in range(int(math.log2(chips)))]
    orders = (bits, bits[::-1])
    stages = len(bits)

    def core_copy(unit, chip):
        return pltpu.make_async_remote_copy(
            src_ref=boxes[unit].at[chip],
            dst_ref=core_inboxes[unit].at[chip],
            send_sem=core_send_sem.at[unit, chip],
            recv_sem=core_recv_sem.at[unit, chip],
            device_id=(own ^ 1, plane),
            device_id_type=MESH,
        )

    def active(half, stage):
        gone = orders[half][:stage]
        return [chip for chip in range(chips) if all(chip & bit == 0 for bit in gone)]

    def slot(stage, half, chip):
        before = sum(chips >> (earlier + 1) for earlier in range(stage))
        return before + active(half, stage + 1).index(chip)

    def copy(unit, half, stage, chip):
        bit = orders[half][stage]
        there = slot(stage, half, chip)
        return pltpu.make_async_remote_copy(
            src_ref=boxes[unit].at[chip ^ bit, half],
            dst_ref=inboxes[unit].at[there, half],
            send_sem=send_sem.at[unit, half, there],
            recv_sem=recv_sem.at[unit, half, there],
            device_id=(own ^ (2 * bit), plane),
            device_id_type=MESH,
        )

    def offer(unit, chip):
        for half in range(2):
            term = units[unit]((own ^ (2 * chip)) ^ 1, half)
            boxes[unit][chip, half] = term.astype(BF16)
        core_copy(unit, chip).start()

    def collect(unit, chip):
        core_copy(unit, chip).wait()
        for half in range(2):
            term = units[unit](own ^ (2 * chip), half)
            term = term + core_inboxes[unit][chip, half].astype(F32)
            boxes[unit][chip, half] = term.astype(BF16)
            bit = orders[half][0]
            if chip & bit:
                copy(unit, half, 0, chip ^ bit).start()

    def take(unit, stage, half):
        for chip in active(half, stage + 1):
            copy(unit, half, stage, chip).wait_recv()
            got = inboxes[unit][slot(stage, half, chip), half].astype(F32)
            total = boxes[unit][chip, half].astype(F32) + got
            if stage < stages - 1:
                boxes[unit][chip, half] = total.astype(BF16)
                bit = orders[half][stage + 1]
                if chip & bit:
                    copy(unit, half, stage + 1, chip ^ bit).start()
            else:
                rows = total.shape[0]
                outs[unit][half * rows : (half + 1) * rows, :] = total

    chip_order = sorted(range(chips), key=lambda chip: -bin(chip).count("1"))
    for unit in range(count):
        for chip in chip_order:
            yield 0.1 + 3 * unit
            offer(unit, chip)
        for chip in chip_order:
            yield 3.2 + 3 * unit
            collect(unit, chip)
    for stage in range(stages):
        for unit in range(count):
            for half in range(2):
                yield 6.0 + pace * (unit + 1 + count * stage)
                take(unit, stage, half)
    for unit in range(count):
        for half in range(2):
            for stage in range(stages):
                for chip in active(half, stage + 1):
                    copy(unit, half, stage, chip).wait_send()


def spread_scratch(shapes, devices):
    chips = devices // 2
    boxes = [pltpu.VMEM((chips, 2, rows // 2, columns), BF16) for rows, columns in shapes]
    inboxes = [pltpu.VMEM((chips - 1, 2, rows // 2, columns), BF16) for rows, columns in shapes]
    return (
        boxes
        + inboxes
        + boxes
        + [pltpu.SemaphoreType.DMA((len(shapes), chips))] * 2
        + [pltpu.SemaphoreType.DMA((len(shapes), 2, chips - 1))] * 2
    )


def window(ref, number, size):
    if size % 128 == 0:
        return ref[:, pl.ds(pl.multiple_of(number * size, size), size)]
    parts = 128 // size
    tile = ref[:, pl.ds(pl.multiple_of(number // parts * 128, 128), 128)].astype(F32)
    return choose(
        number % parts, [tile[:, i * size : (i + 1) * size] for i in range(parts)]
    ).astype(ref.dtype)


def rows_by_owner(left_ref, right_ref, rows):
    def term(owner, half):
        return lax.dot_general(
            window(left_ref, owner * 2 + half, rows // 2),
            right_ref[...],
            (((0,), (0,)), ((), ())),
            preferred_element_type=F32,
        )

    return term


def columns_by_owner(left_ref, right_ref, columns):
    def term(owner, half):
        rows = left_ref.shape[1] // 2
        return lax.dot_general(
            left_ref[:, half * rows : (half + 1) * rows],
            window(right_ref, owner, columns),
            (((0,), (0,)), ((), ())),
            preferred_element_type=F32,
        )

    return term


def ffn_sums_body(
    part_ref, hidden_ref, inv_ref, dy_ref, gain_ref, normed_ref, dgate_ref, dup_ref, inner_ref, dm_ref,
    mixed_part_ref, x_ref,
    gathered, grad_ref, gains_ref, gate_out, up_out, down_out, mixed_gathered, *scratch,
):
    summing, mixing, spreading = scratch[:7], scratch[7:14], scratch[14:]
    own, plane = lax.axis_index("tok"), lax.axis_index("tp")
    devices = lax.axis_size("tok")
    share = normed_ref.shape[1] // devices
    chips = devices // 2
    greet([(own ^ 1, plane)] + [(own ^ (2 << i), plane) for i in range(stages_of("tok") - 1)], True)
    run(
        *sum_flows(
            part_ref,
            gathered,
            summing,
            ffn_math(hidden_ref, inv_ref, dy_ref, gain_ref, grad_ref, gains_ref),
        ),
        *sum_flows(mixed_part_ref, mixed_gathered, mixing, mixed_math(hidden_ref, x_ref), 27.0, 11.0),
        spread_flow(
            [
                rows_by_owner(normed_ref, dgate_ref, share),
                rows_by_owner(normed_ref, dup_ref, share),
                columns_by_owner(inner_ref, dm_ref, share),
            ],
            [gate_out, up_out, down_out],
            spreading,
            15.6,
        ),
    )


def ffn_sums(
    part, hidden, inv, dy, gain, normed, dgate, dup, inner, dm, mixed_part, x, collective_id
):
    planes, halves, rows, width = part.shape
    shard = halves * rows
    devices = lax.axis_size("tok")
    share = width // devices
    wide = dgate.shape[1]
    shapes = [(share, wide), (share, wide), (wide, share)]
    return pl.pallas_call(
        ffn_sums_body,
        out_shape=[
            jax.ShapeDtypeStruct(part.shape, BF16),
            jax.ShapeDtypeStruct(hidden.shape, F32),
            jax.ShapeDtypeStruct((8, width), F32),
        ]
        + [jax.ShapeDtypeStruct(shape, F32) for shape in shapes]
        + [jax.ShapeDtypeStruct(part.shape, BF16)],
        in_specs=[vmem()] * 12,
        out_specs=[vmem()] * 7,
        scratch_shapes=sum_scratch(planes, shard, width, BF16) * 2 + spread_scratch(shapes, devices),
        compiler_params=params(collective_id),
        cost_estimate=cost(0, 80_000_000),
        name="ffn_sums",
    )(part, hidden, inv, dy, gain, normed, dgate, dup, inner, dm, mixed_part, x)


def attn_sums_body(
    lens_ref, flags_ref, part_ref, x_ref, inv_ref, dy_ref, grad_ref, gain_ref, ffn_gains_ref,
    kept_ref, home_ref, normed_ref, dqkv_ref, attended_ref, da_ref,
    gathered, gains_ref, mixed_ref, qkv_out, out_out, *scratch,
):
    summing, undealing, scratch = scratch[:7], scratch[7:12], scratch[12:]
    gains_all, gains_sems, spreading = scratch[0], scratch[1:3], scratch[3:]
    planes = part_ref.shape[0]
    share = normed_ref.shape[1] // lax.axis_size("tok")
    greet(bit_peers(stages_of("tok")), True)
    run(
        *sum_flows(
            part_ref,
            gathered,
            summing,
            attn_math(x_ref, inv_ref, dy_ref, grad_ref, gain_ref, ffn_gains_ref, gains_all),
            extra=(gains_all, ()) + gains_sems,
        ),
        undeal_flow(lens_ref, flags_ref, kept_ref, home_ref, mixed_ref, undealing, 7.0),
        spread_flow(
            [
                rows_by_owner(normed_ref, dqkv_ref, share),
                columns_by_owner(attended_ref, da_ref, share),
            ],
            [qkv_out, out_out],
            spreading,
            15.0,
        ),
    )
    total = gains_all[0]
    for index in range(1, planes):
        total = total + gains_all[index]
    gains_ref[...] = total


def attn_sums(
    doc_lengths, keep_flags, part, x, inv, dy, grad, gain, ffn_gains, kept, home, normed, dqkv,
    attended, da, collective_id,
):
    planes, halves, rows, width = part.shape
    shard = halves * rows
    devices = lax.axis_size("tok")
    share = width // devices
    shapes = [(share, dqkv.shape[1]), (attended.shape[1], share)]
    return pl.pallas_call(
        attn_sums_body,
        out_shape=[
            jax.ShapeDtypeStruct(part.shape, BF16),
            jax.ShapeDtypeStruct((8, width), F32),
            jax.ShapeDtypeStruct(home.shape, BF16),
        ]
        + [jax.ShapeDtypeStruct(shape, F32) for shape in shapes],
        in_specs=[smem(), smem()] + [vmem()] * 13,
        out_specs=[vmem()] * 5,
        scratch_shapes=sum_scratch(planes, shard, width, BF16)
        + deal_scratch(stages_of("tok"), width, BF16)
        + [pltpu.VMEM((planes, 8, width), F32)]
        + line_sems(planes)
        + spread_scratch(shapes, devices),
        compiler_params=params(collective_id),
        cost_estimate=cost(0, 80_000_000),
        name="attn_sums",
    )(
        doc_lengths, keep_flags, part, x, inv, dy, grad, gain, ffn_gains, kept, home, normed, dqkv,
        attended, da,
    )


def rotary_tables(doc_lengths, keep_flags, ranks):
    blocks = keep_flags * (doc_lengths // BLOCK)
    ends = jnp.cumsum(blocks, dtype=jnp.int32)
    starts = ends - blocks
    inside = (ranks[:, None] >= starts[None, :]) & (ranks[:, None] < ends[None, :])
    first = jnp.sum(jnp.where(inside, starts[None, :], 0), axis=1, dtype=jnp.int32)
    offsets = jnp.arange(BLOCK, dtype=jnp.int32)
    positions = (((ranks - first) * BLOCK)[:, None] + offsets[None, :]).reshape(-1)
    half_dim = HD // 2
    freqs = jnp.exp(jnp.arange(half_dim, dtype=jnp.float32) * (-2.0 * math.log(10000.0) / HD))
    angles = positions.astype(jnp.float32)[:, None] * freqs[None, :]
    cosine, sine = jnp.cos(angles), jnp.sin(angles)
    return jnp.concatenate([cosine, cosine], axis=1), jnp.concatenate([sine, -sine], axis=1)


def unrotate(values, cosine, sine):
    half_dim = HD // 2
    swapped = jnp.concatenate([values[:, half_dim:], values[:, :half_dim]], axis=1)
    return values * cosine + swapped * sine


def over_columns(left, right):
    return lax.dot_general(
        left, right, (((1,), (1,)), ((), ())), preferred_element_type=jnp.float32
    )


def on_device(
    tokens,
    gain_attn,
    w_query,
    w_key,
    w_value,
    w_out,
    gain_ffn,
    w_gate,
    w_up,
    w_down,
    cotangent,
    doc_lengths,
    keep_flags,
):
    length = tokens.shape[0]
    model_width = tokens.shape[1]
    devices = lax.axis_size("tok")
    planes = lax.axis_size("tp")
    own_index = lax.axis_index("tok")
    blocks_here = length // BLOCK
    kept_here = blocks_here // 2
    total_blocks = blocks_here * devices
    kept_total = kept_here * devices
    rows = kept_here * BLOCK
    token_blocks = tokens.reshape(blocks_here, BLOCK, model_width)
    grad_blocks = cotangent.reshape(blocks_here, BLOCK, model_width)

    rows_x = deal(doc_lengths, keep_flags, token_blocks, 0).reshape(rows, model_width)

    own_ranks = own_index + jnp.arange(kept_here, dtype=jnp.int32) * devices
    cosine, sine = rotary_tables(doc_lengths, keep_flags, own_ranks)
    own = jnp.reshape(own_index, (1,)).astype(jnp.int32)
    normed_one, inv_one, queries, kv_all = project(
        rows_x, gain_attn.reshape(1, -1), w_query, w_key, w_value, cosine, sine, 2
    )
    attended, attended_wide, log_totals = attend(doc_lengths, keep_flags, own, queries, kv_all)

    shard = rows // planes

    def by_plane(array):
        return array.reshape(planes, HALVES, shard // HALVES, array.shape[1])

    x_planes = by_plane(rows_x)
    rows_dy, normed_two, hidden_res, inv_two = deal_sum(
        doc_lengths,
        keep_flags,
        grad_blocks,
        by_plane(jnp.dot(attended, w_out, preferred_element_type=jnp.float32).astype(jnp.bfloat16)),
        x_planes,
        gain_ffn.reshape(1, -1),
        1,
    )
    rows_dy = rows_dy.reshape(rows, model_width)
    normed_two = normed_two.reshape(rows, model_width)
    gate = jnp.dot(normed_two, w_gate, preferred_element_type=jnp.float32)
    upper = jnp.dot(normed_two, w_up, preferred_element_type=jnp.float32)
    sigma = jax.nn.sigmoid(gate)
    swish = gate * sigma
    inner = (swish * upper).astype(jnp.bfloat16)

    grad_m = (keep_scale * rows_dy.astype(jnp.float32)).astype(jnp.bfloat16)
    grad_inner = over_columns(grad_m, w_down)
    grad_gate_pre = (grad_inner * upper * sigma * (1.0 + gate * (1.0 - sigma))).astype(jnp.bfloat16)
    grad_up_pre = (grad_inner * swish).astype(jnp.bfloat16)
    part_two = (
        over_columns(grad_gate_pre, w_gate) + over_columns(grad_up_pre, w_up)
    ).astype(jnp.bfloat16)

    dy_planes = by_plane(rows_dy)
    grad_a, grad_hidden, gains_ffn, grad_gate, grad_up, grad_down, mixed_rows = ffn_sums(
        by_plane(part_two),
        hidden_res,
        inv_two,
        dy_planes,
        gain_ffn.reshape(1, -1),
        normed_two,
        grad_gate_pre,
        grad_up_pre,
        inner,
        grad_m,
        by_plane(jnp.dot(inner, w_down, preferred_element_type=jnp.float32).astype(jnp.bfloat16)),
        x_planes,
        4,
    )
    grad_a = grad_a.reshape(rows, model_width)

    grad_attended = over_columns(grad_a, w_out).astype(jnp.bfloat16)
    grad_query_pre, grad_kv = attend_back(
        doc_lengths,
        keep_flags,
        own,
        queries,
        grad_attended,
        kv_all,
        attended_wide,
        log_totals,
        cosine,
        sine,
    )
    grad_kv = scatter_tok(grad_kv, 5)
    grad_key_pre = unrotate(grad_kv[:, :HD], cosine, sine).astype(jnp.bfloat16)
    grad_value_pre = grad_kv[:, HD:].astype(jnp.bfloat16)
    part_one = (
        over_columns(grad_query_pre, w_query)
        + over_columns(grad_key_pre, w_key)
        + over_columns(grad_value_pre, w_value)
    ).astype(jnp.bfloat16)
    grad_rows, gains, mixed, grad_qkv, grad_out = attn_sums(
        doc_lengths,
        keep_flags,
        by_plane(part_one),
        x_planes,
        by_plane(inv_one),
        dy_planes,
        grad_hidden,
        gain_attn.reshape(1, -1),
        gains_ffn,
        mixed_rows.reshape(kept_here, BLOCK, model_width),
        token_blocks,
        normed_one,
        jnp.concatenate([grad_query_pre, grad_key_pre, grad_value_pre], axis=1),
        attended,
        grad_a,
        6,
    )
    token_grad, gain_sums = undeal(
        doc_lengths,
        keep_flags,
        grad_rows.reshape(kept_here, BLOCK, model_width),
        grad_blocks,
        gains,
        9,
    )
    own_share = model_width // devices
    if gain_sums.shape[1] != own_share:
        gain_sums = lax.dynamic_slice_in_dim(gain_sums, own_index * own_share, own_share, 1)
    wide, thin = w_query.shape[1], w_key.shape[1]
    grad_query = grad_qkv[:, :wide]
    grad_key = grad_qkv[:, wide : wide + thin]
    grad_value = grad_qkv[:, wide + thin :]

    return (
        mixed.reshape(length, model_width),
        token_grad.reshape(length, model_width),
        gain_sums[1],
        grad_query,
        grad_key,
        grad_value,
        grad_out,
        gain_sums[0],
        grad_gate,
        grad_up,
        grad_down,
    )


def solution(mesh):
    placed = (
        P("tok", None),
        P(),
        P(None, "tp"),
        P(None, "tp"),
        P(None, "tp"),
        P("tp", None),
        P(),
        P(None, "tp"),
        P(None, "tp"),
        P("tp", None),
        P("tok", None),
        P(),
        P(),
    )
    return jax.shard_map(
        on_device,
        mesh=mesh,
        in_specs=placed,
        out_specs=(
            P("tok", None),
            P("tok", None),
            P("tok"),
            P("tok", "tp"),
            P("tok", "tp"),
            P("tok", "tp"),
            P("tp", "tok"),
            P("tok"),
            P("tok", "tp"),
            P("tok", "tp"),
            P("tp", "tok"),
        ),
        check_vma=False,
    )
```

time: 649 us -> 499 us (0.77)
  matrix products: 104 us -> 31.6 us
  local copies, waits for them, and re-layouts: 62 us -> 19.6 us
  other arithmetic: 38.7 us -> 6.85 us
  between operations: 15.4 us -> 1.46 us
  Pallas kernels: 423 us -> 430 us
    dot_general x33 -> x1, matrix products: 69.7 us -> 3.12 us  [on_device(): jnp.dot(attended, w_out, preferred_element_type=jnp.float32)]
    reduce_sum x14 -> x1, other arithmetic: 15 us -> 0.19 us  [rotary_tables(): jnp.sum(jnp.where(inside, starts[None, :], 0), axis=1, dtype=jnp.int32)]
    convert_element_type x8 -> x1, other arithmetic: 11.4 us -> 1.1 us  [on_device(): grad_key_pre = unrotate(grad_kv[:, :HD], cosine, sine).astype(jnp.bfloat16)]
    while x48 -> x0, local copies, waits for them, and re-layouts: 10.1 us -> none
    pallas_call x5 -> x6, Pallas kernels: 308 us -> 311 us  [the longest x1 106 us: ffn_sums(): pl.pallas_call(ffn_sums_body, out_shape=[jax.ShapeDtypeStruct(part.shape,...]
  transfers between devices with their start and end apart: 2 -> 0, of which waited for: 0 -> 0; matrix products, arithmetic and copies ran while one was open for 10% -> 0% of each run, Pallas kernels for 18% -> 0%
where the time goes in v3:
time: 499 us; the launch traced here: 490 us
  Pallas kernels  430 us (86%)
  matrix products  31.6 us (6%)
  local copies, waits for them, and re-layouts  19.6 us (4%)
  other arithmetic  6.85 us (1%)
    pallas_call x1, Pallas kernels, ffn_sums(): pl.pallas_call(ffn_sums_body, out_shape=[jax.ShapeDtypeStruct(part.shape,...  106 us
    pallas_call x1, Pallas kernels, attn_sums(): pl.pallas_call(attn_sums_body, out_shape=[jax.ShapeDtypeStruct(part.shape...  95.9 us
    pallas_call x1, Pallas kernels, deal_sum(): pl.pallas_call(deal_sum_body, out_shape=(jax.ShapeDtypeStruct((SLOTS, BLO...  63.1 us
    pallas_call x1, Pallas kernels, undeal(): pl.pallas_call(undeal_body, out_shape=(jax.ShapeDtypeStruct(home.shape, h...  50 us
    pallas_call x1, Pallas kernels, deal(): pl.pallas_call(deal_body, out_shape=jax.ShapeDtypeStruct((SLOTS, BLOCK, w...  48.9 us
    pallas_call x1, Pallas kernels, project(): pl.pallas_call(project_body, out_shape=(jax.ShapeDtypeStruct(x.shape, BF1...  22.1 us
    pallas_call x1, Pallas kernels, scatter_tok(): pl.pallas_call(scatter_tok_body, out_shape=jax.ShapeDtypeStruct(shard, F3...  20.4 us
    dot_general x7, matrix products, over_columns(): lax.dot_general(left, right, (((1,), (1,)), ((), ())), preferred_element_...  18.7 us

profile of v3, /device:TPU:1, one launch (start us, length us, event | category | flops | bytes accessed | tf_op | source)
XLA Modules:
  0.0 489.8 jit_solution(3952097484324911954)
XLA Ops:
  0.6 0.0 copy-start
  0.7 0.8 fusion.4
  1.5 0.2 reduce-window.8
  1.7 0.2 select_reduce_fusion
  1.9 0.1 convert_bitcast_fusion
  2.0 0.8 multiply_sine_fusion
  2.7 0.9 pad_maximum_fusion.1
  3.7 48.9 %deal.1 = bf16[3,128,2048]{2,1,0:T(8,128)(2,1)} custom-call(s32[6]{0:T(128)} %lens_ref.11, s32[6]{0:T(128)} %flags_ref.11, bf16[6,128,2048]{2,1,0:T(8,128)(2,1)} %bitcast.54), custom_call_target="tpu_custom_call" | custom-call | bytes 40000000 | tf_op jit(solution)/shard_map/deal/pallas_call | solution.py:222
  52.6 22.1 %project.1 = (bf16[384,2048]{1,0:T(8,128)(2,1)}, f32[384,1]{1,0:T(8,128)}, bf16[384,512]{1,0:T(8,128)(2,1)}, bf16[8,384,256]{2,1,0:T(8,128)(2,1)}) custom-call(bf16[384,2048]{1,0:T(8,128)(2,1)} %bitcast.48, f32[1,2048]{1,0:T(1,128)} %bitcast.74, bf16[2048,512]{1,0:T(8,128)(2,1)} %w_query_ref.1, bf16[2048,128]{1,0:T(8,128)(2,1)} %w_key_ref.1, ...), custom_call_target="tpu_custom_call" | custom-call | bytes 30000000 | tf_op jit(solution)/shard_map/project/pallas_call | solution.py:434
  74.7 11.1 %attend.1 = (bf16[384,512]{1,0:T(8,128)(2,1)}, f32[3,128,512]{2,1,0:T(8,128)}, f32[3,8,512]{2,1,0:T(8,128)}) custom-call(s32[6]{0:T(128)} %lens_ref.11, s32[6]{0:T(128)} %flags_ref.11, s32[1]{0:T(128)} %bitcast.own_ref, bf16[384,512]{1,0:T(8,128)(2,1)} %get-tuple-element.38.query_ref, bf16[8,384,256]{2,1,0:T(8,128)(2,1)} %get-tuple-element.39.kv_ref), custom_call_target="tpu_custom_call" | custom-call | flops 1000000000 | bytes 10000000 | tf_op jit(solution)/shard_map/attend/pallas_call | solution.py:523
  85.8 0.0 copy-done
  85.8 3.1 convolution_convert_fusion.1
  88.9 63.1 %deal_sum.1 = (bf16[3,128,2048]{2,1,0:T(8,128)(2,1)}, bf16[4,2,48,2048]{3,2,1,0:T(8,128)(2,1)}, f32[2,48,2048]{2,1,0:T(8,128)}, f32[2,48,1]{2,1,0:T(8,128)}) custom-call(s32[6]{0:T(128)} %lens_ref.11, s32[6]{0:T(128)} %flags_ref.11, bf16[6,128,2048]{2,1,0:T(8,128)(2,1)} %bitcast.56, bf16[4,2,48,2048]{3,2,1,0:T(8,128)(2,1)} %bitcast.67, ...), custom_call_target="tpu_custom_call" | custom-call | bytes 60000000 | tf_op jit(solution)/shard_map/deal_sum/pallas_call | solution.py:937
  152.1 0.0 slice-start.2
  152.1 1.9 multiply_convert_fusion
  154.0 0.0 copy-start.2
  154.0 0.0 copy-start.9
  154.0 0.0 slice-start.3
  154.0 0.0 slice-start.4
  154.0 5.8 %fusion.10 = f32[384,1408]{1,0:T(8,128)S(1)} fusion(bf16[384,2048]{1,0:T(8,128)(2,1)S(1)} %bitcast.59, bf16[1408,2048]{1,0:T(8,128)(2,1)} %param.22), kind=kOutput, calls=%fused_computation.37 | convolution fusion | flops 2214592512 | bytes 9502720 | tf_op jit(solution)/shard_map/dot_general | solution.py:1242
  159.9 0.0 copy-done.2
  159.9 0.0 slice-done.2
  159.9 0.0 copy-done.9
  159.9 0.0 slice-done.3
  159.9 0.0 slice-start.5
  159.9 0.0 slice-start
  159.9 2.6 fusion.11
  162.6 0.0 slice-done.4
  162.6 0.0 slice-start.1
  162.6 3.3 multiply_convert_fusion.1
  165.9 0.0 copy-start.13
  165.9 0.0 copy-start.14
  165.9 0.0 copy-start.15
  166.0 3.8 convolution_convert_fusion
  169.8 0.0 copy-done.14
  169.8 2.6 fusion.12
  172.5 3.7 add_convert_fusion.1
  176.2 106.0 %ffn_sums.1 = (bf16[4,2,48,2048]{3,2,1,0:T(8,128)(2,1)}, f32[2,48,2048]{2,1,0:T(8,128)}, f32[8,2048]{1,0:T(8,128)}, f32[256,1408]{1,0:T(8,128)}, f32[256,1408]{1...) custom-call(bf16[4,2,48,2048]{3,2,1,0:T(8,128)(2,1)} %bitcast.72, ...), custom_call_target="tpu_custom_call" | custom-call | bytes 80000000 | tf_op jit(solution)/shard_map/ffn_sums/pallas_call | solution.py:1134
  282.2 3.2 convolution_convert_fusion.2.grad_ref
  285.4 12.8 %attend_back.1 = (bf16[384,512]{1,0:T(8,128)(2,1)}, bf16[8,384,256]{2,1,0:T(8,128)(2,1)}) custom-call(s32[6]{0:T(128)} %lens_ref.11, s32[6]{0:T(128)} %flags_ref.11, s32[1]{0:T(128)} %bitcast.own_ref, bf16[384,512]{1,0:T(8,128)(2,1)} %get-tuple-element.38.query_ref, bf16[384,512]{1,0:T(8,128)(2,1)} %convolution_convert_fusion.2.grad_ref, ...), custom_call_target="tpu_custom_call" | custom-call | flops 3000000000 | bytes 20000000 | tf_op jit(solution)/shard_map/attend_back/pallas_call | solution.py:585
  298.2 20.4 %scatter_tok.1 = f32[384,256]{1,0:T(8,128)} custom-call(bf16[8,384,256]{2,1,0:T(8,128)(2,1)} %get-tuple-element.49.part_ref), custom_call_target="tpu_custom_call" | custom-call | bytes 10000000 | tf_op jit(solution)/shard_map/scatter_tok/pallas_call | solution.py:654
  318.6 0.0 copy-start.6
  318.6 1.0 slice.42
  319.6 1.1 fusion.6
  320.8 1.1 fusion.2
  321.9 0.9 pad_maximum_fusion.dqkv_ref
  322.7 0.6 fusion.8
  323.3 0.5 copy-done.5
  323.8 0.6 fusion.13
  324.4 1.0 copy-done.1
  325.4 2.2 add_convert_fusion
  327.5 95.9 %attn_sums.1 = (bf16[4,2,48,2048]{3,2,1,0:T(8,128)(2,1)}, f32[8,2048]{1,0:T(8,128)}, bf16[6,128,2048]{2,1,0:T(8,128)(2,1)}, f32[256,768]{1,0:T(8,128)}, f32[512,256]{1,0:T(8,128)}) custom-call(s32[6]{0:T(128)} %lens_ref.11, s32[6]{0:T(128)} %flags_ref.11, bf16[4,2,48,2048]{3,2,1,0:T(8,128)(2,1)} %bitcast.58, bf16[4,2,48,2048]{3,2,1,0:T(8,128)(2,1)} %bitcast.51, ...), custom_call_target="tpu_custom_call" | custom-call | bytes 80000000 | tf_op jit(solution)/shard_map/attn_sums/pallas_call | solution.py:1196
  423.5 1.7 fusion.5
  425.1 1.9 slice.35
  427.0 50.0 %undeal.1 = (bf16[6,128,2048]{2,1,0:T(8,128)(2,1)}, f32[8,256]{1,0:T(8,128)}) custom-call(s32[6]{0:T(128)} %lens_ref.11, s32[6]{0:T(128)} %flags_ref.11, bf16[3,128,2048]{2,1,0:T(8,128)(2,1)} %bitcast.66, bf16[6,128,2048]{2,1,0:T(8,128)(2,1)} %bitcast.57, f32[8,2048]{1,0:T(8,128)} %get-tuple-element.57.gains_ref), custom_call_target="tpu_custom_call" | custom-call | bytes 40000000 | tf_op jit(solution)/shard_map/undeal/pallas_call | solution.py:334
  477.0 1.3 fusion.7
  478.4 4.1 copy.30
  482.5 1.7 copy.31
  484.2 0.8 copy.32
  484.9 0.3 copy-done.12
  485.2 1.1 copy.33
  486.3 1.1 copy.34
  487.4 0.8 copy-done.10
  488.2 1.1 copy.35
  (29 shorter events, 0.1 us)
Async XLA Ops:
  0.6 85.1 %copy-start = (bf16[512,2048]{1,0:T(8,128)(2,1)S(1)}, bf16[512,2048]{1,0:T(8,128)(2,1)}, u32[]{:S(2)}) copy-start(bf16[512,2048]{1,0:T(8,128)(2,1)} %param.18) | copy-start | bytes 6291460
  152.1 7.8 %slice-start.2 = ((s8[5767168]{0:T(1024)(128)(4,1)}), s8[4194304]{0:T(1024)(128)(4,1)S(1)}, s32[]{:S(2)}) async-start(s8[5767168]{0:T(1024)(128)(4,1)} %bitcast.83), calls=%async_computation.2 | async-start | bytes 8388608
  154.0 5.9 %copy-start.2 = (bf16[3,128,2048]{2,1,0:T(8,128)(2,1)}, bf16[3,128,2048]{2,1,0:T(8,128)(2,1)S(1)}, u32[]{:S(2)}) copy-start(bf16[3,128,2048]{2,1,0:T(8,128)(2,1)S(1)} %multiply_convert_fusion) | copy-start | bytes 4718596
  154.0 5.9 %copy-start.9 = (bf16[4,2,48,2048]{3,2,1,0:T(8,128)(2,1)S(1)}, bf16[4,2,48,2048]{3,2,1,0:T(8,128)(2,1)}, u32[]{:S(2)}) copy-start(bf16[4,2,48,2048]{3,2,1,0:T(8,128)(2,1)} %get-tuple-element.42) | copy-start | bytes 4718596
  154.0 5.9 %slice-start.3 = ((s8[5767168]{0:T(1024)(128)(4,1)}), s8[1572864]{0:T(1024)(128)(4,1)S(1)}, s32[]{:S(2)}) async-start(s8[5767168]{0:T(1024)(128)(4,1)} %bitcast.83), calls=%async_computation.3 | async-start | bytes 3145728
  154.0 8.6 %slice-start.4 = ((s8[5767168]{0:T(1024)(128)(4,1)}), s8[4194304]{0:T(1024)(128)(4,1)S(1)}, s32[]{:S(2)}) async-start(s8[5767168]{0:T(1024)(128)(4,1)} %bitcast.85), calls=%async_computation.4 | async-start | bytes 8388608
  159.9 2.7 slice-start.5
  159.9 6.0 %slice-start = ((s8[5767168]{0:T(1024)(128)(4,1)}), s8[4194304]{0:T(1024)(128)(4,1)S(1)}, s32[]{:S(2)}) async-start(s8[5767168]{0:T(1024)(128)(4,1)} %bitcast.81), calls=%async_computation | async-start | bytes 8388608
  162.6 3.3 slice-start.1
  165.9 3.9 copy-start.13
  165.9 3.9 copy-start.14
  165.9 6.5 %copy-start.15 = (bf16[384,1408]{1,0:T(8,128)(2,1)}, bf16[384,1408]{1,0:T(8,128)(2,1)S(1)}, u32[]{:S(2)}) copy-start(bf16[384,1408]{1,0:T(8,128)(2,1)S(1)} %get-tuple-element.67.dup_ref) | copy-start | bytes 3244036
  298.2 22.6 %copy-start.7 = (f32[384,128]{1,0:T(8,128)S(1)}, f32[384,128]{1,0:T(8,128)}, u32[]{:S(2)}) copy-start(f32[384,128]{1,0:T(8,128)} %get-tuple-element.78.sin_ref) | copy-start | bytes 589828
  298.2 23.7 %copy-start.8 = (bf16[384,512]{1,0:T(8,128)(2,1)S(1)}, bf16[384,512]{1,0:T(8,128)(2,1)}, u32[]{:S(2)}) copy-start(bf16[384,512]{1,0:T(8,128)(2,1)} %get-tuple-element.48) | copy-start | bytes 1179652
  318.6 4.2 copy-start.3
  318.6 4.2 copy-start.6
  322.7 1.0 copy-start.5
  323.8 1.6 copy-start.1
  478.4 4.1 copy-start.4
  482.5 1.7 copy-start.16
  482.5 2.8 copy-start.12
  484.2 2.2 copy-start.11
  486.3 1.9 copy-start.10

commit v4 on v3

--- a/solution.py
+++ b/solution.py
@@ -13,6 +13,7 @@
 SLOTS = 3
 CHUNKS = 8
 HALVES = 2
+TILE = 16
 MESH = pl.DeviceIdType.MESH
 VMEM_BYTES = 60 * 2**20
 
@@ -69,11 +70,17 @@
         pl.semaphore_wait(barrier, len(peers) + 2)
 
 
-def run(*flows):
+def run(*flows, done=frozenset()):
     waiting = [[next(flow), number, flow] for number, flow in enumerate(flows)]
+
+    def order(entry):
+        step = entry[0] if isinstance(entry[0], tuple) else (entry[0], None)
+        return (step[1] is not None and step[1] not in done, step[0], entry[1])
+
     while waiting:
-        waiting.sort(key=lambda entry: entry[:2])
+        waiting.sort(key=order)
         entry = waiting[0]
+        assert not order(entry)[0]
         try:
             entry[0] = next(entry[2])
         except StopIteration:
@@ -231,11 +238,14 @@
     )(doc_lengths, keep_flags, blocks)
 
 
-def undeal_flow(lens_ref, flags_ref, kept_ref, home_ref, out_ref, scratch, pace=4.3):
+def undeal_flow(
+    lens_ref, flags_ref, kept_ref, out_ref, home, scratch, start=0.0, pace=4.3, key=None, lag=0.0
+):
     keep, send, recv, send_sem, recv_sem = scratch
     stages = recv.shape[0]
     own = lax.axis_index("tok")
-    blocks_here = home_ref.shape[0]
+    blocks_here = out_ref.shape[0]
+    planes = kept_ref.shape[2]
     rows = BLOCK // CHUNKS
     peers = bit_peers(stages)
     keeps, sends, finals = deal_tables(own, stages, blocks_here, lens_ref, flags_ref)
@@ -258,10 +268,15 @@
     last = stages - 1
     for stage in range(last, -2, -1):
         for chunk in range(CHUNKS):
-            yield 0.0 if stage == last else 1 + pace * (chunk + last - stage - (stage < 0))
+            half = chunk // planes
+            begin = start + lag * half
+            if stage == last:
+                yield (begin, None if key is None else key + (half,))
+            else:
+                yield begin + 1 + pace * (chunk + last - stage - (stage < 0))
             span = pl.ds(chunk * rows, rows)
             if stage == last:
-                options = [kept_ref[slot, span, :] for slot in range(SLOTS)]
+                options = [kept_ref[slot, half, chunk % planes] for slot in range(SLOTS)]
                 places = finals
             else:
                 copy(stage + 1, chunk).wait_recv()
@@ -270,9 +285,11 @@
                 ]
                 places = keeps[stage + 1] + sends[stage + 1]
             if stage < 0:
+                if chunk == 0:
+                    home.wait()
                 for place in range(blocks_here):
-                    home = home_ref[place, span, :]
-                    out_ref[place, span, :] = pick_place(places, options, place, home)
+                    value = out_ref[place, span, :]
+                    out_ref[place, span, :] = pick_place(places, options, place, value)
             else:
                 for slot in range(SLOTS):
                     send[stage, chunk, slot] = pick_place(
@@ -291,60 +308,78 @@
     lax.fori_loop(0, CHUNKS, drain, 0)
 
 
-def undeal_body(lens_ref, flags_ref, kept_ref, home_ref, gains_ref, out_ref, sum_ref, *scratch):
-    undealing = scratch[:5]
-    gain_recv, gain_send_sem, gain_recv_sem = scratch[5:]
+def gain_flow(gains_ref, sum_ref, scratch, start, key=None):
+    gain_recv, gain_send_sem, gain_recv_sem = scratch
     own, plane = lax.axis_index("tok"), lax.axis_index("tp")
     devices = gain_recv.shape[0]
     share = sum_ref.shape[1]
-    greet([(own ^ step, plane) for step in range(1, devices)])
 
     def portion(there):
-        if share % 128 == 0 and share < gains_ref.shape[1]:
+        if share < gains_ref.shape[1]:
             return gains_ref.at[:, pl.ds(pl.multiple_of(there * share, share), share)]
         return gains_ref
 
-    def gain_copy(step):
-        there = own ^ step
+    def copy(step):
         return pltpu.make_async_remote_copy(
-            src_ref=portion(there),
+            src_ref=portion(own ^ step),
             dst_ref=gain_recv.at[step],
             send_sem=gain_send_sem.at[step],
             recv_sem=gain_recv_sem.at[step],
-            device_id=(there, plane),
+            device_id=(own ^ step, plane),
             device_id_type=MESH,
         )
 
+    yield (start, key)
     for step in range(1, devices):
-        gain_copy(step).start()
-    run(undeal_flow(lens_ref, flags_ref, kept_ref, home_ref, out_ref, undealing))
+        copy(step).start()
+    yield 2e5
     total = portion(own)[...]
     for step in range(1, devices):
-        gain_copy(step).wait()
+        copy(step).wait()
         total = total + gain_recv[step]
     sum_ref[...] = total
+
+
+def gain_share(width, devices):
+    share = width // devices
+    return share if share % 128 == 0 else width
+
+
+def gain_scratch(devices, share):
+    return [pltpu.VMEM((devices, 8, share), F32)] + [pltpu.SemaphoreType.DMA((devices,))] * 2
+
+
+def all_peers():
+    own, plane = lax.axis_index("tok"), lax.axis_index("tp")
+    return [(own ^ step, plane) for step in range(1, lax.axis_size("tok"))]
+
+
+def undeal_body(lens_ref, flags_ref, kept_ref, home_ref, gains_ref, out_ref, sum_ref, home_sem, *scratch):
+    home = pltpu.make_async_copy(home_ref, out_ref, home_sem)
+    home.start()
+    greet(all_peers())
+    run(
+        undeal_flow(lens_ref, flags_ref, kept_ref, out_ref, home, scratch[:5]),
+        gain_flow(gains_ref, sum_ref, scratch[5:], 0.0),
+    )
 
 
 def undeal(doc_lengths, keep_flags, kept, home, gains, collective_id):
     stages = stages_of("tok")
     devices = 1 << stages
-    width = kept.shape[2]
-    share = width // devices
-    share = share if share % 128 == 0 else width
+    width = kept.shape[-1]
+    share = gain_share(width, devices)
     return pl.pallas_call(
         undeal_body,
         out_shape=(
             jax.ShapeDtypeStruct(home.shape, home.dtype),
             jax.ShapeDtypeStruct((8, share), F32),
         ),
-        in_specs=[smem(), smem(), vmem(), vmem(), vmem()],
+        in_specs=[smem(), smem(), vmem(), pl.BlockSpec(memory_space=pl.ANY), vmem()],
         out_specs=(vmem(), vmem()),
-        scratch_shapes=deal_scratch(stages, width, kept.dtype)
-        + [
-            pltpu.VMEM((devices, 8, share), F32),
-            pltpu.SemaphoreType.DMA((devices,)),
-            pltpu.SemaphoreType.DMA((devices,)),
-        ],
+        scratch_shapes=[pltpu.SemaphoreType.DMA]
+        + deal_scratch(stages, width, kept.dtype)
+        + gain_scratch(devices, share),
         compiler_params=params(collective_id),
         cost_estimate=cost(0, 40_000_000),
         name="undeal",
@@ -684,13 +719,12 @@
     )
 
 
-def line_gather(own, plane, planes, arrays, start, pace):
+def line_gather(own, plane, planes, arrays, start, pace, ready=None):
     last = planes - 1
 
     def move(array, index, step):
-        out, rest, send_sem, recv_sem = array
-        shard = out.at[(index,) + rest]
-        return line_copy(own, plane, step, shard, shard, send_sem, recv_sem, index)
+        shard, send_sem, recv_sem = array
+        return line_copy(own, plane, step, shard(index), shard(index), send_sem, recv_sem, index)
 
     for step in range(1, planes + 1):
         yield start + pace * (step - 1)
@@ -718,6 +752,9 @@
                     def _():
                         move(array, after, -1).start()
 
+    if ready is not None:
+        ready()
+    yield start + pace * (planes + 1)
     for index in range(planes):
 
         @pl.when((index <= plane) & (plane < last))
@@ -747,7 +784,7 @@
 
     def add(index):
         send[index, half] = (
-            part[index, half].astype(F32) + recv[index, half].astype(F32)
+            part[:, half, index].astype(F32) + recv[index, half].astype(F32)
         ).astype(send.dtype)
 
     for step in range(1, planes):
@@ -758,7 +795,7 @@
         def _():
             @pl.when(plane == 0)
             def _():
-                send[upper, half] = part[upper, half]
+                send[upper, half] = part[:, half, upper]
 
             @pl.when(plane > 0)
             def _():
@@ -771,7 +808,7 @@
         def _():
             @pl.when(plane == last)
             def _():
-                send[lower, half] = part[lower, half]
+                send[lower, half] = part[:, half, lower]
 
             @pl.when(plane < last)
             def _():
@@ -781,7 +818,7 @@
             left(lower).start()
 
     yield start + pace * (planes - 1)
-    total[half] = part[plane, half].astype(F32)
+    total[half] = part[:, half, plane].astype(F32)
 
     @pl.when(plane > 0)
     def _():
@@ -805,14 +842,28 @@
             left(index).wait_send()
 
 
-def sum_flows(part_ref, gathered, scratch, math_rule, start=0.0, pace=8.7, extra=None):
-    total, send, recv, send_sem, recv_sem, gather_send_sem, gather_recv_sem = scratch
-    planes = part_ref.shape[0]
+def gather_flows(gathered, scratch, start, pace, done=None, key=None):
+    send_sem, recv_sem = scratch
+    planes = gathered.shape[2]
     own, plane = lax.axis_index("tok"), lax.axis_index("tp")
-    lag = pace / 2
 
     def flow(half):
-        begin = start + lag * half
+        array = (lambda index: gathered.at[:, half, index], send_sem.at[half], recv_sem.at[half])
+        ready = None if key is None else lambda: done.add(key + (half,))
+        yield from line_gather(own, plane, planes, [array], start + pace / 2 * half, pace, ready)
+
+    return [flow(half) for half in range(HALVES)]
+
+
+def sum_flows(
+    part_ref, gathered, scratch, math_rule, start=0.0, pace=8.7, extra=None, done=None, key=None
+):
+    total, send, recv, send_sem, recv_sem = scratch[:5]
+    planes = part_ref.shape[2]
+    own, plane = lax.axis_index("tok"), lax.axis_index("tp")
+
+    def flow(half):
+        begin = start + pace / 2 * half
         reducing = line_reduce(
             own, plane, planes, half, part_ref, total, send, recv,
             send_sem.at[half], recv_sem.at[half], begin, pace,
@@ -820,102 +871,98 @@
         for number in range(planes):
             yield next(reducing)
         next(reducing)
-        math_rule(plane, half, total, gathered)
-        arrays = [(gathered, (half,), gather_send_sem.at[half], gather_recv_sem.at[half])]
-        if extra is not None and half == HALVES - 1:
-            arrays.append(extra)
-        yield from line_gather(own, plane, planes, arrays, begin + pace * (planes - 1), pace)
+        math_rule(plane, half, total)
+        if gathered is not None:
+            arrays = [
+                (
+                    lambda index: gathered.at[:, half, index],
+                    scratch[5].at[half],
+                    scratch[6].at[half],
+                )
+            ]
+            if extra is not None and half == HALVES - 1:
+                arrays.append(extra)
+            ready = None if key is None else lambda: done.add(key + (half,))
+            yield from line_gather(
+                own, plane, planes, arrays, begin + pace * (planes - 1), pace, ready
+            )
         for _ in reducing:
             pass
 
     return [flow(half) for half in range(HALVES)]
 
 
-def sum_scratch(planes, shard, width, kind):
-    rows = shard // HALVES
+def sum_scratch(planes, width, gathers=True):
+    shard = (HALVES, SLOTS, TILE, width)
     return [
-        pltpu.VMEM((HALVES, rows, width), F32),
-        pltpu.VMEM((planes, HALVES, rows, width), kind),
-        pltpu.VMEM((planes + 1, HALVES, rows, width), kind),
-    ] + [pltpu.SemaphoreType.DMA((HALVES, 2, planes))] * 4
-
-
-def by_tiles(rows, step):
-    lax.fori_loop(0, rows // 16, lambda i, c: (step(pl.ds(pl.multiple_of(i * 16, 16), 16)), c)[1], 0)
-
-
-def norm_math(x_ref, gain_ref, hidden_ref, inv_ref):
-    def rule(plane, half, total, gathered):
-        def tile(rows):
-            hidden = x_ref[plane, half, rows, :].astype(F32) + total[half, rows, :]
+        pltpu.VMEM(shard, F32),
+        pltpu.VMEM((planes,) + shard, BF16),
+        pltpu.VMEM((planes + 1,) + shard, BF16),
+    ] + [pltpu.SemaphoreType.DMA((HALVES, 2, planes))] * (4 if gathers else 2)
+
+
+def norm_math(x_ref, gain_ref, hidden_ref, inv_ref, gathered):
+    def rule(plane, half, total):
+        for block in range(SLOTS):
+            hidden = x_ref[block, half, plane].astype(F32) + total[half, block]
             inv = lax.rsqrt(jnp.mean(hidden * hidden, axis=1, keepdims=True) + norm_eps)
-            hidden_ref[half, rows, :] = hidden
-            inv_ref[half, rows, :] = inv
-            gathered[plane, half, rows, :] = (hidden * inv * gain_ref[...]).astype(BF16)
-
-        by_tiles(total.shape[1], tile)
+            hidden_ref[half, block] = hidden
+            inv_ref[half, block] = inv
+            gathered[block, half, plane] = (hidden * inv * gain_ref[...]).astype(BF16)
 
     return rule
 
 
-def ffn_math(hidden_ref, inv_ref, dy_ref, gain_ref, grad_ref, gains_ref):
-    def rule(plane, half, total, gathered):
+def ffn_math(hidden_ref, inv_ref, dy_ref, gain_ref, grad_ref, gains_ref, gathered):
+    def rule(plane, half, total):
         if half == 0:
             gains_ref[...] = jnp.zeros_like(gains_ref)
-
-        def tile(rows):
-            dn = total[half, rows, :]
-            hidden = hidden_ref[half, rows, :]
-            inv = inv_ref[half, rows, :]
+        for block in range(SLOTS):
+            dn = total[half, block]
+            hidden = hidden_ref[half, block]
+            inv = inv_ref[half, block]
             weighted = gain_ref[...] * dn
             mean = jnp.mean(weighted * hidden, axis=1, keepdims=True)
             grad = (
-                keep_scale * dy_ref[plane, half, rows, :].astype(F32)
+                keep_scale * dy_ref[block, half, plane].astype(F32)
                 + inv * weighted
                 - hidden * (inv * inv * inv * mean)
             )
-            grad_ref[half, rows, :] = grad
-            gathered[plane, half, rows, :] = grad.astype(BF16)
+            grad_ref[half, block] = grad
+            gathered[block, half, plane] = grad.astype(BF16)
             gains_ref[0:1, :] += jnp.sum(dn * hidden * inv, axis=0, keepdims=True)
 
-        by_tiles(total.shape[1], tile)
-
     return rule
 
 
-def mixed_math(hidden_ref, x_ref):
-    def rule(plane, half, total, gathered):
-        def tile(rows):
-            x = x_ref[plane, half, rows, :].astype(F32)
-            branch = (hidden_ref[half, rows, :] - x) + total[half, rows, :]
-            gathered[plane, half, rows, :] = (x + keep_scale * branch).astype(BF16)
-
-        by_tiles(total.shape[1], tile)
+def mixed_math(hidden_ref, x_ref, mixed_ref):
+    def rule(plane, half, total):
+        for block in range(SLOTS):
+            x = x_ref[block, half, plane].astype(F32)
+            branch = (hidden_ref[half, block] - x) + total[half, block]
+            mixed_ref[half, block] = (x + keep_scale * branch).astype(BF16)
 
     return rule
 
 
-def attn_math(x_ref, inv_ref, dy_ref, grad_ref, gain_ref, ffn_gains_ref, gains_all):
-    def rule(plane, half, total, gathered):
+def attn_math(x_ref, inv_ref, dy_ref, grad_ref, gain_ref, ffn_gains_ref, gains_all, gathered):
+    def rule(plane, half, total):
         if half == 0:
             gains_all[plane] = ffn_gains_ref[...]
-
-        def tile(rows):
-            dn = total[half, rows, :]
-            x = x_ref[plane, half, rows, :].astype(F32)
-            inv = inv_ref[plane, half, rows, :]
+        for block in range(SLOTS):
+            dn = total[half, block]
+            x = x_ref[block, half, plane].astype(F32)
+            inv = inv_ref[block, half, plane]
             weighted = gain_ref[...] * dn
             mean = jnp.mean(weighted * x, axis=1, keepdims=True)
             grad = (
-                (1.0 - keep_scale) * dy_ref[plane, half, rows, :].astype(F32)
-                + grad_ref[half, rows, :]
+                (1.0 - keep_scale) * dy_ref[block, half, plane].astype(F32)
+                + grad_ref[half, block]
                 + inv * weighted
                 - x * (inv * inv * inv * mean)
             )
-            gathered[plane, half, rows, :] = grad.astype(BF16)
+            gathered[block, half, plane] = grad.astype(BF16)
             gains_all[plane, 1:2, :] += jnp.sum(dn * x * inv, axis=0, keepdims=True)
-
-        by_tiles(total.shape[1], tile)
 
     return rule
 
@@ -926,33 +973,35 @@
 ):
     dealing, summing = scratch[:5], scratch[5:]
     greet(bit_peers(dealing[1].shape[0]), line=True)
+    rule = norm_math(x_ref, gain_ref, hidden_ref, inv_ref, gathered)
     run(
-        *sum_flows(part_ref, gathered, summing, norm_math(x_ref, gain_ref, hidden_ref, inv_ref)),
+        *sum_flows(part_ref, gathered, summing, rule),
         deal_flow(lens_ref, flags_ref, own_ref, out_ref, dealing),
     )
 
 
 def deal_sum(doc_lengths, keep_flags, blocks, part, x, gain, collective_id):
-    planes, halves, rows, width = part.shape
+    planes, width = part.shape[2], part.shape[4]
+    shard = (HALVES, SLOTS, TILE)
     return pl.pallas_call(
         deal_sum_body,
         out_shape=(
             jax.ShapeDtypeStruct((SLOTS, BLOCK, width), blocks.dtype),
             jax.ShapeDtypeStruct(part.shape, BF16),
-            jax.ShapeDtypeStruct((halves, rows, width), F32),
-            jax.ShapeDtypeStruct((halves, rows, 1), F32),
+            jax.ShapeDtypeStruct(shard + (width,), F32),
+            jax.ShapeDtypeStruct(shard + (1,), F32),
         ),
         in_specs=[smem(), smem()] + [vmem()] * 4,
         out_specs=(vmem(),) * 4,
         scratch_shapes=deal_scratch(stages_of("tok"), width, blocks.dtype)
-        + sum_scratch(planes, halves * rows, width, BF16),
+        + sum_scratch(planes, width),
         compiler_params=params(collective_id),
         cost_estimate=cost(0, 60_000_000),
         name="deal_sum",
     )(doc_lengths, keep_flags, blocks, part, x, gain)
 
 
-def spread_flow(units, outs, scratch, pace):
+def spread_flow(units, outs, scratch, pace, start=0.0):
     own, plane = lax.axis_index("tok"), lax.axis_index("tp")
     count = len(units)
     boxes, inboxes, core_inboxes = scratch[:count], scratch[count : 2 * count], scratch[2 * count : 3 * count]
@@ -1025,15 +1074,15 @@
     chip_order = sorted(range(chips), key=lambda chip: -bin(chip).count("1"))
     for unit in range(count):
         for chip in chip_order:
-            yield 0.1 + 3 * unit
+            yield start + 0.1 + 3 * unit
             offer(unit, chip)
         for chip in chip_order:
-            yield 3.2 + 3 * unit
+            yield start + 3.2 + 3 * unit
             collect(unit, chip)
     for stage in range(stages):
         for unit in range(count):
             for half in range(2):
-                yield 6.0 + pace * (unit + 1 + count * stage)
+                yield start + 6.0 + pace * (unit + 1 + count * stage)
                 take(unit, stage, half)
     for unit in range(count):
         for half in range(2):
@@ -1093,9 +1142,9 @@
 def ffn_sums_body(
     part_ref, hidden_ref, inv_ref, dy_ref, gain_ref, normed_ref, dgate_ref, dup_ref, inner_ref, dm_ref,
     mixed_part_ref, x_ref,
-    gathered, grad_ref, gains_ref, gate_out, up_out, down_out, mixed_gathered, *scratch,
+    gathered, grad_ref, gains_ref, gate_out, up_out, down_out, mixed_ref, *scratch,
 ):
-    summing, mixing, spreading = scratch[:7], scratch[7:14], scratch[14:]
+    summing, mixing, spreading = scratch[:7], scratch[7:12], scratch[12:]
     own, plane = lax.axis_index("tok"), lax.axis_index("tp")
     devices = lax.axis_size("tok")
     share = normed_ref.shape[1] // devices
@@ -1106,9 +1155,9 @@
             part_ref,
             gathered,
             summing,
-            ffn_math(hidden_ref, inv_ref, dy_ref, gain_ref, grad_ref, gains_ref),
+            ffn_math(hidden_ref, inv_ref, dy_ref, gain_ref, grad_ref, gains_ref, gathered),
         ),
-        *sum_flows(mixed_part_ref, mixed_gathered, mixing, mixed_math(hidden_ref, x_ref), 27.0, 11.0),
+        *sum_flows(mixed_part_ref, None, mixing, mixed_math(hidden_ref, x_ref, mixed_ref), 27.0, 11.0),
         spread_flow(
             [
                 rows_by_owner(normed_ref, dgate_ref, share),
@@ -1125,8 +1174,7 @@
 def ffn_sums(
     part, hidden, inv, dy, gain, normed, dgate, dup, inner, dm, mixed_part, x, collective_id
 ):
-    planes, halves, rows, width = part.shape
-    shard = halves * rows
+    planes, width = part.shape[2], part.shape[4]
     devices = lax.axis_size("tok")
     share = width // devices
     wide = dgate.shape[1]
@@ -1139,82 +1187,143 @@
             jax.ShapeDtypeStruct((8, width), F32),
         ]
         + [jax.ShapeDtypeStruct(shape, F32) for shape in shapes]
-        + [jax.ShapeDtypeStruct(part.shape, BF16)],
+        + [jax.ShapeDtypeStruct(hidden.shape, BF16)],
         in_specs=[vmem()] * 12,
         out_specs=[vmem()] * 7,
-        scratch_shapes=sum_scratch(planes, shard, width, BF16) * 2 + spread_scratch(shapes, devices),
+        scratch_shapes=sum_scratch(planes, width)
+        + sum_scratch(planes, width, False)
+        + spread_scratch(shapes, devices),
         compiler_params=params(collective_id),
         cost_estimate=cost(0, 80_000_000),
         name="ffn_sums",
     )(part, hidden, inv, dy, gain, normed, dgate, dup, inner, dm, mixed_part, x)
 
 
+def together():
+    return stages_of("tok") <= 3
+
+
 def attn_sums_body(
-    lens_ref, flags_ref, part_ref, x_ref, inv_ref, dy_ref, grad_ref, gain_ref, ffn_gains_ref,
-    kept_ref, home_ref, normed_ref, dqkv_ref, attended_ref, da_ref,
-    gathered, gains_ref, mixed_ref, qkv_out, out_out, *scratch,
+    lens_ref, flags_ref, part_ref, mixed_ref, x_ref, inv_ref, dy_ref, grad_ref, gain_ref, ffn_gains_ref,
+    normed_ref, dqkv_ref, attended_ref, da_ref, home_ref, grad_home_ref, *refs,
 ):
-    summing, undealing, scratch = scratch[:7], scratch[7:12], scratch[12:]
-    gains_all, gains_sems, spreading = scratch[0], scratch[1:3], scratch[3:]
-    planes = part_ref.shape[0]
+    both = together()
+    gathered, gains_ref, mixed_out, qkv_out, out_out = refs[:5]
+    refs = refs[5:]
+    if both:
+        grad_out, gathered = gathered, refs[0]
+        gain_sums, gains_ref = gains_ref, refs[1]
+        refs = refs[2:]
+    summing, undealing, refs = refs[:7], refs[7:12], refs[12:]
+    mixed_all, mixed_sems, home_sems = refs[0], refs[1:3], refs[3]
+    gains_all, gains_sems, refs = refs[4], refs[5:7], refs[7:]
+    planes = part_ref.shape[2]
+    plane = lax.axis_index("tp")
     share = normed_ref.shape[1] // lax.axis_size("tok")
-    greet(bit_peers(stages_of("tok")), True)
-    run(
+    home = pltpu.make_async_copy(home_ref, mixed_out, home_sems.at[0])
+    home.start()
+    if both:
+        grad_home = pltpu.make_async_copy(grad_home_ref, grad_out, home_sems.at[1])
+        grad_home.start()
+        grad_undealing, gaining, refs = refs[:5], refs[5:8], refs[8:]
+    greet(all_peers() if both else bit_peers(stages_of("tok")), True)
+    for half in range(HALVES):
+        mixed_all[:, half, plane] = mixed_ref[half]
+    done = set()
+
+    def sum_gains():
+        yield (70.0, ("grad", HALVES - 1))
+        total = gains_all[0]
+        for index in range(1, planes):
+            total = total + gains_all[index]
+        gains_ref[...] = total
+        done.add(("gains",))
+
+    flows = [
+        *gather_flows(mixed_all, mixed_sems, 0.0, 8.7, done, ("mixed",)),
         *sum_flows(
             part_ref,
             gathered,
             summing,
-            attn_math(x_ref, inv_ref, dy_ref, grad_ref, gain_ref, ffn_gains_ref, gains_all),
-            extra=(gains_all, ()) + gains_sems,
+            attn_math(
+                x_ref, inv_ref, dy_ref, grad_ref, gain_ref, ffn_gains_ref, gains_all, gathered
+            ),
+            9.0,
+            10.0,
+            (lambda index: gains_all.at[index],) + gains_sems,
+            done,
+            ("grad",),
         ),
-        undeal_flow(lens_ref, flags_ref, kept_ref, home_ref, mixed_ref, undealing, 7.0),
         spread_flow(
             [
                 rows_by_owner(normed_ref, dqkv_ref, share),
                 columns_by_owner(attended_ref, da_ref, share),
             ],
             [qkv_out, out_out],
-            spreading,
-            15.0,
+            refs,
+            9.0,
         ),
-    )
-    total = gains_all[0]
-    for index in range(1, planes):
-        total = total + gains_all[index]
-    gains_ref[...] = total
+        undeal_flow(
+            lens_ref, flags_ref, mixed_all, mixed_out, home, undealing, 28.0, 4.5, ("mixed",), 6.0
+        ),
+        sum_gains(),
+    ]
+    if both:
+        flows += [
+            undeal_flow(
+                lens_ref, flags_ref, gathered, grad_out, grad_home, grad_undealing,
+                55.0, 4.5, ("grad",), 8.0,
+            ),
+            gain_flow(gains_ref, gain_sums, gaining, 72.0, ("gains",)),
+        ]
+    run(*flows, done=done)
 
 
 def attn_sums(
-    doc_lengths, keep_flags, part, x, inv, dy, grad, gain, ffn_gains, kept, home, normed, dqkv,
-    attended, da, collective_id,
+    doc_lengths, keep_flags, part, mixed, x, inv, dy, grad, gain, ffn_gains, normed, dqkv, attended,
+    da, home, grad_home, collective_id,
 ):
-    planes, halves, rows, width = part.shape
-    shard = halves * rows
+    planes, width = part.shape[2], part.shape[4]
     devices = lax.axis_size("tok")
     share = width // devices
     shapes = [(share, dqkv.shape[1]), (attended.shape[1], share)]
-    return pl.pallas_call(
+    both = together()
+    rows_shape = jax.ShapeDtypeStruct(part.shape, BF16)
+    gains_shape = jax.ShapeDtypeStruct((8, width), F32)
+    blocks_shape = jax.ShapeDtypeStruct(home.shape, BF16)
+    gain_part = gain_share(width, devices)
+    first = (
+        [blocks_shape, jax.ShapeDtypeStruct((8, gain_part), F32)] if both else [rows_shape, gains_shape]
+    )
+    dealing = deal_scratch(stages_of("tok"), width, BF16)
+    grads, gains, mixed_blocks, qkv, out = pl.pallas_call(
         attn_sums_body,
-        out_shape=[
-            jax.ShapeDtypeStruct(part.shape, BF16),
-            jax.ShapeDtypeStruct((8, width), F32),
-            jax.ShapeDtypeStruct(home.shape, BF16),
-        ]
+        out_shape=first
+        + [blocks_shape]
         + [jax.ShapeDtypeStruct(shape, F32) for shape in shapes],
-        in_specs=[smem(), smem()] + [vmem()] * 13,
+        in_specs=[smem(), smem()] + [vmem()] * 12 + [pl.BlockSpec(memory_space=pl.ANY)] * 2,
         out_specs=[vmem()] * 5,
-        scratch_shapes=sum_scratch(planes, shard, width, BF16)
-        + deal_scratch(stages_of("tok"), width, BF16)
-        + [pltpu.VMEM((planes, 8, width), F32)]
+        scratch_shapes=(
+            [pltpu.VMEM(part.shape, BF16), pltpu.VMEM((8, width), F32)] if both else []
+        )
+        + sum_scratch(planes, width)
+        + dealing
+        + [pltpu.VMEM(part.shape, BF16)]
+        + [pltpu.SemaphoreType.DMA((HALVES, 2, planes))] * 2
+        + [pltpu.SemaphoreType.DMA((2,)), pltpu.VMEM((planes, 8, width), F32)]
         + line_sems(planes)
+        + (dealing + gain_scratch(devices, gain_part) if both else [])
         + spread_scratch(shapes, devices),
         compiler_params=params(collective_id),
         cost_estimate=cost(0, 80_000_000),
         name="attn_sums",
     )(
-        doc_lengths, keep_flags, part, x, inv, dy, grad, gain, ffn_gains, kept, home, normed, dqkv,
-        attended, da,
-    )
+        doc_lengths, keep_flags, part, mixed, x, inv, dy, grad, gain, ffn_gains, normed, dqkv, attended,
+        da, home, grad_home,
+    )
+    if not both:
+        grads, gains = undeal(doc_lengths, keep_flags, grads, grad_home, gains, collective_id + 1)
+    return mixed_blocks, grads, gains, qkv, out
 
 
 def rotary_tables(doc_lengths, keep_flags, ranks):
@@ -1266,8 +1375,6 @@
     own_index = lax.axis_index("tok")
     blocks_here = length // BLOCK
     kept_here = blocks_here // 2
-    total_blocks = blocks_here * devices
-    kept_total = kept_here * devices
     rows = kept_here * BLOCK
     token_blocks = tokens.reshape(blocks_here, BLOCK, model_width)
     grad_blocks = cotangent.reshape(blocks_here, BLOCK, model_width)
@@ -1282,10 +1389,8 @@
     )
     attended, attended_wide, log_totals = attend(doc_lengths, keep_flags, own, queries, kv_all)
 
-    shard = rows // planes
-
     def by_plane(array):
-        return array.reshape(planes, HALVES, shard // HALVES, array.shape[1])
+        return array.reshape(kept_here, HALVES, planes, TILE, array.shape[1])
 
     x_planes = by_plane(rows_x)
     rows_dy, normed_two, hidden_res, inv_two = deal_sum(
@@ -1352,31 +1457,24 @@
         + over_columns(grad_key_pre, w_key)
         + over_columns(grad_value_pre, w_value)
     ).astype(jnp.bfloat16)
-    grad_rows, gains, mixed, grad_qkv, grad_out = attn_sums(
+    mixed, token_grad, gain_sums, grad_qkv, grad_out = attn_sums(
         doc_lengths,
         keep_flags,
         by_plane(part_one),
+        mixed_rows,
         x_planes,
         by_plane(inv_one),
         dy_planes,
         grad_hidden,
         gain_attn.reshape(1, -1),
         gains_ffn,
-        mixed_rows.reshape(kept_here, BLOCK, model_width),
-        token_blocks,
         normed_one,
         jnp.concatenate([grad_query_pre, grad_key_pre, grad_value_pre], axis=1),
         attended,
         grad_a,
+        token_blocks,
+        grad_blocks,
         6,
-    )
-    token_grad, gain_sums = undeal(
-        doc_lengths,
-        keep_flags,
-        grad_rows.reshape(kept_here, BLOCK, model_width),
-        grad_blocks,
-        gains,
-        9,
     )
     own_share = model_width // devices
     if gain_sums.shape[1] != own_share:

time: 499 us -> 450 us (0.902)
  Pallas kernels: 430 us -> 382 us
    pallas_call x2 -> x1, Pallas kernels: 146 us -> 116 us  [attn_sums(): pl.pallas_call(attn_sums_body, out_shape=first + [blocks_shape] + [jax.Sh...]
    pallas_call x1, Pallas kernels: 106 us -> 85.8 us  [ffn_sums(): pl.pallas_call(ffn_sums_body, out_shape=[jax.ShapeDtypeStruct(part.shape,...]
where the time goes in v4:
time: 450 us; the launch traced here: 441 us
  Pallas kernels  382 us (85%)
  matrix products  31.5 us (7%)
  local copies, waits for them, and re-layouts  18.8 us (4%)
  other arithmetic  6.86 us (2%)
    pallas_call x1, Pallas kernels, attn_sums(): pl.pallas_call(attn_sums_body, out_shape=first + [blocks_shape] + [jax.Sh...  116 us
    pallas_call x1, Pallas kernels, ffn_sums(): pl.pallas_call(ffn_sums_body, out_shape=[jax.ShapeDtypeStruct(part.shape,...  85.8 us
    pallas_call x1, Pallas kernels, deal_sum(): pl.pallas_call(deal_sum_body, out_shape=(jax.ShapeDtypeStruct((SLOTS, BLO...  61.7 us
    pallas_call x1, Pallas kernels, deal(): pl.pallas_call(deal_body, out_shape=jax.ShapeDtypeStruct((SLOTS, BLOCK, w...  48.9 us
    pallas_call x1, Pallas kernels, project(): pl.pallas_call(project_body, out_shape=(jax.ShapeDtypeStruct(x.shape, BF1...  22.1 us
    dot_general x7, matrix products, over_columns(): lax.dot_general(left, right, (((1,), (1,)), ((), ())), preferred_element_...  18.7 us
    pallas_call x1, Pallas kernels, attend_back(): pl.pallas_call(attend_back_body, out_shape=(jax.ShapeDtypeStruct(query.sh...  16.9 us
    pallas_call x1, Pallas kernels, scatter_tok(): pl.pallas_call(scatter_tok_body, out_shape=jax.ShapeDtypeStruct(shard, F3...  15.7 us

profile of v4, /device:TPU:1, one launch (start us, length us, event | category | flops | bytes accessed | tf_op | source)
XLA Modules:
  0.0 441.1 jit_solution(4784219802760902256)
XLA Ops:
  0.6 0.0 copy-start
  0.7 0.8 fusion.4
  1.5 0.2 reduce-window.8
  1.7 0.2 select_reduce_fusion
  1.9 0.1 convert_bitcast_fusion
  2.0 0.8 multiply_sine_fusion
  2.7 0.9 pad_maximum_fusion.1
  3.7 48.9 %deal.1 = bf16[3,128,2048]{2,1,0:T(8,128)(2,1)} custom-call(s32[6]{0:T(128)} %lens_ref.9, s32[6]{0:T(128)} %flags_ref.9, bf16[6,128,2048]{2,1,0:T(8,128)(2,1)} %bitcast.52), custom_call_target="tpu_custom_call" | custom-call | bytes 40000000 | tf_op jit(solution)/shard_map/deal/pallas_call | solution.py:229
  52.6 22.1 %project.1 = (bf16[384,2048]{1,0:T(8,128)(2,1)}, f32[384,1]{1,0:T(8,128)}, bf16[384,512]{1,0:T(8,128)(2,1)}, bf16[8,384,256]{2,1,0:T(8,128)(2,1)}) custom-call(bf16[384,2048]{1,0:T(8,128)(2,1)} %bitcast.46, f32[1,2048]{1,0:T(1,128)} %bitcast.70, bf16[2048,512]{1,0:T(8,128)(2,1)} %w_query_ref.1, bf16[2048,128]{1,0:T(8,128)(2,1)} %w_key_ref.1, ...), custom_call_target="tpu_custom_call" | custom-call | bytes 30000000 | tf_op jit(solution)/shard_map/project/pallas_call | solution.py:469
  74.7 15.3 %attend.1 = (bf16[384,512]{1,0:T(8,128)(2,1)}, f32[3,128,512]{2,1,0:T(8,128)}, f32[3,8,512]{2,1,0:T(8,128)}) custom-call(s32[6]{0:T(128)} %lens_ref.9, s32[6]{0:T(128)} %flags_ref.9, s32[1]{0:T(128)} %bitcast.own_ref, bf16[384,512]{1,0:T(8,128)(2,1)} %get-tuple-element.36.query_ref, bf16[8,384,256]{2,1,0:T(8,128)(2,1)} %get-tuple-element.37.kv_ref), custom_call_target="tpu_custom_call" | custom-call | flops 1000000000 | bytes 10000000 | tf_op jit(solution)/shard_map/attend/pallas_call | solution.py:558
  90.0 0.0 copy-done
  90.0 3.1 convolution_convert_fusion.1
  93.1 61.7 %deal_sum.1 = (bf16[3,128,2048]{2,1,0:T(8,128)(2,1)}, bf16[3,2,4,16,2048]{4,3,2,1,0:T(8,128)(2,1)}, f32[2,3,16,2048]{3,2,1,0:T(8,128)}, f32[2,3,16,1]{3,2,1,0:T(8,128)}) custom-call(s32[6]{0:T(128)} %lens_ref.9, s32[6]{0:T(128)} %flags_ref.9, bf16[6,128,2048]{2,1,0:T(8,128)(2,1)} %bitcast.54, bf16[3,2,4,16,2048]{4,3,2,1,0:T(8,128)(2,1)} %bitcast.61, ...), custom_call_target="tpu_custom_call" | custom-call | bytes 60000000 | tf_op jit(solution)/shard_map/deal_sum/pallas_call | solution.py:986
  154.8 0.0 slice-start.2
  154.8 1.9 multiply_convert_fusion
  156.7 0.0 copy-start.2
  156.7 0.0 copy-start.9
  156.7 0.0 slice-start.3
  156.7 0.0 slice-start.4
  156.7 5.8 %fusion.10 = f32[384,1408]{1,0:T(8,128)S(1)} fusion(bf16[384,2048]{1,0:T(8,128)(2,1)S(1)} %bitcast.56, bf16[1408,2048]{1,0:T(8,128)(2,1)} %param.22), kind=kOutput, calls=%fused_computation.37 | convolution fusion | flops 2214592512 | bytes 9502720 | tf_op jit(solution)/shard_map/dot_general | solution.py:1351
  162.6 0.0 copy-done.2
  162.6 0.0 slice-done.2
  162.6 0.0 copy-done.9
  162.6 0.0 slice-done.3
  162.6 0.0 slice-start.5
  162.7 0.0 slice-start
  162.7 2.6 fusion.11
  165.3 0.0 slice-start.1
  165.4 3.3 multiply_convert_fusion.1
  168.6 0.0 copy-start.13
  168.6 0.0 copy-start.14
  168.7 0.0 copy-start.15
  168.7 3.8 convolution_convert_fusion
  172.5 2.6 fusion.12
  175.2 3.7 add_convert_fusion.1
  178.9 85.8 %ffn_sums.1 = (bf16[3,2,4,16,2048]{4,3,2,1,0:T(8,128)(2,1)}, f32[2,3,16,2048]{3,2,1,0:T(8,128)}, f32[8,2048]{1,0:T(8,128)}, f32[256,1408]{1,0:T(8,128)}, f32[256...) custom-call(bf16[3,2,4,16,2048]{4,3,2,1,0:T(8,128)(2,1)} %bitcast.66, ...), custom_call_target="tpu_custom_call" | custom-call | bytes 80000000 | tf_op jit(solution)/shard_map/ffn_sums/pallas_call | solution.py:1182
  264.8 3.2 convolution_convert_fusion.2.grad_ref
  267.9 16.9 %attend_back.1 = (bf16[384,512]{1,0:T(8,128)(2,1)}, bf16[8,384,256]{2,1,0:T(8,128)(2,1)}) custom-call(s32[6]{0:T(128)} %lens_ref.9, s32[6]{0:T(128)} %flags_ref.9, s32[1]{0:T(128)} %bitcast.own_ref, bf16[384,512]{1,0:T(8,128)(2,1)} %get-tuple-element.36.query_ref, bf16[384,512]{1,0:T(8,128)(2,1)} %convolution_convert_fusion.2.grad_ref, ...), custom_call_target="tpu_custom_call" | custom-call | flops 3000000000 | bytes 20000000 | tf_op jit(solution)/shard_map/attend_back/pallas_call | solution.py:620
  284.8 0.0 copy-start.6
  284.8 15.7 %scatter_tok.1 = f32[384,256]{1,0:T(8,128)} custom-call(bf16[8,384,256]{2,1,0:T(8,128)(2,1)} %get-tuple-element.47.part_ref), custom_call_target="tpu_custom_call" | custom-call | bytes 10000000 | tf_op jit(solution)/shard_map/scatter_tok/pallas_call | solution.py:689
  300.5 1.0 slice.42
  301.5 1.1 fusion.6
  302.7 0.0 copy-done.7
  302.7 1.1 fusion.2
  303.8 0.9 pad_maximum_fusion.dqkv_ref
  304.7 0.0 copy-done.6
  304.7 0.6 fusion.8
  305.2 0.5 copy-done.5
  305.7 0.6 fusion.13
  306.3 1.0 copy-done.1
  307.3 2.2 add_convert_fusion
  309.4 116.1 %attn_sums.1 = (bf16[6,128,2048]{2,1,0:T(8,128)(2,1)}, f32[8,256]{1,0:T(8,128)}, bf16[6,128,2048]{2,1,0:T(8,128)(2,1)}, f32[256,768]{1,0:T(8,128)}, f32[512,256]{1,0:T(8,128)}) custom-call(s32[6]{0:T(128)} %lens_ref.9, s32[6]{0:T(128)} %flags_ref.9, bf16[3,2,4,16,2048]{4,3,2,1,0:T(8,128)(2,1)} %bitcast.58, ...), custom_call_target="tpu_custom_call" | custom-call | bytes 80000000 | tf_op jit(solution)/shard_map/attn_sums/pallas_call | solution.py:1299
  425.6 1.3 fusion.7
  426.9 1.7 fusion.5
  428.6 1.9 slice.35
  430.5 4.1 copy.30
  434.6 0.0 copy-done.4
  434.6 1.7 copy.31
  436.3 0.8 copy.32
  437.1 0.3 copy-done.12
  437.4 1.1 copy.33
  438.5 0.0 copy-done.11
  438.5 1.1 copy.34
  439.6 1.1 copy.35
  (28 shorter events, 0.1 us)
Async XLA Ops:
  0.6 89.3 %copy-start = (bf16[512,2048]{1,0:T(8,128)(2,1)S(1)}, bf16[512,2048]{1,0:T(8,128)(2,1)}, u32[]{:S(2)}) copy-start(bf16[512,2048]{1,0:T(8,128)(2,1)} %param.18) | copy-start | bytes 6291460
  154.8 7.8 %slice-start.2 = ((s8[5767168]{0:T(1024)(128)(4,1)}), s8[4194304]{0:T(1024)(128)(4,1)S(1)}, s32[]{:S(2)}) async-start(s8[5767168]{0:T(1024)(128)(4,1)} %bitcast.79), calls=%async_computation.2 | async-start | bytes 8388608
  156.7 5.9 %copy-start.2 = (bf16[3,128,2048]{2,1,0:T(8,128)(2,1)}, bf16[3,128,2048]{2,1,0:T(8,128)(2,1)S(1)}, u32[]{:S(2)}) copy-start(bf16[3,128,2048]{2,1,0:T(8,128)(2,1)S(1)} %multiply_convert_fusion) | copy-start | bytes 4718596
  156.7 5.9 %copy-start.9 = (bf16[3,2,4,16,2048]{4,3,2,1,0:T(8,128)(2,1)S(1)}, bf16[3,2,4,16,2048]{4,3,2,1,0:T(8,128)(2,1)}, u32[]{:S(2)}) copy-start(bf16[3,2,4,16,2048]{4,3,2,1,0:T(8,128)(2,1)} %get-tuple-element.40) | copy-start | bytes 4718596
  156.7 5.9 %slice-start.3 = ((s8[5767168]{0:T(1024)(128)(4,1)}), s8[1572864]{0:T(1024)(128)(4,1)S(1)}, s32[]{:S(2)}) async-start(s8[5767168]{0:T(1024)(128)(4,1)} %bitcast.79), calls=%async_computation.3 | async-start | bytes 3145728
  156.7 8.6 %slice-start.4 = ((s8[5767168]{0:T(1024)(128)(4,1)}), s8[4194304]{0:T(1024)(128)(4,1)S(1)}, s32[]{:S(2)}) async-start(s8[5767168]{0:T(1024)(128)(4,1)} %bitcast.81), calls=%async_computation.4 | async-start | bytes 8388608
  162.6 2.7 slice-start.5
  162.7 6.0 %slice-start = ((s8[5767168]{0:T(1024)(128)(4,1)}), s8[4194304]{0:T(1024)(128)(4,1)S(1)}, s32[]{:S(2)}) async-start(s8[5767168]{0:T(1024)(128)(4,1)} %bitcast.77), calls=%async_computation | async-start | bytes 8388608
  165.3 3.3 slice-start.1
  168.6 3.9 copy-start.13
  168.6 3.9 copy-start.14
  168.7 6.5 %copy-start.15 = (bf16[384,1408]{1,0:T(8,128)(2,1)}, bf16[384,1408]{1,0:T(8,128)(2,1)S(1)}, u32[]{:S(2)}) copy-start(bf16[384,1408]{1,0:T(8,128)(2,1)S(1)} %get-tuple-element.63.dup_ref) | copy-start | bytes 3244036
  284.8 17.9 %copy-start.7 = (f32[384,128]{1,0:T(8,128)S(1)}, f32[384,128]{1,0:T(8,128)}, u32[]{:S(2)}) copy-start(f32[384,128]{1,0:T(8,128)} %get-tuple-element.74.sin_ref) | copy-start | bytes 589828
  284.8 19.0 %copy-start.8 = (bf16[384,512]{1,0:T(8,128)(2,1)S(1)}, bf16[384,512]{1,0:T(8,128)(2,1)}, u32[]{:S(2)}) copy-start(bf16[384,512]{1,0:T(8,128)(2,1)} %get-tuple-element.46) | copy-start | bytes 1179652
  284.8 19.8 %copy-start.6 = (bf16[2048,128]{1,0:T(8,128)(2,1)S(1)}, bf16[2048,128]{1,0:T(8,128)(2,1)}, u32[]{:S(2)}) copy-start(bf16[2048,128]{1,0:T(8,128)(2,1)} %w_value_ref.1) | copy-start | bytes 1572868
  300.5 4.2 copy-start.3
  304.7 1.0 copy-start.5
  305.7 1.6 copy-start.1
  430.5 4.1 copy-start.4
  434.6 1.7 copy-start.16
  434.6 2.8 copy-start.12
  436.3 2.2 copy-start.11
  437.4 2.2 copy-start.10

commit v5 on v4

--- a/solution.py
+++ b/solution.py
@@ -14,6 +14,7 @@
 CHUNKS = 8
 HALVES = 2
 TILE = 16
+HOP = 2.0
 MESH = pl.DeviceIdType.MESH
 VMEM_BYTES = 60 * 2**20
 
@@ -85,6 +86,48 @@
             entry[0] = next(entry[2])
         except StopIteration:
             waiting.pop(0)
+
+
+def anywhere():
+    return pl.BlockSpec(memory_space=pl.ANY)
+
+
+class Loaded:
+    def __init__(self, source, target, sem):
+        self.copy = pltpu.make_async_copy(source, target, sem)
+        self.target = target
+        self.here = False
+        self.shape = target.shape
+
+    def get(self):
+        if not self.here:
+            self.copy.wait()
+            self.here = True
+        return self.target
+
+
+def load_all(sources, targets, sems):
+    loads = [Loaded(*pair, sems.at[i]) for i, pair in enumerate(zip(sources, targets))]
+    for load in loads:
+        load.copy.start()
+    return loads
+
+
+class Stored:
+    def __init__(self, target, source, sem):
+        self.copy = pltpu.make_async_copy(source, target, sem)
+        self.ref = source
+
+    def send(self):
+        self.copy.start()
+
+
+def store_all(targets, sources, sems):
+    return [Stored(*pair, sems.at[i]) for i, pair in enumerate(zip(targets, sources))]
+
+
+def buffers(arrays):
+    return [pltpu.VMEM(array.shape, array.dtype) for array in arrays]
 
 
 def deal_tables(own, stages, blocks_here, lens_ref, flags_ref):
@@ -141,13 +184,24 @@
     return keeps, sends, finals
 
 
-def choose(index, options, default=None):
-    value = options[0] if default is None else default
-    for number, option in enumerate(options):
-        if number == 0 and default is None:
-            continue
-        value = jnp.where(index == number, option, value)
+def choose(index, options):
+    value = options[0]
+    for number, option in enumerate(options[1:]):
+        value = jnp.where(index == number + 1, option, value)
     return value
+
+
+def slot_of(keep, recv, chunk, index):
+    stayed = keep[chunk, jnp.clip(index, 0, SLOTS - 1)]
+    arrived = recv[jnp.clip(index - SLOTS, 0, SLOTS - 1)]
+    return jnp.where(index < SLOTS, stayed, arrived)
+
+
+def deal_refs(scratch):
+    keep, send = scratch[:2]
+    stages = send.shape[0]
+    recv = [scratch[2 + i * CHUNKS : 2 + (i + 1) * CHUNKS] for i in range(stages)]
+    return keep, send, recv, *scratch[2 + stages * CHUNKS : 4 + stages * CHUNKS]
 
 
 def bit_peers(stages):
@@ -155,11 +209,11 @@
     return [(own ^ (1 << stage), plane) for stage in range(stages)]
 
 
-def deal_flow(lens_ref, flags_ref, own_ref, out_ref, scratch, pace=4.3):
-    keep, send, recv, send_sem, recv_sem = scratch
+def deal_flow(lens_ref, flags_ref, blocks, finish, scratch, pace=4.3, urgent=False):
+    keep, send, recv, send_sem, recv_sem = deal_refs(scratch)
     stages = send.shape[0]
     own = lax.axis_index("tok")
-    blocks_here = own_ref.shape[0]
+    blocks_here = blocks.shape[0]
     rows = BLOCK // CHUNKS
     peers = bit_peers(stages)
     keeps, sends, finals = deal_tables(own, stages, blocks_here, lens_ref, flags_ref)
@@ -167,82 +221,66 @@
     def copy(stage, chunk):
         return pltpu.make_async_remote_copy(
             src_ref=send.at[stage, chunk],
-            dst_ref=recv.at[stage, chunk],
+            dst_ref=recv[stage][chunk],
             send_sem=send_sem.at[stage, chunk],
             recv_sem=recv_sem.at[stage, chunk],
             device_id=peers[stage],
             device_id_type=MESH,
         )
 
-    def held(stage, chunk):
+    def held(stage, chunk, index):
         if stage == 0:
-            return [own_ref[i, pl.ds(chunk * rows, rows), :] for i in range(blocks_here)]
-        return [keep[chunk, i] for i in range(SLOTS)] + [
-            recv[stage - 1, chunk, i] for i in range(SLOTS)
-        ]
+            block = jnp.clip(index, 0, blocks_here - 1)
+            return blocks.get()[block, pl.ds(chunk * rows, rows), :]
+        return slot_of(keep, recv[stage - 1][chunk], chunk, index)
 
     for stage in range(stages + 1):
         for chunk in range(CHUNKS):
-            yield 0.0 if stage == 0 else 1 + 0.4 * chunk + pace * (stage - 1) * (chunk + 1)
+            if stage < 2:
+                yield 1.5 * stage + 0.3 * chunk
+            else:
+                slack = 4.0 if stage == stages and not urgent else 0.0
+                yield 1.5 + HOP * (stage - 1) + pace * (chunk + stage - 1) + slack
             if stage > 0:
                 copy(stage - 1, chunk).wait_recv()
-            options = held(stage, chunk)
             if stage == stages:
-                for slot in range(SLOTS):
-                    out_ref[slot, pl.ds(chunk * rows, rows), :] = choose(finals[slot], options)
+                finish(chunk, [held(stage, chunk, finals[slot]) for slot in range(SLOTS)])
             else:
                 for slot in range(SLOTS):
-                    send[stage, chunk, slot] = choose(sends[stage][slot], options)
+                    send[stage, chunk, slot] = held(stage, chunk, sends[stage][slot])
                 copy(stage, chunk).start()
+                stay = [held(stage, chunk, keeps[stage][slot]) for slot in range(SLOTS)]
                 for slot in range(SLOTS):
-                    keep[chunk, slot] = choose(keeps[stage][slot], options)
+                    keep[chunk, slot] = stay[slot]
     yield 1e6
 
-    def drain(chunk, carry):
-        for stage in range(stages):
+    for stage in range(stages):
+        for chunk in range(CHUNKS):
             copy(stage, chunk).wait_send()
-        return carry
-
-    lax.fori_loop(0, CHUNKS, drain, 0)
 
 
 def deal_scratch(stages, width, kind):
-    moved = (CHUNKS, SLOTS, BLOCK // CHUNKS, width)
+    part = (SLOTS, BLOCK // CHUNKS, width)
     return (
-        [pltpu.VMEM(moved, kind)]
-        + [pltpu.VMEM((stages,) + moved, kind)] * 2
+        [pltpu.VMEM((CHUNKS,) + part, kind), pltpu.VMEM((stages, CHUNKS) + part, kind)]
+        + [pltpu.VMEM(part, kind)] * (stages * CHUNKS)
         + [pltpu.SemaphoreType.DMA((stages, CHUNKS))] * 2
     )
+
+
+def deal_count():
+    return 4 + stages_of("tok") * CHUNKS
 
 
 def stages_of(axis):
     return int(math.log2(lax.axis_size(axis)))
-
-
-def deal_body(lens_ref, flags_ref, own_ref, out_ref, *scratch):
-    greet(bit_peers(scratch[1].shape[0]))
-    run(deal_flow(lens_ref, flags_ref, own_ref, out_ref, scratch))
-
-
-def deal(doc_lengths, keep_flags, blocks, collective_id):
-    width = blocks.shape[2]
-    return pl.pallas_call(
-        deal_body,
-        out_shape=jax.ShapeDtypeStruct((SLOTS, BLOCK, width), blocks.dtype),
-        in_specs=[smem(), smem(), vmem()],
-        out_specs=vmem(),
-        scratch_shapes=deal_scratch(stages_of("tok"), width, blocks.dtype),
-        compiler_params=params(collective_id),
-        cost_estimate=cost(0, 40_000_000),
-        name="deal",
-    )(doc_lengths, keep_flags, blocks)
 
 
 def undeal_flow(
     lens_ref, flags_ref, kept_ref, out_ref, home, scratch, start=0.0, pace=4.3, key=None, lag=0.0
 ):
-    keep, send, recv, send_sem, recv_sem = scratch
-    stages = recv.shape[0]
+    keep, send, recv, send_sem, recv_sem = deal_refs(scratch)
+    stages = send.shape[0]
     own = lax.axis_index("tok")
     blocks_here = out_ref.shape[0]
     planes = kept_ref.shape[2]
@@ -253,59 +291,60 @@
     def copy(stage, chunk):
         return pltpu.make_async_remote_copy(
             src_ref=send.at[stage, chunk],
-            dst_ref=recv.at[stage, chunk],
+            dst_ref=recv[stage][chunk],
             send_sem=send_sem.at[stage, chunk],
             recv_sem=recv_sem.at[stage, chunk],
             device_id=peers[stage],
             device_id_type=MESH,
         )
 
-    def pick_place(places, options, place, value):
-        for index, option in zip(places, options):
-            value = jnp.where(index == place, option, value)
-        return value
+    def source(places, place):
+        index = jnp.int32(-1)
+        for number, other in enumerate(places):
+            index = jnp.where(other == place, number, index)
+        return index
 
     last = stages - 1
     for stage in range(last, -2, -1):
+        count = 2 * SLOTS if stage >= 0 else blocks_here
+        places = finals if stage == last else keeps[stage + 1] + sends[stage + 1]
+        sources = [source(places, place) for place in range(count)]
         for chunk in range(CHUNKS):
             half = chunk // planes
             begin = start + lag * half
             if stage == last:
                 yield (begin, None if key is None else key + (half,))
+                options = [kept_ref[slot, half, chunk % planes] for slot in range(SLOTS)]
             else:
-                yield begin + 1 + pace * (chunk + last - stage - (stage < 0))
-            span = pl.ds(chunk * rows, rows)
-            if stage == last:
-                options = [kept_ref[slot, half, chunk % planes] for slot in range(SLOTS)]
-                places = finals
-            else:
+                hops = last - stage
+                slack = 5.0 if stage < 0 else 0.0
+                yield begin + HOP * hops + pace * (chunk + hops - (stage < 0)) + slack
                 copy(stage + 1, chunk).wait_recv()
-                options = [keep[chunk, i] for i in range(SLOTS)] + [
-                    recv[stage + 1, chunk, i] for i in range(SLOTS)
-                ]
-                places = keeps[stage + 1] + sends[stage + 1]
+
+            def block(place):
+                if stage == last:
+                    return choose(sources[place], options)
+                return slot_of(keep, recv[stage + 1][chunk], chunk, sources[place])
+
             if stage < 0:
                 if chunk == 0:
                     home.wait()
+                span = pl.ds(chunk * rows, rows)
                 for place in range(blocks_here):
                     value = out_ref[place, span, :]
-                    out_ref[place, span, :] = pick_place(places, options, place, value)
+                    out_ref[place, span, :] = jnp.where(sources[place] >= 0, block(place), value)
             else:
                 for slot in range(SLOTS):
-                    send[stage, chunk, slot] = pick_place(
-                        places, options, SLOTS + slot, options[0]
-                    )
+                    send[stage, chunk, slot] = block(SLOTS + slot)
                 copy(stage, chunk).start()
+                stay = [block(slot) for slot in range(SLOTS)]
                 for slot in range(SLOTS):
-                    keep[chunk, slot] = pick_place(places, options, slot, options[0])
+                    keep[chunk, slot] = stay[slot]
     yield 1e6
 
-    def drain(chunk, carry):
-        for stage in range(stages):
+    for stage in range(stages):
+        for chunk in range(CHUNKS):
             copy(stage, chunk).wait_send()
-        return carry
-
-    lax.fori_loop(0, CHUNKS, drain, 0)
 
 
 def gain_flow(gains_ref, sum_ref, scratch, start, key=None):
@@ -359,8 +398,8 @@
     home.start()
     greet(all_peers())
     run(
-        undeal_flow(lens_ref, flags_ref, kept_ref, out_ref, home, scratch[:5]),
-        gain_flow(gains_ref, sum_ref, scratch[5:], 0.0),
+        undeal_flow(lens_ref, flags_ref, kept_ref, out_ref, home, scratch[: deal_count()]),
+        gain_flow(gains_ref, sum_ref, scratch[deal_count() :], 0.0),
     )
 
 
@@ -386,19 +425,78 @@
     )(doc_lengths, keep_flags, kept, home, gains)
 
 
-def project_body(
-    x_ref, gain_ref, w_query_ref, w_key_ref, w_value_ref, cos_ref, sin_ref,
-    normed_ref, inv_ref, query_ref, out_ref,
-    mine_ref, send_sem, recv_sem, relay_send_sem, relay_recv_sem,
+def deal_project_body(
+    lens_ref, flags_ref, gain_ref, cos_ref, sin_ref, own_hbm, w_query_hbm, w_key_hbm, w_value_hbm,
+    x_hbm, normed_hbm, inv_ref, query_ref, out_ref,
+    own_half, w_query, w_key, w_value, x_ref, normed_ref, mine_ref, pair_send, pair_recv,
+    load_sems, store_sems, pair_send_sem, pair_recv_sem,
+    send_sem, recv_sem, relay_send_sem, relay_recv_sem, *dealing,
 ):
     devices = out_ref.shape[0]
     chips = devices // 2
     own = lax.axis_index("tok")
     plane = lax.axis_index("tp")
     partner = (own ^ 1, plane)
-    rows = x_ref.shape[0]
-    thin = w_key_ref.shape[1]
-    greet([partner] + [(own ^ (2 * step), plane) for step in range(1, chips)])
+    width = own_half.shape[2]
+    tile = BLOCK // CHUNKS
+    thin = w_key.shape[1]
+    columns = pl.ds(pl.multiple_of((plane % 2) * width, width), width)
+    blocks, w_query, w_key, w_value = load_all(
+        [own_hbm.at[:, :, columns], w_query_hbm, w_key_hbm, w_value_hbm],
+        [own_half, w_query, w_key, w_value],
+        load_sems,
+    )
+    steps = sorted({1 << i for i in range(stages_of("tok"))} | {2 * i for i in range(1, chips)})
+    greet([(own ^ step, plane) for step in steps] + [(own, plane ^ 1)])
+
+    def pair_copy(chunk):
+        return pltpu.make_async_remote_copy(
+            src_ref=pair_send.at[chunk],
+            dst_ref=pair_recv.at[chunk],
+            send_sem=pair_send_sem.at[chunk],
+            recv_sem=pair_recv_sem.at[chunk],
+            device_id=(own, plane ^ 1),
+            device_id_type=MESH,
+        )
+
+    def finish(chunk, values):
+        for slot, value in enumerate(values):
+            pair_send[chunk, slot] = value
+        pair_copy(chunk).start()
+        for slot, value in enumerate(values):
+            x_ref[slot, pl.ds(chunk * tile, tile), columns] = value
+
+    def norms():
+        for chunk in range(CHUNKS):
+            yield 500.0 + chunk, (chunk,)
+            other = pl.ds(pl.multiple_of((1 - plane % 2) * width, width), width)
+            pair_copy(chunk).wait_recv()
+            span = pl.ds(chunk * tile, tile)
+            for slot in range(SLOTS):
+                x_ref[slot, span, other] = pair_recv[chunk, slot]
+            for slot in range(SLOTS):
+                x = x_ref[slot, span, :].astype(F32)
+                inv = lax.rsqrt(jnp.mean(x * x, axis=1, keepdims=True) + norm_eps)
+                rows = pl.ds(slot * BLOCK + chunk * tile, tile)
+                inv_ref[rows, :] = inv
+                normed_ref[rows, :] = (x * inv * gain_ref[...]).astype(BF16)
+
+    done = set()
+
+    def mark(chunk, values):
+        finish(chunk, values)
+        done.add((chunk,))
+
+    run(
+        deal_flow(lens_ref, flags_ref, blocks, mark, dealing, 2.2, True),
+        norms(),
+        done=done,
+    )
+    stores = store_all([x_hbm, normed_hbm], [x_ref, normed_ref], store_sems)
+    for store in stores:
+        store.send()
+    for chunk in range(CHUNKS):
+        pair_copy(chunk).wait_send()
 
     def copy(step):
         return pltpu.make_async_remote_copy(
@@ -420,32 +518,22 @@
             device_id_type=MESH,
         )
 
-    def norm(index, carry):
-        span = pl.ds(pl.multiple_of(index * 16, 16), 16)
-        x = x_ref[span, :].astype(F32)
-        inv = lax.rsqrt(jnp.mean(x * x, axis=1, keepdims=True) + norm_eps)
-        inv_ref[span, :] = inv
-        normed_ref[span, :] = (x * inv * gain_ref[...]).astype(BF16)
-        return carry
-
-    lax.fori_loop(0, rows // 16, norm, 0)
-
-    def product(w_ref):
+    def product(weight):
         return lax.dot_general(
-            normed_ref[...], w_ref[...], (((1,), (0,)), ((), ())), preferred_element_type=F32
-        )
-
-    keys = product(w_key_ref)
+            normed_ref[...], weight.get()[...], (((1,), (0,)), ((), ())), preferred_element_type=F32
+        )
+
+    keys = product(w_key)
     for group in range(thin // HD):
         one = keys[:, group * HD : (group + 1) * HD]
         mine_ref[:, group * HD : (group + 1) * HD] = turn(one, cos_ref, sin_ref, -1.0).astype(BF16)
-    mine_ref[:, thin:] = product(w_value_ref).astype(BF16)
+    mine_ref[:, thin:] = product(w_value).astype(BF16)
     for step in range(1, chips):
         copy(step).start()
     relay(0).start()
     out_ref[own] = mine_ref[...]
-    queries = product(w_query_ref)
-    for head in range(w_query_ref.shape[1] // HD):
+    queries = product(w_query)
+    for head in range(w_query.shape[1] // HD):
         one = queries[:, head * HD : (head + 1) * HD]
         query_ref[:, head * HD : (head + 1) * HD] = turn(one, cos_ref, sin_ref, -1.0).astype(BF16)
     for step in range(1, chips):
@@ -455,32 +543,53 @@
         relay(step).wait()
     for step in range(1, chips):
         copy(step).wait_send()
+    for store in stores:
+        store.copy.wait()
 
 
 def turn(values, cos_ref, sin_ref, sign):
     return values * cos_ref[...] + pltpu.roll(values, HD // 2, 1) * (sin_ref[...] * sign)
 
 
-def project(x, gain, w_query, w_key, w_value, cosine, sine, collective_id):
+def deal_project(
+    doc_lengths, keep_flags, gain, cosine, sine, blocks, w_query, w_key, w_value, collective_id
+):
     devices = lax.axis_size("tok")
     chips = devices // 2
-    rows = x.shape[0]
+    width = blocks.shape[2]
+    rows = SLOTS * BLOCK
     both = w_key.shape[1] + w_value.shape[1]
+    x_shape, normed_shape = (SLOTS, BLOCK, width), (rows, width)
+    weights = [w_query, w_key, w_value]
     return pl.pallas_call(
-        project_body,
+        deal_project_body,
         out_shape=(
-            jax.ShapeDtypeStruct(x.shape, BF16),
+            jax.ShapeDtypeStruct(x_shape, BF16),
+            jax.ShapeDtypeStruct(normed_shape, BF16),
             jax.ShapeDtypeStruct((rows, 1), F32),
             jax.ShapeDtypeStruct((rows, w_query.shape[1]), BF16),
             jax.ShapeDtypeStruct((devices, rows, both), BF16),
         ),
-        in_specs=[vmem()] * 7,
-        out_specs=(vmem(),) * 4,
-        scratch_shapes=[pltpu.VMEM((rows, both), BF16)] + [pltpu.SemaphoreType.DMA((chips,))] * 4,
+        in_specs=[smem()] * 2 + [vmem()] * 3 + [anywhere()] * 4,
+        out_specs=(anywhere(),) * 2 + (vmem(),) * 3,
+        scratch_shapes=[pltpu.VMEM(blocks.shape[:2] + (width // 2,), BF16)]
+        + buffers(weights)
+        + [
+            pltpu.VMEM(x_shape, BF16),
+            pltpu.VMEM(normed_shape, BF16),
+            pltpu.VMEM((rows, both), BF16),
+            pltpu.VMEM((CHUNKS, SLOTS, BLOCK // CHUNKS, width // 2), BF16),
+            pltpu.VMEM((CHUNKS, SLOTS, BLOCK // CHUNKS, width // 2), BF16),
+            pltpu.SemaphoreType.DMA((4,)),
+            pltpu.SemaphoreType.DMA((2,)),
+        ]
+        + [pltpu.SemaphoreType.DMA((CHUNKS,))] * 2
+        + [pltpu.SemaphoreType.DMA((chips,))] * 4
+        + deal_scratch(stages_of("tok"), width // 2, BF16),
         compiler_params=params(collective_id),
-        cost_estimate=cost(0, 30_000_000),
-        name="project",
-    )(x, gain, w_query, w_key, w_value, cosine, sine)
+        cost_estimate=cost(0, 60_000_000),
+        name="deal_project",
+    )(doc_lengths, keep_flags, gain, cosine, sine, blocks, *weights)
 
 
 def first_rank(lens_ref, flags_ref, rank):
@@ -571,14 +680,41 @@
     )(doc_lengths, keep_flags, own, query, kv)
 
 
+class Passed:
+    def __init__(self, source, passing, targets, sems):
+        self.first = pltpu.make_async_copy(source, passing, sems.at[0])
+        self.rest = [pltpu.make_async_copy(part, to, sems.at[1]) for part, to in targets(passing)]
+        self.first.start()
+
+    def turn(self):
+        self.first.wait()
+        for copy in self.rest:
+            copy.start()
+
+    def end(self):
+        for copy in self.rest:
+            copy.wait()
+
+
 def attend_back_body(
     lens_ref, flags_ref, own_ref, query_ref, grad_ref, kv_ref, wide_ref, log_ref, cos_ref, sin_ref,
-    grad_query_ref, grad_kv_ref, grad_kv, total,
+    *refs,
 ):
+    sources, grad_query_ref, grad_kv_ref, targets, grad_kv, total = (
+        refs[:3], refs[3], refs[4], refs[5:8], refs[8], refs[9],
+    )
+    passing, sems = refs[10:13], refs[13]
+    passes = [
+        Passed(sources[i], passing[i], lambda ref, i=i: [(ref, targets[i])], sems.at[i])
+        for i in range(3)
+    ]
     devices = kv_ref.shape[0]
     scale = 1.0 / math.sqrt(HD)
     grad_kv[...] = jnp.zeros_like(grad_kv)
     for slot in range(SLOTS):
+        if slot == 1:
+            for one in passes:
+                one.turn()
         rank = own_ref[0] + devices * slot
         query = stack_heads(query_ref, slot)
         grad = stack_heads(grad_ref, slot)
@@ -613,23 +749,69 @@
                 one, cos_ref.at[span], sin_ref.at[span], 1.0
             ).astype(BF16)
     grad_kv_ref[...] = grad_kv[...].astype(BF16)
-
-
-def attend_back(doc_lengths, keep_flags, own, query, grad, kv, wide, log_total, cosine, sine):
+    for one in passes:
+        one.end()
+
+
+def attend_back(doc_lengths, keep_flags, own, query, grad, kv, wide, log_total, cosine, sine, results):
     count = query.shape[1] // HD * BLOCK
     return pl.pallas_call(
         attend_back_body,
         out_shape=(
             jax.ShapeDtypeStruct(query.shape, BF16),
             jax.ShapeDtypeStruct(kv.shape, BF16),
-        ),
-        in_specs=[smem()] * 3 + [vmem()] * 7,
-        out_specs=(vmem(),) * 2,
-        scratch_shapes=[pltpu.VMEM(kv.shape, F32), pltpu.VMEM((HD, count), F32)],
+        )
+        + tuple(jax.ShapeDtypeStruct(result.shape, result.dtype) for result in results),
+        in_specs=[smem()] * 3 + [vmem()] * 7 + [anywhere()] * 3,
+        out_specs=(vmem(),) * 2 + (anywhere(),) * 3,
+        scratch_shapes=[
+            pltpu.VMEM(kv.shape, F32),
+            pltpu.VMEM((HD, count), F32),
+        ]
+        + buffers(results)
+        + [pltpu.SemaphoreType.DMA((3, 2))],
         compiler_params=pltpu.CompilerParams(vmem_limit_bytes=VMEM_BYTES),
         cost_estimate=cost(3_000_000_000, 20_000_000),
         name="attend_back",
-    )(doc_lengths, keep_flags, own, query, grad, kv, wide, log_total, cosine, sine)
+    )(doc_lengths, keep_flags, own, query, grad, kv, wide, log_total, cosine, sine, *results)
+
+
+def finish_body(mixed_ref, grad_ref, qkv_ref, out_ref, *refs):
+    query_ref, key_ref = refs[2], refs[3]
+    wide, thin = query_ref.shape[1], key_ref.shape[1]
+    passing, sems = refs[6:10], refs[10]
+
+    def parts(ref):
+        yield ref.at[:, pl.ds(0, wide)], query_ref
+        yield ref.at[:, pl.ds(wide, thin)], key_ref
+        yield ref.at[:, pl.ds(wide + thin, thin)], refs[4]
+
+    passes = [
+        Passed(mixed_ref, passing[0], lambda ref: [(ref, refs[0])], sems.at[0]),
+        Passed(grad_ref, passing[1], lambda ref: [(ref, refs[1])], sems.at[1]),
+        Passed(out_ref, passing[2], lambda ref: [(ref, refs[5])], sems.at[2]),
+        Passed(qkv_ref, passing[3], parts, sems.at[3]),
+    ]
+    for one in passes:
+        one.turn()
+    for one in passes:
+        one.end()
+
+
+def finish(mixed, grad, qkv, out, thin):
+    share, wide = qkv.shape[0], qkv.shape[1] - 2 * thin
+    shapes = [(mixed.shape, BF16), (grad.shape, BF16), ((share, wide), F32)]
+    shapes += [((share, thin), F32)] * 2 + [(out.shape, F32)]
+    return pl.pallas_call(
+        finish_body,
+        out_shape=[jax.ShapeDtypeStruct(*shape) for shape in shapes],
+        in_specs=[anywhere()] * 4,
+        out_specs=[anywhere()] * 6,
+        scratch_shapes=buffers([mixed, grad, out, qkv]) + [pltpu.SemaphoreType.DMA((4, 2))],
+        compiler_params=pltpu.CompilerParams(vmem_limit_bytes=VMEM_BYTES),
+        cost_estimate=cost(0, 20_000_000),
+        name="finish",
+    )(mixed, grad, qkv, out)
 
 
 def scatter_tok_body(
@@ -789,6 +971,8 @@
 
     for step in range(1, planes):
         yield start + pace * (step - 1)
+        if step == 1:
+            part = part.get()
         upper, lower = planes - step + plane, step - planes + plane
 
         @pl.when((upper <= last) & (plane < last))
@@ -901,8 +1085,9 @@
     ] + [pltpu.SemaphoreType.DMA((HALVES, 2, planes))] * (4 if gathers else 2)
 
 
-def norm_math(x_ref, gain_ref, hidden_ref, inv_ref, gathered):
+def norm_math(x, gain_ref, hidden_ref, inv_ref, gathered):
     def rule(plane, half, total):
+        x_ref = x.get()
         for block in range(SLOTS):
             hidden = x_ref[block, half, plane].astype(F32) + total[half, block]
             inv = lax.rsqrt(jnp.mean(hidden * hidden, axis=1, keepdims=True) + norm_eps)
@@ -913,10 +1098,11 @@
     return rule
 
 
-def ffn_math(hidden_ref, inv_ref, dy_ref, gain_ref, grad_ref, gains_ref, gathered):
+def ffn_math(hiddens, inv_ref, dy, gain_ref, grad_ref, gains_ref, gathered):
     def rule(plane, half, total):
         if half == 0:
             gains_ref[...] = jnp.zeros_like(gains_ref)
+        hidden_ref, dy_ref = hiddens.get(), dy.get()
         for block in range(SLOTS):
             dn = total[half, block]
             hidden = hidden_ref[half, block]
@@ -935,8 +1121,9 @@
     return rule
 
 
-def mixed_math(hidden_ref, x_ref, mixed_ref):
+def mixed_math(hiddens, xs, mixed_ref):
     def rule(plane, half, total):
+        hidden_ref, x_ref = hiddens.get(), xs.get()
         for block in range(SLOTS):
             x = x_ref[block, half, plane].astype(F32)
             branch = (hidden_ref[half, block] - x) + total[half, block]
@@ -945,8 +1132,9 @@
     return rule
 
 
-def attn_math(x_ref, inv_ref, dy_ref, grad_ref, gain_ref, ffn_gains_ref, gains_all, gathered):
+def attn_math(xs, inv_ref, dy, grads, gain_ref, ffn_gains_ref, gains_all, gathered):
     def rule(plane, half, total):
+        x_ref, dy_ref, grad_ref = xs.get(), dy.get(), grads.get()
         if half == 0:
             gains_all[plane] = ffn_gains_ref[...]
         for block in range(SLOTS):
@@ -968,37 +1156,54 @@
 
 
 def deal_sum_body(
-    lens_ref, flags_ref, own_ref, part_ref, x_ref, gain_ref,
-    out_ref, gathered, hidden_ref, inv_ref, *scratch,
+    lens_ref, flags_ref, gain_ref, own_hbm, part_hbm, x_hbm,
+    out_hbm, gathered_hbm, hidden_ref, inv_ref,
+    own_blocks, part, x, out_ref, gathered, load_sems, store_sems, *scratch,
 ):
-    dealing, summing = scratch[:5], scratch[5:]
-    greet(bit_peers(dealing[1].shape[0]), line=True)
-    rule = norm_math(x_ref, gain_ref, hidden_ref, inv_ref, gathered)
+    dealing, summing = scratch[: deal_count()], scratch[deal_count() :]
+    part, blocks, x = load_all([part_hbm, own_hbm, x_hbm], [part, own_blocks, x], load_sems)
+    out, rows = store_all([out_hbm, gathered_hbm], [out_ref, gathered], store_sems)
+    greet(bit_peers(stages_of("tok")), line=True)
+    tile = BLOCK // CHUNKS
+
+    def finish(chunk, values):
+        for slot, value in enumerate(values):
+            out_ref[slot, pl.ds(chunk * tile, tile), :] = value
+        if chunk == CHUNKS - 1:
+            out.send()
+
     run(
-        *sum_flows(part_ref, gathered, summing, rule),
-        deal_flow(lens_ref, flags_ref, own_ref, out_ref, dealing),
-    )
+        *sum_flows(part, gathered, summing, norm_math(x, gain_ref, hidden_ref, inv_ref, gathered)),
+        deal_flow(lens_ref, flags_ref, blocks, finish, dealing),
+    )
+    rows.send()
+    rows.copy.wait()
+    out.copy.wait()
 
 
 def deal_sum(doc_lengths, keep_flags, blocks, part, x, gain, collective_id):
     planes, width = part.shape[2], part.shape[4]
     shard = (HALVES, SLOTS, TILE)
+    dealt = jax.ShapeDtypeStruct((SLOTS, BLOCK, width), blocks.dtype)
+    rows = jax.ShapeDtypeStruct(part.shape, BF16)
     return pl.pallas_call(
         deal_sum_body,
         out_shape=(
-            jax.ShapeDtypeStruct((SLOTS, BLOCK, width), blocks.dtype),
-            jax.ShapeDtypeStruct(part.shape, BF16),
+            dealt,
+            rows,
             jax.ShapeDtypeStruct(shard + (width,), F32),
             jax.ShapeDtypeStruct(shard + (1,), F32),
         ),
-        in_specs=[smem(), smem()] + [vmem()] * 4,
-        out_specs=(vmem(),) * 4,
-        scratch_shapes=deal_scratch(stages_of("tok"), width, blocks.dtype)
+        in_specs=[smem(), smem(), vmem()] + [anywhere()] * 3,
+        out_specs=(anywhere(),) * 2 + (vmem(),) * 2,
+        scratch_shapes=buffers([blocks, part, x, dealt, rows])
+        + [pltpu.SemaphoreType.DMA((3,)), pltpu.SemaphoreType.DMA((2,))]
+        + deal_scratch(stages_of("tok"), width, blocks.dtype)
         + sum_scratch(planes, width),
         compiler_params=params(collective_id),
         cost_estimate=cost(0, 60_000_000),
         name="deal_sum",
-    )(doc_lengths, keep_flags, blocks, part, x, gain)
+    )(doc_lengths, keep_flags, gain, blocks, part, x)
 
 
 def spread_flow(units, outs, scratch, pace, start=0.0):
@@ -1069,7 +1274,9 @@
                     copy(unit, half, stage + 1, chip ^ bit).start()
             else:
                 rows = total.shape[0]
-                outs[unit][half * rows : (half + 1) * rows, :] = total
+                outs[unit].ref[half * rows : (half + 1) * rows, :] = total
+                if half == 1:
+                    outs[unit].send()
 
     chip_order = sorted(range(chips), key=lambda chip: -bin(chip).count("1"))
     for unit in range(count):
@@ -1084,6 +1291,9 @@
             for half in range(2):
                 yield start + 6.0 + pace * (unit + 1 + count * stage)
                 take(unit, stage, half)
+    yield 1e6
+    for out in outs:
+        out.copy.wait()
     for unit in range(count):
         for half in range(2):
             for stage in range(stages):
@@ -1114,11 +1324,11 @@
     ).astype(ref.dtype)
 
 
-def rows_by_owner(left_ref, right_ref, rows):
+def rows_by_owner(left, right, rows):
     def term(owner, half):
         return lax.dot_general(
-            window(left_ref, owner * 2 + half, rows // 2),
-            right_ref[...],
+            window(left.get(), owner * 2 + half, rows // 2),
+            right.get()[...],
             (((0,), (0,)), ((), ())),
             preferred_element_type=F32,
         )
@@ -1126,12 +1336,12 @@
     return term
 
 
-def columns_by_owner(left_ref, right_ref, columns):
+def columns_by_owner(left, right, columns):
     def term(owner, half):
-        rows = left_ref.shape[1] // 2
+        rows = left.shape[1] // 2
         return lax.dot_general(
-            left_ref[:, half * rows : (half + 1) * rows],
-            window(right_ref, owner, columns),
+            left.get()[:, half * rows : (half + 1) * rows],
+            window(right.get(), owner, columns),
             (((0,), (0,)), ((), ())),
             preferred_element_type=F32,
         )
@@ -1139,36 +1349,50 @@
     return term
 
 
-def ffn_sums_body(
-    part_ref, hidden_ref, inv_ref, dy_ref, gain_ref, normed_ref, dgate_ref, dup_ref, inner_ref, dm_ref,
-    mixed_part_ref, x_ref,
-    gathered, grad_ref, gains_ref, gate_out, up_out, down_out, mixed_ref, *scratch,
-):
-    summing, mixing, spreading = scratch[:7], scratch[7:12], scratch[12:]
+def ffn_sums_body(*refs):
+    inv_ref, gain_ref = refs[:2]
+    sources, (grad_ref, gains_ref, mixed_ref), targets = refs[2:12], refs[12:15], refs[15:19]
+    loaded, stored, refs = refs[19:29], refs[29:33], refs[33:]
+    load_sems, store_sems, refs = refs[0], refs[1], refs[2:]
+    summing, mixing, spreading = refs[:7], refs[7:12], refs[12:]
     own, plane = lax.axis_index("tok"), lax.axis_index("tp")
-    devices = lax.axis_size("tok")
-    share = normed_ref.shape[1] // devices
-    chips = devices // 2
+    loads = load_all(sources, loaded, load_sems)
+    part, normed, dgate, dup, inner, dm, hidden, dy, mixed_part, x = loads
+    rows, *grads = store_all(targets, stored, store_sems)
+    gathered = rows.ref
+    share = normed.shape[1] // lax.axis_size("tok")
     greet([(own ^ 1, plane)] + [(own ^ (2 << i), plane) for i in range(stages_of("tok") - 1)], True)
+    done = set()
+
+    def leave():
+        for half in range(HALVES):
+            yield 80.0, ("rows", half)
+        rows.send()
+
     run(
         *sum_flows(
-            part_ref,
+            part,
             gathered,
             summing,
-            ffn_math(hidden_ref, inv_ref, dy_ref, gain_ref, grad_ref, gains_ref, gathered),
+            ffn_math(hidden, inv_ref, dy, gain_ref, grad_ref, gains_ref, gathered),
+            done=done,
+            key=("rows",),
         ),
-        *sum_flows(mixed_part_ref, None, mixing, mixed_math(hidden_ref, x_ref, mixed_ref), 27.0, 11.0),
+        *sum_flows(mixed_part, None, mixing, mixed_math(hidden, x, mixed_ref), 27.0, 11.0),
         spread_flow(
             [
-                rows_by_owner(normed_ref, dgate_ref, share),
-                rows_by_owner(normed_ref, dup_ref, share),
-                columns_by_owner(inner_ref, dm_ref, share),
+                rows_by_owner(normed, dgate, share),
+                rows_by_owner(normed, dup, share),
+                columns_by_owner(inner, dm, share),
             ],
-            [gate_out, up_out, down_out],
+            grads,
             spreading,
             15.6,
         ),
-    )
+        leave(),
+        done=done,
+    )
+    rows.copy.wait()
 
 
 def ffn_sums(
@@ -1179,53 +1403,62 @@
     share = width // devices
     wide = dgate.shape[1]
     shapes = [(share, wide), (share, wide), (wide, share)]
-    return pl.pallas_call(
+    rows = jax.ShapeDtypeStruct(part.shape, BF16)
+    grads = [jax.ShapeDtypeStruct(shape, F32) for shape in shapes]
+    sources = [part, normed, dgate, dup, inner, dm, hidden, dy, mixed_part, x]
+    grad, gains, mixed, rows, gate, up, down = pl.pallas_call(
         ffn_sums_body,
         out_shape=[
-            jax.ShapeDtypeStruct(part.shape, BF16),
             jax.ShapeDtypeStruct(hidden.shape, F32),
             jax.ShapeDtypeStruct((8, width), F32),
+            jax.ShapeDtypeStruct(hidden.shape, BF16),
+            rows,
         ]
-        + [jax.ShapeDtypeStruct(shape, F32) for shape in shapes]
-        + [jax.ShapeDtypeStruct(hidden.shape, BF16)],
-        in_specs=[vmem()] * 12,
-        out_specs=[vmem()] * 7,
-        scratch_shapes=sum_scratch(planes, width)
+        + grads,
+        in_specs=[vmem()] * 2 + [anywhere()] * len(sources),
+        out_specs=[vmem()] * 3 + [anywhere()] * 4,
+        scratch_shapes=buffers(sources + [rows] + grads)
+        + [pltpu.SemaphoreType.DMA((len(sources),)), pltpu.SemaphoreType.DMA((4,))]
+        + sum_scratch(planes, width)
         + sum_scratch(planes, width, False)
         + spread_scratch(shapes, devices),
         compiler_params=params(collective_id),
         cost_estimate=cost(0, 80_000_000),
         name="ffn_sums",
-    )(part, hidden, inv, dy, gain, normed, dgate, dup, inner, dm, mixed_part, x)
+    )(inv, gain, *sources)
+    return rows, grad, gains, gate, up, down, mixed
 
 
 def together():
     return stages_of("tok") <= 3
 
 
-def attn_sums_body(
-    lens_ref, flags_ref, part_ref, mixed_ref, x_ref, inv_ref, dy_ref, grad_ref, gain_ref, ffn_gains_ref,
-    normed_ref, dqkv_ref, attended_ref, da_ref, home_ref, grad_home_ref, *refs,
-):
+def attn_sums_body(lens_ref, flags_ref, *refs):
     both = together()
-    gathered, gains_ref, mixed_out, qkv_out, out_out = refs[:5]
-    refs = refs[5:]
+    mixed_ref, inv_ref, gain_ref, ffn_gains_ref = refs[:4]
+    sources, home_ref, grad_home_ref, refs = refs[4:12], refs[12], refs[13], refs[14:]
+    gathered, gains_ref, mixed_out = refs[:3]
+    targets, refs = refs[3:5], refs[5:]
+    loaded, stored, load_sems, store_sems, refs = refs[:8], refs[8:10], refs[10], refs[11], refs[12:]
+    part, normed, dqkv, attended, da, x, dy, grad = load_all(sources, loaded, load_sems)
+    weight_grads = store_all(targets, stored, store_sems)
     if both:
         grad_out, gathered = gathered, refs[0]
         gain_sums, gains_ref = gains_ref, refs[1]
         refs = refs[2:]
-    summing, undealing, refs = refs[:7], refs[7:12], refs[12:]
+    summing, undealing, refs = refs[:7], refs[7 : 7 + deal_count()], refs[7 + deal_count() :]
     mixed_all, mixed_sems, home_sems = refs[0], refs[1:3], refs[3]
     gains_all, gains_sems, refs = refs[4], refs[5:7], refs[7:]
-    planes = part_ref.shape[2]
+    planes = part.shape[2]
     plane = lax.axis_index("tp")
-    share = normed_ref.shape[1] // lax.axis_size("tok")
+    share = normed.shape[1] // lax.axis_size("tok")
     home = pltpu.make_async_copy(home_ref, mixed_out, home_sems.at[0])
     home.start()
     if both:
         grad_home = pltpu.make_async_copy(grad_home_ref, grad_out, home_sems.at[1])
         grad_home.start()
-        grad_undealing, gaining, refs = refs[:5], refs[5:8], refs[8:]
+        grad_undealing, refs = refs[: deal_count()], refs[deal_count() :]
+        gaining, refs = refs[:3], refs[3:]
     greet(all_peers() if both else bit_peers(stages_of("tok")), True)
     for half in range(HALVES):
         mixed_all[:, half, plane] = mixed_ref[half]
@@ -1242,12 +1475,10 @@
     flows = [
         *gather_flows(mixed_all, mixed_sems, 0.0, 8.7, done, ("mixed",)),
         *sum_flows(
-            part_ref,
+            part,
             gathered,
             summing,
-            attn_math(
-                x_ref, inv_ref, dy_ref, grad_ref, gain_ref, ffn_gains_ref, gains_all, gathered
-            ),
+            attn_math(x, inv_ref, dy, grad, gain_ref, ffn_gains_ref, gains_all, gathered),
             9.0,
             10.0,
             (lambda index: gains_all.at[index],) + gains_sems,
@@ -1256,10 +1487,10 @@
         ),
         spread_flow(
             [
-                rows_by_owner(normed_ref, dqkv_ref, share),
-                columns_by_owner(attended_ref, da_ref, share),
+                rows_by_owner(normed, dqkv, share),
+                columns_by_owner(attended, da, share),
             ],
-            [qkv_out, out_out],
+            weight_grads,
             refs,
             9.0,
         ),
@@ -1296,14 +1527,18 @@
         [blocks_shape, jax.ShapeDtypeStruct((8, gain_part), F32)] if both else [rows_shape, gains_shape]
     )
     dealing = deal_scratch(stages_of("tok"), width, BF16)
+    sources = [part, normed, dqkv, attended, da, x, dy, grad]
+    weight_grads = [jax.ShapeDtypeStruct(shape, F32) for shape in shapes]
     grads, gains, mixed_blocks, qkv, out = pl.pallas_call(
         attn_sums_body,
         out_shape=first
         + [blocks_shape]
-        + [jax.ShapeDtypeStruct(shape, F32) for shape in shapes],
-        in_specs=[smem(), smem()] + [vmem()] * 12 + [pl.BlockSpec(memory_space=pl.ANY)] * 2,
-        out_specs=[vmem()] * 5,
-        scratch_shapes=(
+        + weight_grads,
+        in_specs=[smem(), smem()] + [vmem()] * 4 + [anywhere()] * 10,
+        out_specs=[vmem()] * 3 + [anywhere()] * 2,
+        scratch_shapes=buffers(sources + weight_grads)
+        + [pltpu.SemaphoreType.DMA((8,)), pltpu.SemaphoreType.DMA((2,))]
+        + (
             [pltpu.VMEM(part.shape, BF16), pltpu.VMEM((8, width), F32)] if both else []
         )
         + sum_scratch(planes, width)
@@ -1318,8 +1553,7 @@
         cost_estimate=cost(0, 80_000_000),
         name="attn_sums",
     )(
-        doc_lengths, keep_flags, part, mixed, x, inv, dy, grad, gain, ffn_gains, normed, dqkv, attended,
-        da, home, grad_home,
+        doc_lengths, keep_flags, mixed, inv, gain, ffn_gains, *sources, home, grad_home
     )
     if not both:
         grads, gains = undeal(doc_lengths, keep_flags, grads, grad_home, gains, collective_id + 1)
@@ -1379,14 +1613,22 @@
     token_blocks = tokens.reshape(blocks_here, BLOCK, model_width)
     grad_blocks = cotangent.reshape(blocks_here, BLOCK, model_width)
 
-    rows_x = deal(doc_lengths, keep_flags, token_blocks, 0).reshape(rows, model_width)
-
     own_ranks = own_index + jnp.arange(kept_here, dtype=jnp.int32) * devices
     cosine, sine = rotary_tables(doc_lengths, keep_flags, own_ranks)
     own = jnp.reshape(own_index, (1,)).astype(jnp.int32)
-    normed_one, inv_one, queries, kv_all = project(
-        rows_x, gain_attn.reshape(1, -1), w_query, w_key, w_value, cosine, sine, 2
-    )
+    rows_x, normed_one, inv_one, queries, kv_all = deal_project(
+        doc_lengths,
+        keep_flags,
+        gain_attn.reshape(1, -1),
+        cosine,
+        sine,
+        token_blocks,
+        w_query,
+        w_key,
+        w_value,
+        0,
+    )
+    rows_x = rows_x.reshape(rows, model_width)
     attended, attended_wide, log_totals = attend(doc_lengths, keep_flags, own, queries, kv_all)
 
     def by_plane(array):
@@ -1437,7 +1679,7 @@
     grad_a = grad_a.reshape(rows, model_width)
 
     grad_attended = over_columns(grad_a, w_out).astype(jnp.bfloat16)
-    grad_query_pre, grad_kv = attend_back(
+    grad_query_pre, grad_kv, grad_gate, grad_up, grad_down = attend_back(
         doc_lengths,
         keep_flags,
         own,
@@ -1448,6 +1690,7 @@
         log_totals,
         cosine,
         sine,
+        [grad_gate, grad_up, grad_down],
     )
     grad_kv = scatter_tok(grad_kv, 5)
     grad_key_pre = unrotate(grad_kv[:, :HD], cosine, sine).astype(jnp.bfloat16)
@@ -1479,10 +1722,9 @@
     own_share = model_width // devices
     if gain_sums.shape[1] != own_share:
         gain_sums = lax.dynamic_slice_in_dim(gain_sums, own_index * own_share, own_share, 1)
-    wide, thin = w_query.shape[1], w_key.shape[1]
-    grad_query = grad_qkv[:, :wide]
-    grad_key = grad_qkv[:, wide : wide + thin]
-    grad_value = grad_qkv[:, wide + thin :]
+    mixed, token_grad, grad_query, grad_key, grad_value, grad_out = finish(
+        mixed, token_grad, grad_qkv, grad_out, w_key.shape[1]
+    )
 
     return (
         mixed.reshape(length, model_width),

time: 450 us -> 420 us (0.933)
  Pallas kernels: 382 us -> 367 us
  local copies, waits for them, and re-layouts: 18.8 us -> 5.07 us
    pallas_call x5, Pallas kernels: 335 us -> 322 us  [the longest x1 114 us: attn_sums(): pl.pallas_call(attn_sums_body, out_shape=first + [blocks_shape] + weight_...]
    unnamed x52 -> x36, local copies, waits for them, and re-layouts: 11.8 us -> 1.59 us
where the time goes in v5:
time: 420 us; the launch traced here: 412 us
  Pallas kernels  367 us (87%)
  matrix products  31.5 us (8%)
  other arithmetic  6.86 us (2%)
  local copies, waits for them, and re-layouts  5.07 us (1%)
    pallas_call x1, Pallas kernels, attn_sums(): pl.pallas_call(attn_sums_body, out_shape=first + [blocks_shape] + weight_...  114 us
    pallas_call x1, Pallas kernels, ffn_sums(): pl.pallas_call(ffn_sums_body, out_shape=[jax.ShapeDtypeStruct(hidden.shap...  84.9 us
    pallas_call x1, Pallas kernels, deal_project(): pl.pallas_call(deal_project_body, out_shape=(jax.ShapeDtypeStruct(x_shape...  59.9 us
    pallas_call x1, Pallas kernels, deal_sum(): pl.pallas_call(deal_sum_body, out_shape=(dealt, rows, jax.ShapeDtypeStruc...  58.6 us
    pallas_call x1, Pallas kernels, scatter_tok(): pl.pallas_call(scatter_tok_body, out_shape=jax.ShapeDtypeStruct(shard, F3...  19.3 us
    dot_general x7, matrix products, over_columns(): lax.dot_general(left, right, (((1,), (1,)), ((), ())), preferred_element_...  18.7 us
    pallas_call x1, Pallas kernels, attend_back(): pl.pallas_call(attend_back_body, out_shape=(jax.ShapeDtypeStruct(query.sh...  14 us
    pallas_call x1, Pallas kernels, attend(): pl.pallas_call(attend_body, out_shape=(jax.ShapeDtypeStruct(query.shape,...  11.1 us

profile of v5, /device:TPU:1, one launch (start us, length us, event | category | flops | bytes accessed | tf_op | source)
XLA Modules:
  0.0 411.8 jit_solution(3257821079646521592)
XLA Ops:
  0.6 0.0 copy-start
  0.7 0.8 fusion.4
  1.5 0.2 reduce-window.8
  1.7 0.2 select_reduce_fusion
  1.9 0.1 convert_bitcast_fusion
  2.0 0.8 multiply_sine_fusion
  2.7 0.9 pad_maximum_fusion.1
  3.7 59.9 %deal_project.1 = (bf16[3,128,2048]{2,1,0:T(8,128)(2,1)}, bf16[384,2048]{1,0:T(8,128)(2,1)}, f32[384,1]{1,0:T(8,128)}, bf16[384,512]{1,0:T(8,128)(2,1)}, bf16[8,384,256]{2,1,0:T(8,128)(2,1)}) custom-call(s32[6]{0:T(128)} %lens_ref.9, s32[6]{0:T(128)} %flags_ref.9, f32[1,2048]{1,0:T(1,128)} %bitcast.66, f32[384,128]{1,0:T(8,128)} %get-tuple-element.91.cos_ref, ...), custom_call_target="tpu_custom_call" | custom-call | bytes 60000000 | tf_op jit(solution)/shard_map/deal_project/pallas_call | solution.py:564
  63.6 11.1 %attend.1 = (bf16[384,512]{1,0:T(8,128)(2,1)}, f32[3,128,512]{2,1,0:T(8,128)}, f32[3,8,512]{2,1,0:T(8,128)}) custom-call(s32[6]{0:T(128)} %lens_ref.9, s32[6]{0:T(128)} %flags_ref.9, s32[1]{0:T(128)} %bitcast.2.own_ref, bf16[384,512]{1,0:T(8,128)(2,1)} %get-tuple-element.46.query_ref, bf16[8,384,256]{2,1,0:T(8,128)(2,1)} %get-tuple-element.47.kv_ref), custom_call_target="tpu_custom_call" | custom-call | flops 1000000000 | bytes 10000000 | tf_op jit(solution)/shard_map/attend/pallas_call | solution.py:667
  74.7 0.0 copy-done
  74.7 3.1 convolution_convert_fusion.1
  77.8 58.6 %deal_sum.1 = (bf16[3,128,2048]{2,1,0:T(8,128)(2,1)}, bf16[3,2,4,16,2048]{4,3,2,1,0:T(8,128)(2,1)}, f32[2,3,16,2048]{3,2,1,0:T(8,128)}, f32[2,3,16,1]{3,2,1,0:T(8,128)}) custom-call(s32[6]{0:T(128)} %lens_ref.9, s32[6]{0:T(128)} %flags_ref.9, f32[1,2048]{1,0:T(1,128)} %bitcast.68, bf16[6,128,2048]{2,1,0:T(8,128)(2,1)} %bitcast.52, ...), custom_call_target="tpu_custom_call" | custom-call | bytes 60000000 | tf_op jit(solution)/shard_map/deal_sum/pallas_call | solution.py:1189
  136.5 0.0 slice-start.2
  136.5 1.9 multiply_convert_fusion
  138.4 0.0 copy-start.2
  138.4 0.0 copy-start.8
  138.4 0.0 slice-start.3
  138.4 0.0 slice-start.4
  138.4 5.8 %fusion.9 = f32[384,1408]{1,0:T(8,128)S(1)} fusion(bf16[384,2048]{1,0:T(8,128)(2,1)S(1)} %bitcast.54, bf16[1408,2048]{1,0:T(8,128)(2,1)} %param.22), kind=kOutput, calls=%fused_computation.36 | convolution fusion | flops 2214592512 | bytes 9502720 | tf_op jit(solution)/shard_map/dot_general | solution.py:1585
  144.3 0.0 copy-done.2
  144.3 0.0 slice-done.2
  144.3 0.0 copy-done.8
  144.3 0.0 slice-done.3
  144.3 0.0 slice-start.5
  144.4 0.0 slice-start
  144.4 2.6 fusion.10
  147.0 0.0 slice-done.4
  147.0 0.0 slice-done.5
  147.0 0.0 slice-start.1
  147.0 3.3 multiply_convert_fusion.1
  150.3 0.0 copy-start.9
  150.3 0.0 copy-start.10
  150.3 0.0 copy-start.11
  150.4 0.0 slice-done
  150.4 0.0 slice-done.1
  150.4 3.8 convolution_convert_fusion
  154.2 0.0 copy-done.9
  154.2 0.0 copy-done.10
  154.2 2.6 fusion.11
  156.8 0.0 copy-done.11
  156.8 3.7 add_convert_fusion.1
  160.6 84.9 %ffn_sums.1 = (f32[2,3,16,2048]{3,2,1,0:T(8,128)}, f32[8,2048]{1,0:T(8,128)}, bf16[2,3,16,2048]{3,2,1,0:T(8,128)(2,1)}, bf16[3,2,4,16,2048]{4,3,2,1,0:T(8,128)(2...) custom-call(f32[2,3,16,1]{3,2,1,0:T(8,128)} %get-tuple-element.50.refs_0_, ...), custom_call_target="tpu_custom_call" | custom-call | bytes 80000000 | tf_op jit(solution)/shard_map/ffn_sums/pallas_call | solution.py:1409
  245.5 3.2 convolution_convert_fusion.2.grad_ref
  248.7 14.0 %attend_back.1 = (bf16[384,512]{1,0:T(8,128)(2,1)}, bf16[8,384,256]{2,1,0:T(8,128)(2,1)}, f32[256,1408]{1,0:T(8,128)}, f32[256,1408]{1,0:T(8,128)}, f32[1408,256]{1,0:T(8,128)}) custom-call(s32[6]{0:T(128)} %lens_ref.9, s32[6]{0:T(128)} %flags_ref.9, s32[1]{0:T(128)} %bitcast.2.own_ref, bf16[384,512]{1,0:T(8,128)(2,1)} %get-tuple-element.46.query_ref, ...), custom_call_target="tpu_custom_call" | custom-call | flops 3000000000 | bytes 20000000 | tf_op jit(solution)/shard_map/attend_back/pallas_call | solution.py:758
  262.7 0.0 copy-start.6
  262.7 0.0 copy-start.7
  262.7 0.0 copy-start.5
  262.7 19.3 %scatter_tok.1 = f32[384,256]{1,0:T(8,128)} custom-call(bf16[8,384,256]{2,1,0:T(8,128)(2,1)} %get-tuple-element.64.part_ref), custom_call_target="tpu_custom_call" | custom-call | bytes 10000000 | tf_op jit(solution)/shard_map/scatter_tok/pallas_call | solution.py:871
  282.1 0.0 copy-start.3
  282.1 1.0 slice.30
  283.1 1.1 fusion.5
  284.2 0.0 copy-done.6
  284.2 1.1 fusion.2
  285.3 0.0 copy-done.7
  285.3 0.9 pad_maximum_fusion.refs_6_
  286.2 0.0 copy-done.5
  286.2 0.6 fusion.7
  286.8 0.5 copy-done.4
  287.2 0.6 fusion.12
  287.8 1.0 copy-done.1
  288.8 2.2 add_convert_fusion
  291.0 114.0 %attn_sums.1 = (bf16[6,128,2048]{2,1,0:T(8,128)(2,1)}, f32[8,256]{1,0:T(8,128)}, bf16[6,128,2048]{2,1,0:T(8,128)(2,1)}, f32[256,768]{1,0:T(8,128)}, f32[512,256]{1,0:T(8,128)}) custom-call(s32[6]{0:T(128)} %lens_ref.9, s32[6]{0:T(128)} %flags_ref.9, bf16[2,3,16,2048]{3,2,1,0:T(8,128)(2,1)} %get-tuple-element.54.refs_0_, f32[3,2,4,16,1]{4,3,2,1,0:T(8,128)} %bitcast.65, ...), custom_call_target="tpu_custom_call" | custom-call | bytes 80000000 | tf_op jit(solution)/shard_map/attn_sums/pallas_call | solution.py:1532
  405.0 5.0 %finish.1 = (bf16[6,128,2048]{2,1,0:T(8,128)(2,1)}, bf16[6,128,2048]{2,1,0:T(8,128)(2,1)}, f32[256,512]{1,0:T(8,128)}, f32[256,128]{1,0:T(8,128)}, f32[256,128]{1,0:T(8,128)}, /*index=5*/f32[512,256]{1,0:T(8,128)}) custom-call(bf16[6,128,2048]{2,1,0:T(8,128)(2,1)} %get-tuple-element.67.mixed_ref, bf16[6,128,2048]{2,1,0:T(8,128)(2,1)} %get-tuple-element.68.grad_ref, ...), custom_call_target="tpu_custom_call" | custom-call | bytes 20000000 | tf_op jit(solution)/shard_map/finish/pallas_call | solution.py:805
  410.0 1.3 fusion.6
  (10 shorter events, 0.0 us)
Async XLA Ops:
  0.6 74.1 %copy-start = (bf16[512,2048]{1,0:T(8,128)(2,1)S(1)}, bf16[512,2048]{1,0:T(8,128)(2,1)}, u32[]{:S(2)}) copy-start(bf16[512,2048]{1,0:T(8,128)(2,1)} %param.18) | copy-start | bytes 6291460
  136.5 7.8 %slice-start.2 = ((s8[5767168]{0:T(1024)(128)(4,1)}), s8[4194304]{0:T(1024)(128)(4,1)S(1)}, s32[]{:S(2)}) async-start(s8[5767168]{0:T(1024)(128)(4,1)} %bitcast.75), calls=%async_computation.2 | async-start | bytes 8388608
  138.4 5.9 %copy-start.2 = (bf16[3,128,2048]{2,1,0:T(8,128)(2,1)}, bf16[3,128,2048]{2,1,0:T(8,128)(2,1)S(1)}, u32[]{:S(2)}) copy-start(bf16[3,128,2048]{2,1,0:T(8,128)(2,1)S(1)} %multiply_convert_fusion) | copy-start | bytes 4718596
  138.4 5.9 %copy-start.8 = (bf16[3,2,4,16,2048]{4,3,2,1,0:T(8,128)(2,1)S(1)}, bf16[3,2,4,16,2048]{4,3,2,1,0:T(8,128)(2,1)}, u32[]{:S(2)}) copy-start(bf16[3,2,4,16,2048]{4,3,2,1,0:T(8,128)(2,1)} %get-tuple-element.52) | copy-start | bytes 4718596
  138.4 5.9 %slice-start.3 = ((s8[5767168]{0:T(1024)(128)(4,1)}), s8[1572864]{0:T(1024)(128)(4,1)S(1)}, s32[]{:S(2)}) async-start(s8[5767168]{0:T(1024)(128)(4,1)} %bitcast.75), calls=%async_computation.3 | async-start | bytes 3145728
  138.4 8.6 %slice-start.4 = ((s8[5767168]{0:T(1024)(128)(4,1)}), s8[4194304]{0:T(1024)(128)(4,1)S(1)}, s32[]{:S(2)}) async-start(s8[5767168]{0:T(1024)(128)(4,1)} %bitcast.77), calls=%async_computation.4 | async-start | bytes 8388608
  144.3 2.7 slice-start.5
  144.4 6.0 %slice-start = ((s8[5767168]{0:T(1024)(128)(4,1)}), s8[4194304]{0:T(1024)(128)(4,1)S(1)}, s32[]{:S(2)}) async-start(s8[5767168]{0:T(1024)(128)(4,1)} %bitcast.73), calls=%async_computation | async-start | bytes 8388608
  147.0 3.3 slice-start.1
  150.3 3.9 copy-start.9
  150.3 3.9 copy-start.10
  150.3 6.5 %copy-start.11 = (bf16[384,1408]{1,0:T(8,128)(2,1)}, bf16[384,1408]{1,0:T(8,128)(2,1)S(1)}, u32[]{:S(2)}) copy-start(bf16[384,1408]{1,0:T(8,128)(2,1)S(1)} %get-tuple-element.83.refs_5_) | copy-start | bytes 3244036
  262.7 21.5 %copy-start.6 = (f32[384,128]{1,0:T(8,128)S(1)}, f32[384,128]{1,0:T(8,128)}, u32[]{:S(2)}) copy-start(f32[384,128]{1,0:T(8,128)} %get-tuple-element.92.sin_ref) | copy-start | bytes 589828
  262.7 22.6 %copy-start.7 = (bf16[384,512]{1,0:T(8,128)(2,1)S(1)}, bf16[384,512]{1,0:T(8,128)(2,1)}, u32[]{:S(2)}) copy-start(bf16[384,512]{1,0:T(8,128)(2,1)} %get-tuple-element.63) | copy-start | bytes 1179652
  262.7 23.5 %copy-start.5 = (bf16[2048,128]{1,0:T(8,128)(2,1)S(1)}, bf16[2048,128]{1,0:T(8,128)(2,1)}, u32[]{:S(2)}) copy-start(bf16[2048,128]{1,0:T(8,128)(2,1)} %w_value_hbm.1) | copy-start | bytes 1572868
  282.1 4.2 %copy-start.3 = (f32[384,256]{1,0:T(8,128)S(1)}, f32[384,256]{1,0:T(8,128)}, u32[]{:S(2)}) copy-start(f32[384,256]{1,0:T(8,128)} %scatter_tok.1) | copy-start | bytes 1179652
  286.2 1.0 copy-start.4
  287.2 1.6 copy-start.1
